TPU v7x, 32 devices: a whole 2x2x4 slice. The times are simulated.
32 devices in a mesh: pair: 4 (over y, x), row: 8 (over z, core).
Axes of the slice: x: 2, y: 2, z: 4, core: 2. Of those that a mesh axis runs over, the one named last changes fastest.
Arguments:
- matrix: float32 [2, 32768, 512], P(None, 'row', 'pair'), may hold values from -100 to 100, as said below
Outputs:
- rotated_matrix: float32 [2, 32768, 512], P(None, 'row', 'pair')
Inputs may be any that keep to these rules, and one draw needn't show every extreme that they name: `matrix`: entries are real values with column blocks that are far from orthogonal to one another.
All inputs are finite; a program needn't handle non-finite values.
Results may differ from a plain program's by a relative error of at most 0.00014.
Values sent between devices are 32-bit elements; how exact they have to be, the bound alone decides.
No kernel may reach another device: no remote copies, remote signals or barrier semaphores. Data moves between devices by JAX's collectives and lax.ppermute only.
A program may use at most 64 MiB of HBM per device.

v0:
```python
import jax
import jax.numpy as jnp
from jax import lax
from jax.sharding import PartitionSpec as P

STEPS = 2
SWEEPS = 2
NEWTON = 3


def shifted(block, axis, distance):
    devices = range(lax.axis_size(axis))
    route = [(i - distance, i) for i in devices if i - distance in devices]
    return lax.ppermute(block, axis, route)


def gram_of(left_cols, right_cols):
    return lax.dot_general(
        left_cols,
        right_cols,
        (((0,), (0,)), ((), ())),
        precision=lax.Precision.HIGHEST,
        preferred_element_type=jnp.float32,
    )


def product(left_mat, right_mat):
    return jnp.dot(
        left_mat, right_mat, precision=lax.Precision.HIGHEST, preferred_element_type=jnp.float32
    )


def polar_turn(gram_matrix):
    half_width = gram_matrix.shape[0] // 2
    diagonal = jnp.diagonal(gram_matrix)
    inverse = 1.0 / jnp.sqrt(diagonal + 1e-06)
    cross_part = (
        gram_matrix[:half_width, half_width:]
        * inverse[:half_width, None]
        * inverse[None, half_width:]
    )
    cross_part = cross_part / (1.0 + jnp.sqrt(jnp.sum(cross_part * cross_part)))
    zero_block = jnp.zeros((half_width, half_width), jnp.float32)
    skew_part = jnp.concatenate(
        [
            jnp.concatenate([zero_block, cross_part], 1),
            jnp.concatenate([-cross_part.T, zero_block], 1),
        ],
        0,
    )
    identity = jnp.eye(2 * half_width, dtype=jnp.float32)
    factor = identity + skew_part
    for repeat in range(NEWTON):
        factor = product(factor, 1.5 * identity - 0.5 * gram_of(factor, factor))
    return factor


def pair_rotation(gram_matrix):
    rotation = jnp.eye(gram_matrix.shape[0], dtype=jnp.float32)
    current = gram_matrix
    for sweep_index in range(SWEEPS):
        factor = polar_turn(current)
        rotation = product(rotation, factor)
        if sweep_index + 1 < SWEEPS:
            current = gram_of(factor, product(current, factor))
    return (rotation, current)


def plain_move(upper_block, lower_block):
    pairs_count = lax.axis_size("pair")
    position = lax.axis_index("pair")
    outgoing = jnp.where(position == 0, lower_block, upper_block)
    arrived = shifted(outgoing, "pair", 1)
    below = shifted(lower_block, "pair", -1)
    new_upper = jnp.where(position == 0, upper_block, arrived)
    new_lower = jnp.where(position == pairs_count - 1, upper_block, below)
    return (new_upper, new_lower)


def body(matrix):
    upper_block = matrix[0]
    lower_block = matrix[1]
    half_width = upper_block.shape[1]
    for step_index in range(STEPS):
        pair_cols = jnp.concatenate([upper_block, lower_block], 1)
        gram_matrix = lax.psum(gram_of(pair_cols, pair_cols), "row")
        rotation, current = pair_rotation(gram_matrix)
        rotated = product(pair_cols, rotation)
        upper_block = rotated[:, :half_width]
        lower_block = rotated[:, half_width:]
        upper_block, lower_block = plain_move(upper_block, lower_block)
    return jnp.stack([upper_block, lower_block], 0)


def solution(mesh):
    in_specs = (P(None, "row", "pair"),)
    out_specs = P(None, "row", "pair")
    return jax.shard_map(body, mesh=mesh, in_specs=in_specs, out_specs=out_specs, check_vma=False)
```

profile of v0, /device:TPU:0, one launch (start us, length us, event | category | flops | bytes accessed | tf_op | source)
XLA Modules:
  0.0 389.0 jit_solution(12013390697289789309)
XLA Ops:
  6.5 2.5 slice_bitcast_fusion.1
  9.0 1.3 copy-done.1
  10.4 7.8 %fusion.3 = f32[256,256]{1,0:T(8,128)} fusion(f32[4096,128]{1,0:T(8,128)S(1)} %get-tuple-element.22, f32[4096,128]{1,0:T(8,128)S(1)} %get-tuple-element.21), kind=kOutput, calls=%fused_computation.10 | convolution fusion | flops 3222274048 | bytes 4456448 | tf_op jit(solution)/shard_map/dot_general | solution.py:18
  18.8 57.2 %all-reduce.11.cloned.1.call-done = f32[256,256]{1,0:T(8,128)} async-done(((f32[256,256]{1,0:T(8,128)}), f32[256,256]{1,0:T(8,128)}) %all-reduce.11.cloned.1.call-update) | async-done | bytes 262160 | tf_op jit(solution)/shard_map/psum | solution.py:86
  75.9 2.6 gather_fusion
  78.5 1.6 multiply_reduce_fusion.3
  80.8 0.9 negate_bitcast_fusion.3
  86.1 2.5 gather_fusion.1
  88.7 0.7 multiply_reduce_fusion.2
  93.5 4.0 %fusion.2 = f32[4096,256]{0,1:T(8,128)S(1)} fusion(f32[256,256]{1,0:T(8,128)S(1)} %fusion.76, f32[4096,128]{1,0:T(8,128)S(1)} %copy-done.2, f32[4096,128]{1,0:T(8,128)S(1)} %get-tuple-element.21), kind=kOutput, calls=%fused_computation.9 | convolution fusion | flops 3222274048 | bytes 8650752 | tf_op jit(solution)/shard_map/dot_general | solution.py:28
  97.5 2.4 slice_select_fusion.3
  100.0 0.8 copy-done
  100.8 3.5 collective-permute-start
  104.3 1.5 collective-permute-start.1
  105.8 41.9 %collective-permute-done = f32[4096,128]{0,1:T(8,128)S(1)} collective-permute-done((f32[4096,128]{0,1:T(8,128)}, f32[4096,128]{0,1:T(8,128)S(1)}, u32[]{:S(2)}, u32[]{:S(2)}) %collective-permute-start) | collective-permute-done | bytes 2097184 | tf_op jit(solution)/shard_map/ppermute | solution.py:14
  147.7 1.3 copy-done.7
  149.0 45.5 %collective-permute-done.1 = f32[4096,128]{0,1:T(8,128)} collective-permute-done((f32[4096,128]{0,1:T(8,128)}, f32[4096,128]{0,1:T(8,128)}, u32[]{:S(2)}, u32[]{:S(2)}) %collective-permute-start.1) | collective-permute-done | bytes 2097184 | tf_op jit(solution)/shard_map/ppermute | solution.py:14
  194.5 2.6 slice_select_fusion.2
  197.1 1.3 copy-done.3
  198.5 4.2 %fusion.1 = f32[256,256]{1,0:T(8,128)} fusion(f32[4096,128]{0,1:T(8,128)S(1)} %get-tuple-element.18, f32[4096,128]{0,1:T(8,128)S(1)} %get-tuple-element.17), kind=kOutput, calls=%fused_computation.8 | convolution fusion | flops 3222274048 | bytes 4456448 | tf_op jit(solution)/shard_map/dot_general | solution.py:18
  202.7 54.7 %all-reduce.13.cloned.1.call-done = f32[256,256]{1,0:T(8,128)} async-done(((f32[256,256]{1,0:T(8,128)}), f32[256,256]{1,0:T(8,128)}) %all-reduce.13.cloned.1.call-update) | async-done | bytes 262160 | tf_op jit(solution)/shard_map/psum | solution.py:86
  257.4 2.6 gather_fusion.2
  260.0 1.6 multiply_reduce_fusion.1
  262.2 0.9 negate_bitcast_fusion.1
  267.6 2.6 gather_fusion.3
  275.1 4.3 %fusion = f32[4096,256]{0,1:T(8,128)S(1)} fusion(f32[256,256]{1,0:T(8,128)S(1)} %fusion.83, f32[4096,128]{0,1:T(8,128)S(1)} %copy-done.4, f32[4096,128]{0,1:T(8,128)S(1)} %get-tuple-element.17), kind=kOutput, calls=%fused_computation.7 | convolution fusion | flops 3222274048 | bytes 8650752 | tf_op jit(solution)/shard_map/dot_general | solution.py:28
  279.9 3.5 collective-permute-start.2
  283.4 1.3 collective-permute-start.3
  284.7 41.7 %collective-permute-done.2 = f32[4096,128]{0,1:T(8,128)S(1)} collective-permute-done((f32[4096,128]{0,1:T(8,128)S(1)}, f32[4096,128]{0,1:T(8,128)S(1)}, u32[]{:S(2)}, u32[]{:S(2)}) %collective-permute-start.2) | collective-permute-done | bytes 2097184 | tf_op jit(solution)/shard_map/ppermute | solution.py:14
  326.4 46.9 %collective-permute-done.3 = f32[4096,128]{0,1:T(8,128)S(1)} collective-permute-done((f32[4096,128]{0,1:T(8,128)S(1)}, f32[4096,128]{0,1:T(8,128)S(1)}, u32[]{:S(2)}, u32[]{:S(2)}) %collective-permute-start.3) | collective-permute-done | bytes 2097184 | tf_op jit(solution)/shard_map/ppermute | solution.py:14
  373.8 2.4 pad_maximum_fusion.2
  376.3 5.6 %copy.15 = f32[2,4096,128]{2,1,0:T(8,128)} copy(f32[2,4096,128]{1,2,0:T(8,128)} %pad_maximum_fusion.2) | data formatting | bytes 8388608 | tf_op jit(solution)/shard_map/stack | solution.py:92
  (66 shorter events, 18.0 us)
Async XLA Ops:
  6.5 69.4 %all-reduce.11.cloned.1.call-start = ((), (), s32[]{:S(2)}) async-start(), calls=%async_computation | async-start | bytes 524288 | tf_op jit(solution)/shard_map/psum | solution.py:86
  9.0 1.3 copy-start.1
  18.2 239.2 %all-reduce.13.cloned.1.call-start = ((), (), s32[]{:S(2)}) async-start(), calls=%async_computation.1 | async-start | bytes 524288 | tf_op jit(solution)/shard_map/psum | solution.py:86
  82.2 2.9 copy-start.5
  91.1 2.5 copy-start.2
  97.5 3.3 copy-start
  100.8 46.9 %collective-permute-start = (f32[4096,128]{0,1:T(8,128)}, f32[4096,128]{0,1:T(8,128)S(1)}, u32[]{:S(2)}, u32[]{:S(2)}) collective-permute-start(f32[4096,128]{0,1:T(8,128)} %get-tuple-element.19), channel_id=1, source_target_pairs={{0,8},{8,16},{16,24},{1,9},{9,17},{17,25},{2,10},{10,18},{18,26},{... | collective-permute-start | bytes 6291464 | tf_op jit(solution)/shard_map/ppermute | solution.py:14
  104.3 90.2 %collective-permute-start.1 = (f32[4096,128]{0,1:T(8,128)}, f32[4096,128]{0,1:T(8,128)}, u32[]{:S(2)}, u32[]{:S(2)}) collective-permute-start(f32[4096,128]{0,1:T(8,128)} %get-tuple-element.20), channel_id=1, source_target_pairs={{8,0},{16,8},{24,16},{9,1},{17,9},{25,17},{10,2},{18,10},{26,18},{... | collective-permute-start | bytes 6291464 | tf_op jit(solution)/shard_map/ppermute | solution.py:14
  147.7 1.3 copy-start.7
  197.1 1.3 copy-start.3
  263.7 2.9 copy-start.6
  272.6 2.5 copy-start.4
  279.9 46.6 %collective-permute-start.2 = (f32[4096,128]{0,1:T(8,128)S(1)}, f32[4096,128]{0,1:T(8,128)S(1)}, u32[]{:S(2)}, u32[]{:S(2)}) collective-permute-start(f32[4096,128]{0,1:T(8,128)S(1)} %get-tuple-element.15), channel_id=1, source_target_pairs={{0,8},{8,16},{16,24},{1,9},{9,17},{17,25},{2,10},{10,18},{18,26},{... | collective-permute-start | bytes 6291464 | tf_op jit(solution)/shard_map/ppermute | solution.py:14
  283.4 89.9 %collective-permute-start.3 = (f32[4096,128]{0,1:T(8,128)S(1)}, f32[4096,128]{0,1:T(8,128)S(1)}, u32[]{:S(2)}, u32[]{:S(2)}) collective-permute-start(f32[4096,128]{0,1:T(8,128)S(1)} %get-tuple-element.16), channel_id=1, source_target_pairs={{8,0},{16,8},{24,16},{9,1},{17,9},{25,17},{10,2},{18,10},{26,18},{... | collective-permute-start | bytes 6291464 | tf_op jit(solution)/shard_map/ppermute | solution.py:14
Sparse Core Ops, SparseCore 0:
  18.3 57.6 all-reduce.10
  202.8 54.5 all-reduce.12
where the time goes:
time: 395 us; the launch traced here: 389 us
  waiting for transfers between devices  288 us (73%)
  matrix products  35.4 us (9%)
  local copies, waits for them, and re-layouts  23.5 us (6%)
  between operations  16.8 us (4%)
  other arithmetic  15 us (4%)
  starting transfers between devices  10.4 us (3%)
    ppermute x4, waiting for transfers between devices, shifted(): return lax.ppermute(block, axis, route)  176 us
    psum x2, waiting for transfers between devices, body(): gram_matrix = lax.psum(gram_of(pair_cols, pair_cols), 'row')  112 us
    dot_general x16, matrix products, gram_of(): lax.dot_general(left_cols, right_cols, (((0,), (0,)), ((), ())), precisio...  19.7 us
    dot_general x20, matrix products, product(): jnp.dot(left_mat, right_mat, precision=lax.Precision.HIGHEST, preferred_e...  15.7 us
    gather x4, local copies, waits for them, and re-layouts, polar_turn(): diagonal = jnp.diagonal(gram_matrix)  10.2 us
    ppermute x4, starting transfers between devices, shifted(): return lax.ppermute(block, axis, route)  9.8 us
  transfers between devices with their start and end apart: 6, of which 6 were waited for; matrix products, arithmetic and copies ran while one was open for 0% of the time, Pallas kernels for 0%

commit v1 on v0

v1 whole, which is shorter than its diff:
```python
import functools

import jax
import jax.numpy as jnp
from jax import lax
from jax.experimental import pallas as pl
from jax.experimental.pallas import tpu as pltpu
from jax.sharding import PartitionSpec as P


F32 = jnp.float32
BF16 = jnp.bfloat16
VMEM_LIMIT = 48 * 1024 * 1024


def after(p, n):
    if p == 0:
        return 1
    if p % 2:
        return n - 2 if p == n - 1 else p + 2
    return p - 2


def halves(x):
    high = x.astype(BF16)
    return high, (x - high.astype(F32)).astype(BF16)


def dot3(left, right, contract):
    def one(a, b):
        return lax.dot_general(a, b, (contract, ((), ())), preferred_element_type=F32)

    return one(left[0], right[0]) + (one(left[0], right[1]) + one(left[1], right[0]))


PLAIN = ((1,), (0,))
LEFT_T = ((0,), (0,))
RIGHT_T = ((1,), (1,))


def eye_of(width):
    rows = lax.broadcasted_iota(jnp.int32, (width, width), 0)
    cols = lax.broadcasted_iota(jnp.int32, (width, width), 1)
    return rows, cols


def polar(cross, sign):
    width = cross.shape[0]
    rows, cols = eye_of(width)
    unit = (rows == cols).astype(F32)
    x = halves(cross)
    squares = [dot3(x, x, RIGHT_T), dot3(x, x, LEFT_T)]
    firsts, lasts, thirds = [], [], []
    for s in squares:
        sh = halves(s)
        s2 = dot3(sh, sh, PLAIN)
        e = 0.75 * s2 - 0.25 * dot3(halves(s2), sh, PLAIN)
        eh = halves(e)
        e2 = dot3(eh, eh, PLAIN)
        z = unit - 0.5 * s + 0.5 * e - 0.25 * dot3(sh, eh, PLAIN)
        f = 0.75 * e2 + 0.25 * dot3(halves(e2), eh, PLAIN)
        fh = halves(f)
        thirds.append(fh)
        firsts.append(z)
        lasts.append(z + 0.5 * dot3(halves(z), fh, PLAIN))
    xz = dot3(x, halves(firsts[1]), PLAIN)
    wide = sign * (xz + 0.5 * dot3(halves(xz), thirds[1], PLAIN))
    return jnp.concatenate(
        [jnp.concatenate([lasts[0], wide], 1), jnp.concatenate([-wide.T, lasts[1]], 1)], 0
    )


def scaled(cross, down, across):
    x = cross * lax.rsqrt(down + 1e-06) * lax.rsqrt(across + 1e-06)
    return x / (1.0 + jnp.sqrt(jnp.sum(x * x)))


def rotation_of(upper, cross, lower, sign):
    width = cross.shape[0]
    rows, cols = eye_of(width)
    same = rows == cols
    zero = jnp.zeros((width, width), F32)
    down = jnp.sum(jnp.where(same, upper, zero), 1, keepdims=True)
    across = jnp.sum(jnp.where(same, lower, zero), 0, keepdims=True)
    first = polar(scaled(cross, down, across), sign)
    gram = jnp.concatenate(
        [jnp.concatenate([upper, cross], 1), jnp.concatenate([cross.T, lower], 1)], 0
    )
    first_halves = halves(first)
    turned = dot3(halves(gram), first_halves, PLAIN)
    second_cross = dot3(halves(first[:, :width]), halves(turned[:, width:]), LEFT_T)
    diagonal = jnp.sum(first * turned, 0, keepdims=True)
    down = jnp.sum(jnp.where(same, diagonal[:, :width], zero), 1, keepdims=True)
    second = polar(scaled(second_cross, down, diagonal[:, width:]), sign)
    return gram, dot3(first_halves, halves(second), PLAIN)


def core_of():
    return lax.rem(lax.axis_index("row"), 2)


def first_is_upper():
    p = lax.axis_index("pair")
    clock_upper = (p == 0) | (lax.rem(p, 2) == 1)
    return (core_of() == 0) == clock_upper


def gram_kernel(matrix_ref, keep_ref, give_ref, main_ref, rest_ref):
    step = pl.program_id(0)
    block = jnp.concatenate([matrix_ref[0], matrix_ref[1]], 1)
    high, low = halves(block)
    main = lax.dot_general(high, high, (LEFT_T, ((), ())), preferred_element_type=F32)
    rest = lax.dot_general(high, low, (LEFT_T, ((), ())), preferred_element_type=F32)

    @pl.when(step == 0)
    def _():
        main_ref[...] = main
        rest_ref[...] = rest

    @pl.when(step > 0)
    def _():
        main_ref[...] += main
        rest_ref[...] += rest

    @pl.when(step == pl.num_programs(0) - 1)
    def _():
        total = main_ref[...] + (rest_ref[...] + rest_ref[...].T)
        width = total.shape[0] // 2
        rows, cols = eye_of(width)
        upper, lower = total[:width, :width], total[width:, width:]
        diagonal = jnp.sum(jnp.where(rows == cols, lower, jnp.zeros_like(lower)), 0, keepdims=True)
        packed = jnp.where(rows <= cols, upper, lower)
        pad = jnp.broadcast_to(diagonal, (8, width))
        cross = total[:width, width:]
        mine = core_of() == 0
        keep_ref[:width] = jnp.where(mine, cross, packed)
        give_ref[:width] = jnp.where(mine, packed, cross)
        keep_ref[width:] = pad
        give_ref[width:] = pad


def local_gram(matrix, chunk):
    rows, width = matrix.shape[1:]
    out = jax.ShapeDtypeStruct((width + 8, width), F32)
    whole = pl.BlockSpec((width + 8, width), lambda i: (0, 0))
    return pl.pallas_call(
        gram_kernel,
        grid=(rows // chunk,),
        in_specs=[pl.BlockSpec((2, chunk, width), lambda i: (0, i, 0))],
        out_specs=[whole, whole],
        out_shape=[out, out],
        scratch_shapes=[pltpu.VMEM((2 * width, 2 * width), F32)] * 2,
        compiler_params=pltpu.CompilerParams(vmem_limit_bytes=VMEM_LIMIT),
        cost_estimate=pl.CostEstimate(flops=16 * rows * width * width, bytes_accessed=8 * rows * width, transcendentals=0),
        name="gram",
    )(matrix)


def rotate_kernel(mine_ref, other_ref, first_ref, second_ref, gram_ref):
    width = mine_ref.shape[1]
    holds_cross = core_of() == 0
    mine, other = mine_ref[...], other_ref[...]
    cross = jnp.where(holds_cross, mine[:width], other[:width])
    packed = jnp.where(holds_cross, other, mine)
    diagonal = packed[width : width + 1]
    packed = packed[:width]
    rows, cols = eye_of(width)
    flipped = packed.T
    upper = jnp.where(rows <= cols, packed, flipped)
    lower = jnp.where(rows > cols, packed, flipped)
    lower = jnp.where(rows == cols, diagonal, lower)
    gram, rotation = rotation_of(upper, cross, lower, 1.0)
    left, right = rotation[:, :width], rotation[:, width:]
    upper_first = first_is_upper()
    first_ref[...] = jnp.where(upper_first, left, right)
    second_ref[...] = jnp.where(upper_first, right, left)
    gram_ref[...] = gram


def first_rotation(mine, other):
    width = mine.shape[1]
    half = jax.ShapeDtypeStruct((2 * width, width), F32)
    return pl.pallas_call(
        rotate_kernel,
        out_shape=[half, half, jax.ShapeDtypeStruct((2 * width, 2 * width), F32)],
        compiler_params=pltpu.CompilerParams(vmem_limit_bytes=VMEM_LIMIT),
        name="first_rotation",
    )(mine, other)


def blocks_kernel(gram_ref, first_ref, second_ref, first_gram_ref, second_gram_ref):
    gram = halves(gram_ref[...])
    for turn_ref, out_ref in ((first_ref, first_gram_ref), (second_ref, second_gram_ref)):
        turn = halves(turn_ref[...])
        out_ref[...] = dot3(turn, halves(dot3(gram, turn, PLAIN)), LEFT_T)


def block_grams(gram, first, second):
    width = first.shape[1]
    out = jax.ShapeDtypeStruct((width, width), F32)
    return pl.pallas_call(
        blocks_kernel,
        out_shape=[out, out],
        compiler_params=pltpu.CompilerParams(vmem_limit_bytes=VMEM_LIMIT),
        name="block_grams",
    )(gram, first, second)


def product_kernel(matrix_ref, turn_ref, out_ref):
    width = out_ref.shape[1]
    turn = halves(turn_ref[...])
    upper, lower = halves(matrix_ref[0]), halves(matrix_ref[1])
    top = tuple(t[:width] for t in turn)
    bottom = tuple(t[width:] for t in turn)
    out_ref[...] = dot3(upper, top, PLAIN) + dot3(lower, bottom, PLAIN)


def rotated(matrix, turn, start, count, chunk):
    width = matrix.shape[2]
    offset = start // chunk
    return pl.pallas_call(
        product_kernel,
        grid=(count // chunk,),
        in_specs=[
            pl.BlockSpec((2, chunk, width), lambda i: (0, i + offset, 0)),
            pl.BlockSpec((2 * width, width), lambda i: (0, 0)),
        ],
        out_specs=pl.BlockSpec((chunk, width), lambda i: (i, 0)),
        out_shape=jax.ShapeDtypeStruct((count, width), F32),
        compiler_params=pltpu.CompilerParams(vmem_limit_bytes=VMEM_LIMIT),
        cost_estimate=pl.CostEstimate(flops=12 * count * width * width, bytes_accessed=12 * count * width, transcendentals=0),
        name="product",
    )(matrix, turn)


def cross_kernel(own_ref, far_ref, total_ref, out_ref):
    part = dot3(halves(own_ref[...]), halves(far_ref[...]), LEFT_T)

    @pl.when(pl.program_id(0) == 0)
    def _():
        out_ref[...] = total_ref[...] + part

    @pl.when(pl.program_id(0) > 0)
    def _():
        out_ref[...] += part


def cross_gram(own, far, total, start, chunk):
    count, width = far.shape
    offset = start // chunk
    return pl.pallas_call(
        cross_kernel,
        grid=(count // chunk,),
        in_specs=[
            pl.BlockSpec((chunk, width), lambda i: (i + offset, 0)),
            pl.BlockSpec((chunk, width), lambda i: (i, 0)),
            pl.BlockSpec((width, width), lambda i: (0, 0)),
        ],
        out_specs=pl.BlockSpec((width, width), lambda i: (0, 0)),
        out_shape=jax.ShapeDtypeStruct((width, width), F32),
        compiler_params=pltpu.CompilerParams(vmem_limit_bytes=VMEM_LIMIT),
        cost_estimate=pl.CostEstimate(flops=6 * count * width * width, bytes_accessed=8 * count * width, transcendentals=0),
        name="cross_gram",
    )(own, far, total)


def second_kernel(own_gram_ref, far_gram_ref, here_ref, there_ref, out_ref):
    width = out_ref.shape[1]
    p, n = lax.axis_index("pair"), lax.axis_size("pair")
    odd = lax.rem(p, 2) == 1
    outward = core_of() == 1
    own_upper_out = (p == 0) | (odd & (p != n - 1))
    own_upper = (outward & own_upper_out) | (jnp.logical_not(outward) & jnp.logical_not(odd))
    sign = jnp.where(own_upper, 1.0, -1.0).astype(F32)
    cross = here_ref[...] + there_ref[...].T
    _, rotation = rotation_of(own_gram_ref[...], cross, far_gram_ref[...], sign)
    keeps_own = (outward & (p == 0)) | (jnp.logical_not(outward) & (p == 1))
    out_ref[...] = jnp.where(keeps_own, rotation[:, :width], rotation[:, width:])


def second_rotation(own_gram, far_gram, here, there):
    width = here.shape[1]
    return pl.pallas_call(
        second_kernel,
        out_shape=jax.ShapeDtypeStruct((2 * width, width), F32),
        compiler_params=pltpu.CompilerParams(vmem_limit_bytes=VMEM_LIMIT),
        name="second_rotation",
    )(own_gram, far_gram, here, there)


def last_kernel(slot_ref, own_ref, *rest):
    del slot_ref
    far_refs, turn_ref, out_ref = rest[:-2], rest[-2], rest[-1]
    width = own_ref.shape[1]
    turn = halves(turn_ref[...])
    top = tuple(t[:width] for t in turn)
    bottom = tuple(t[width:] for t in turn)
    step = pl.program_id(0)
    for k, far_ref in enumerate(far_refs):

        @pl.when(step == k)
        def _():
            out_ref[0] = dot3(halves(own_ref[...]), top, PLAIN) + dot3(halves(far_ref[...]), bottom, PLAIN)


def last_first_kernel(slot_ref, own_ref, *rest):
    last_kernel(slot_ref, own_ref, *rest)


def last_second_kernel(slot_ref, own_ref, *rest):
    last_kernel(slot_ref, own_ref, *rest[:-2], rest[-1])


def last_product(slot, own, fars, turn, done):
    rows, width = own.shape
    count = rows // len(fars)
    grid_spec = pltpu.PrefetchScalarGridSpec(
        num_scalar_prefetch=1,
        grid=(len(fars),),
        in_specs=[pl.BlockSpec((count, width), lambda i, s: (i, 0))]
        + [pl.BlockSpec((count, width), lambda i, s: (0, 0))] * len(fars)
        + [pl.BlockSpec((2 * width, width), lambda i, s: (0, 0))]
        + ([pl.BlockSpec(memory_space=pl.ANY)] if done is not None else []),
        out_specs=pl.BlockSpec((1, count, width), lambda i, s: (s[0], i, 0)),
    )
    return pl.pallas_call(
        last_first_kernel if done is None else last_second_kernel,
        grid_spec=grid_spec,
        out_shape=jax.ShapeDtypeStruct((2, rows, width), F32),
        input_output_aliases={} if done is None else {3 + len(fars): 0},
        compiler_params=pltpu.CompilerParams(vmem_limit_bytes=VMEM_LIMIT),
        cost_estimate=pl.CostEstimate(flops=12 * rows * width * width, bytes_accessed=16 * rows * width, transcendentals=0),
        name="last_product",
    )(slot, own, *fars, turn, *([] if done is None else [done]))


def body(pairs_count, rows_count, matrix):
    rows, width = matrix.shape[1:]
    parts = 4
    part = rows // parts
    chunk = min(1024, part)
    flat = [(p, r) for p in range(pairs_count) for r in range(rows_count)]
    ahead = {p: after(p, pairs_count) for p in range(pairs_count)}
    behind = {q: p for p, q in ahead.items()}

    def route(moves):
        return [(p * rows_count + r, q * rows_count + t) for (p, r) in flat for (q, t) in [moves(p, r)]]

    outward = route(lambda p, r: (ahead[p] if r % 2 == 0 else behind[p], r))
    inward = route(lambda p, r: (behind[p] if r % 2 == 0 else ahead[p], r))
    crossing = route(lambda p, r: (behind[p] if r % 2 == 0 else ahead[p], r ^ 1))
    core = [(r, r ^ 1) for r in range(rows_count)]

    def travel(block, moves):
        return lax.ppermute(block, ("pair", "row"), moves)

    def chip_sum(block):
        distance = 2
        while distance < rows_count:
            block = block + lax.ppermute(block, "row", [(r, r ^ distance) for r in range(rows_count)])
            distance *= 2
        return block

    keep, give = local_gram(matrix, chunk)
    mine = chip_sum(keep + lax.ppermute(give, "row", core))
    other = lax.ppermute(mine, "row", core)
    turn_first, turn_second, gram = first_rotation(mine, other)

    sent = [rotated(matrix, turn_first, k * part, part, chunk) for k in range(parts)]
    far_first = [travel(block, outward) for block in sent]
    second = rotated(matrix, turn_second, 0, rows, chunk)
    first_gram, second_gram = block_grams(gram, turn_first, turn_second)
    far_gram = travel(first_gram, outward)

    cross = jnp.zeros((width, width), F32)
    for k in range(parts):
        cross = cross_gram(second, far_first[k], cross, k * part, chunk)
    far_second = [travel(second, inward)]

    here = chip_sum(cross)
    there = travel(here, crossing)
    turn_here = second_rotation(second_gram, far_gram, here, there)
    turn_there = lax.ppermute(turn_here, "row", core)

    p = lax.axis_index("pair")
    c = lax.axis_index("row") % 2
    slot = jnp.where(p % 2 == c, 1, 0).astype(jnp.int32).reshape(1)
    done = last_product(slot, second, far_first, turn_here, None)
    first = jnp.concatenate(sent, 0)
    return last_product(1 - slot, first, far_second, turn_there, done)


def solution(mesh):
    spec = P(None, "row", "pair")
    run = functools.partial(body, mesh.shape["pair"], mesh.shape["row"])
    return jax.shard_map(run, mesh=mesh, in_specs=(spec,), out_specs=spec, check_vma=False)
```

time: 395 us -> 107 us (0.27); the launches traced: 389 us -> 106 us
  waiting for transfers between devices: 288 us -> 53.3 us
  matrix products: 35.4 us -> 0 us
  Pallas kernels: 0 us -> 29.5 us
  local copies, waits for them, and re-layouts: 23.5 us -> 2.23 us
  between operations: 16.8 us -> 0.28 us
  other arithmetic: 15 us -> 1.8 us
  starting transfers between devices: 10.4 us -> 19.2 us
    ppermute x4 -> x14, waiting for transfers between devices: 176 us -> 53.3 us  [the longest x7 42 us: travel(): return lax.ppermute(block, ('pair', 'row'), moves)]
    psum x2 -> x0, waiting for transfers between devices: 112 us -> none  [body(): gram_matrix = lax.psum(gram_of(pair_cols, pair_cols), 'row')]
    dot_general x36 -> x0, matrix products: 35.4 us -> none  [the longest x16 19.7 us: gram_of(): lax.dot_general(left_cols, right_cols, (((0,), (0,)), ((), ())), precisio...]
    pallas_call x0 -> x15, Pallas kernels: none -> 29.5 us  [the longest x2 8.14 us: last_product(): pl.pallas_call(last_first_kernel if done is None else last_second_kernel,...]
    gather x4 -> x0, local copies, waits for them, and re-layouts: 10.2 us -> none  [polar_turn(): diagonal = jnp.diagonal(gram_matrix)]
    ppermute x4 -> x14, starting transfers between devices: 9.8 us -> 19.2 us  [the longest x4 10.8 us: chip_sum(): lax.ppermute(block, 'row', [(r, r ^ distance) for r in range(rows_count)])]
    another operation x1 -> x0, local copies, waits for them, and re-layouts: 5.59 us -> none  [body(): return jnp.stack([upper_block, lower_block], 0)]
    select_n x3 -> x0, other arithmetic: 5.48 us -> none  [the longest x2 2.89 us: plain_move(): outgoing = jnp.where(position == 0, lower_block, upper_block)]
  transfers between devices with their start and end apart: 6 -> 14, of which waited for: 6 -> 12; matrix products, arithmetic and copies ran while one was open for 0% -> 2% of each run, Pallas kernels for 0% -> 12%
where the time goes in v1:
time: 107 us; the launch traced here: 106 us
  waiting for transfers between devices  53.3 us (50%)
  Pallas kernels  29.5 us (28%)
  starting transfers between devices  19.2 us (18%)
  local copies, waits for them, and re-layouts  2.23 us (2%)
  other arithmetic  1.8 us (2%)
    ppermute x7, waiting for transfers between devices, travel(): return lax.ppermute(block, ('pair', 'row'), moves)  42 us
    ppermute x4, starting transfers between devices, chip_sum(): lax.ppermute(block, 'row', [(r, r ^ distance) for r in range(rows_count)])  10.8 us
    ppermute x4, waiting for transfers between devices, chip_sum(): lax.ppermute(block, 'row', [(r, r ^ distance) for r in range(rows_count)])  9.19 us
    pallas_call x2, Pallas kernels, last_product(): pl.pallas_call(last_first_kernel if done is None else last_second_kernel,...  8.14 us
    ppermute x7, starting transfers between devices, travel(): return lax.ppermute(block, ('pair', 'row'), moves)  7.65 us
    pallas_call x5, Pallas kernels, rotated(): pl.pallas_call(product_kernel, grid=(count // chunk,), in_specs=[pl.Block...  6.68 us
    pallas_call x1, Pallas kernels, first_rotation(): pl.pallas_call(rotate_kernel, out_shape=[half, half, jax.ShapeDtypeStruct...  4.91 us
    pallas_call x1, Pallas kernels, second_rotation(): pl.pallas_call(second_kernel, out_shape=jax.ShapeDtypeStruct((2 * width,...  4.87 us
  transfers between devices with their start and end apart: 14, of which 12 were waited for; matrix products, arithmetic and copies ran while one was open for 2% of the time, Pallas kernels for 12%

profile of v1, /device:TPU:0, one launch (start us, length us, event | category | flops | bytes accessed | tf_op | source)
XLA Modules:
  0.0 106.3 jit_solution(10851036540473953048)
XLA Ops:
  0.0 2.2 %copy-done = f32[2,4096,128]{2,1,0:T(8,128)S(1)} copy-done((f32[2,4096,128]{2,1,0:T(8,128)S(1)}, f32[2,4096,128]{2,1,0:T(8,128)}, u32[]{:S(2)}) %copy-start) | copy-done | bytes 4194328
  2.2 2.5 %gram.1 = (f32[136,128]{1,0:T(8,128)S(1)}, f32[136,128]{1,0:T(8,128)S(1)}) custom-call(f32[2,4096,128]{2,1,0:T(8,128)S(1)} %copy-done), custom_call_target="tpu_custom_call" | custom-call | flops 1073741824 | bytes 4194304 | tf_op jit(solution)/shard_map/gram/pallas_call | solution.py:146
  5.2 0.9 collective-permute-done
  6.1 3.0 %collective-permute-start.1 = (f32[136,128]{1,0:T(8,128)S(1)}, f32[136,128]{1,0:T(8,128)S(1)}, u32[]{:S(2)}, u32[]{:S(2)}) collective-permute-start(f32[136,128]{1,0:T(8,128)S(1)} %add.24), channel_id=1, source_target_pairs={{0,2},{1,3},{2,0},{3,1},{4,6},{5,7},{6,4},{7,5},{8,10},{9,11},{10,... | collective-permute-start | bytes 208904 | tf_op jit(solution)/shard_map/ppermute | solution.py:360
  9.1 2.5 %collective-permute-done.1 = f32[136,128]{1,0:T(8,128)S(1)} collective-permute-done((f32[136,128]{1,0:T(8,128)S(1)}, f32[136,128]{1,0:T(8,128)S(1)}, u32[]{:S(2)}, u32[]{:S(2)}) %collective-permute-start.1) | collective-permute-done | bytes 69664 | tf_op jit(solution)/shard_map/ppermute | solution.py:360
  11.6 2.9 %collective-permute-start.2 = (f32[136,128]{1,0:T(8,128)S(1)}, f32[136,128]{1,0:T(8,128)S(1)}, u32[]{:S(2)}, u32[]{:S(2)}) collective-permute-start(f32[136,128]{1,0:T(8,128)S(1)} %add.25), channel_id=1, source_target_pairs={{0,4},{1,5},{2,6},{3,7},{4,0},{5,1},{6,2},{7,3},{8,12},{9,13},{10,... | collective-permute-start | bytes 208904 | tf_op jit(solution)/shard_map/ppermute | solution.py:360
  14.5 2.6 %collective-permute-done.2 = f32[136,128]{1,0:T(8,128)S(1)} collective-permute-done((f32[136,128]{1,0:T(8,128)S(1)}, f32[136,128]{1,0:T(8,128)S(1)}, u32[]{:S(2)}, u32[]{:S(2)}) %collective-permute-start.2) | collective-permute-done | bytes 69664 | tf_op jit(solution)/shard_map/ppermute | solution.py:360
  17.2 1.2 %collective-permute-done.3.other_ref = f32[136,128]{1,0:T(8,128)S(1)} collective-permute-done((f32[136,128]{1,0:T(8,128)S(1)}, f32[136,128]{1,0:T(8,128)S(1)}, u32[]{:S(2)}, u32[]{:S(2)}) %collective-permute-start.3) | collective-permute-done | bytes 69664 | tf_op jit(solution)/shard_map/ppermute | solution.py:366
  18.4 4.9 %first_rotation.1 = (f32[256,128]{1,0:T(8,128)S(1)}, f32[256,128]{1,0:T(8,128)S(1)}, f32[256,256]{1,0:T(8,128)S(1)}) custom-call(f32[136,128]{1,0:T(8,128)S(1)} %add.26.mine_ref, f32[136,128]{1,0:T(8,128)S(1)} %collective-permute-done.3.other_ref), custom_call_target="tpu_custom_call" | custom-call | tf_op jit(solution)/shard_map/first_rotation/pallas_call | solution.py:183
  23.4 4.4 %product.9.own_ref = f32[4096,128]{1,0:T(8,128)S(1)} custom-call(f32[2,4096,128]{2,1,0:T(8,128)} %matrix_ref.11, f32[256,128]{1,0:T(8,128)S(1)} %get-tuple-element.15.turn_ref.second_ref), custom_call_target="tpu_custom_call" | custom-call | flops 805306368 | bytes 6291456 | tf_op jit(solution)/shard_map/product/pallas_call | solution.py:221
  27.8 1.6 %collective-permute-start.4 = (f32[4096,128]{1,0:T(8,128)S(1)}, f32[4096,128]{1,0:T(8,128)}, u32[]{:S(2)}, u32[]{:S(2)}) collective-permute-start(f32[4096,128]{1,0:T(8,128)S(1)} %product.9.own_ref), channel_id=1, source_target_pairs={{0,16},{1,9},{2,18},{3,11},{4,20},{5,13},{6,22},{7,15},{8,0},{9,25... | collective-permute-start | bytes 6291464 | tf_op jit(solution)/shard_map/ppermute | solution.py:355
  29.4 0.6 product.5
  30.5 0.6 product.7
  31.7 1.6 %collective-permute-start.8 = (f32[1024,128]{1,0:T(8,128)S(1)}, f32[1024,128]{1,0:T(8,128)S(1)}, u32[]{:S(2)}, u32[]{:S(2)}) collective-permute-start(f32[1024,128]{1,0:T(8,128)S(1)} %product.6), channel_id=1, source_target_pairs={{0,8},{1,17},{2,10},{3,19},{4,12},{5,21},{6,14},{7,23},{8,24},{9,1... | collective-permute-start | bytes 1572872 | tf_op jit(solution)/shard_map/ppermute | solution.py:355
  33.3 1.5 %collective-permute-start.7 = (f32[1024,128]{1,0:T(8,128)S(1)}, f32[1024,128]{1,0:T(8,128)S(1)}, u32[]{:S(2)}, u32[]{:S(2)}) collective-permute-start(f32[1024,128]{1,0:T(8,128)S(1)} %product.7), channel_id=1, source_target_pairs={{0,8},{1,17},{2,10},{3,19},{4,12},{5,21},{6,14},{7,23},{8,24},{9,1... | collective-permute-start | bytes 1572872 | tf_op jit(solution)/shard_map/ppermute | solution.py:355
  35.4 0.6 collective-permute-start.6
  36.0 8.9 %collective-permute-done.9.far_ref.rest_0_ = f32[1024,128]{1,0:T(8,128)S(1)} collective-permute-done((f32[1024,128]{1,0:T(8,128)S(1)}, f32[1024,128]{1,0:T(8,128)S(1)}, u32[]{:S(2)}, u32[]{:S(2)}) %collective-permute-start.9) | collective-permute-done | bytes 524320 | tf_op jit(solution)/shard_map/ppermute | solution.py:355
  45.3 10.8 %collective-permute-done.8.far_ref.rest_1_ = f32[1024,128]{1,0:T(8,128)S(1)} collective-permute-done((f32[1024,128]{1,0:T(8,128)S(1)}, f32[1024,128]{1,0:T(8,128)S(1)}, u32[]{:S(2)}, u32[]{:S(2)}) %collective-permute-start.8) | collective-permute-done | bytes 524320 | tf_op jit(solution)/shard_map/ppermute | solution.py:355
  56.6 10.8 %collective-permute-done.7.far_ref.rest_2_ = f32[1024,128]{1,0:T(8,128)S(1)} collective-permute-done((f32[1024,128]{1,0:T(8,128)S(1)}, f32[1024,128]{1,0:T(8,128)S(1)}, u32[]{:S(2)}, u32[]{:S(2)}) %collective-permute-start.7) | collective-permute-done | bytes 524320 | tf_op jit(solution)/shard_map/ppermute | solution.py:355
  67.8 7.7 %collective-permute-done.6.far_ref.rest_3_ = f32[1024,128]{1,0:T(8,128)S(1)} collective-permute-done((f32[1024,128]{1,0:T(8,128)S(1)}, f32[1024,128]{1,0:T(8,128)S(1)}, u32[]{:S(2)}, u32[]{:S(2)}) %collective-permute-start.6) | collective-permute-done | bytes 524320 | tf_op jit(solution)/shard_map/ppermute | solution.py:355
  76.0 1.7 %collective-permute-start.10 = (f32[128,128]{1,0:T(8,128)S(1)}, f32[128,128]{1,0:T(8,128)S(1)}, u32[]{:S(2)}, u32[]{:S(2)}) collective-permute-start(f32[128,128]{1,0:T(8,128)S(1)} %cross_gram.7), channel_id=1, source_target_pairs={{0,2},{1,3},{2,0},{3,1},{4,6},{5,7},{6,4},{7,5},{8,10},{9,11},{10,... | collective-permute-start | bytes 196616 | tf_op jit(solution)/shard_map/ppermute | solution.py:360
  77.7 3.0 %collective-permute-done.10 = f32[128,128]{1,0:T(8,128)S(1)} collective-permute-done((f32[128,128]{1,0:T(8,128)S(1)}, f32[128,128]{1,0:T(8,128)S(1)}, u32[]{:S(2)}, u32[]{:S(2)}) %collective-permute-start.10) | collective-permute-done | bytes 65568 | tf_op jit(solution)/shard_map/ppermute | solution.py:360
  80.7 3.2 %collective-permute-start.11 = (f32[128,128]{1,0:T(8,128)S(1)}, f32[128,128]{1,0:T(8,128)S(1)}, u32[]{:S(2)}, u32[]{:S(2)}) collective-permute-start(f32[128,128]{1,0:T(8,128)S(1)} %add.27), channel_id=1, source_target_pairs={{0,4},{1,5},{2,6},{3,7},{4,0},{5,1},{6,2},{7,3},{8,12},{9,13},{10,... | collective-permute-start | bytes 196616 | tf_op jit(solution)/shard_map/ppermute | solution.py:360
  83.9 0.8 block_grams.1
  84.7 1.7 %collective-permute-start.5 = (f32[128,128]{1,0:T(8,128)S(1)}, f32[128,128]{1,0:T(8,128)S(1)}, u32[]{:S(2)}, u32[]{:S(2)}) collective-permute-start(f32[128,128]{1,0:T(8,128)S(1)} %get-tuple-element.18), channel_id=1, source_target_pairs={{0,8},{1,17},{2,10},{3,19},{4,12},{5,21},{6,14},{7,23},{8,24},{9,1... | collective-permute-start | bytes 196616 | tf_op jit(solution)/shard_map/ppermute | solution.py:355
  86.4 1.1 %collective-permute-done.11 = f32[128,128]{1,0:T(8,128)S(1)} collective-permute-done((f32[128,128]{1,0:T(8,128)S(1)}, f32[128,128]{1,0:T(8,128)S(1)}, u32[]{:S(2)}, u32[]{:S(2)}) %collective-permute-start.11) | collective-permute-done | bytes 65568 | tf_op jit(solution)/shard_map/ppermute | solution.py:360
  87.7 1.5 %collective-permute-done.5.far_gram_ref = f32[128,128]{1,0:T(8,128)S(1)} collective-permute-done((f32[128,128]{1,0:T(8,128)S(1)}, f32[128,128]{1,0:T(8,128)S(1)}, u32[]{:S(2)}, u32[]{:S(2)}) %collective-permute-start.5) | collective-permute-done | bytes 65568 | tf_op jit(solution)/shard_map/ppermute | solution.py:355
  89.2 2.1 %collective-permute-done.12.there_ref = f32[128,128]{1,0:T(8,128)S(1)} collective-permute-done((f32[128,128]{1,0:T(8,128)S(1)}, f32[128,128]{1,0:T(8,128)S(1)}, u32[]{:S(2)}, u32[]{:S(2)}) %collective-permute-start.12) | collective-permute-done | bytes 65568 | tf_op jit(solution)/shard_map/ppermute | solution.py:355
  91.3 4.9 %second_rotation.1.rest_4_ = f32[256,128]{1,0:T(8,128)S(1)} custom-call(f32[128,128]{1,0:T(8,128)S(1)} %get-tuple-element.17.own_gram_ref, f32[128,128]{1,0:T(8,128)S(1)} %collective-permute-done.5.far_gram_ref, f32[128,128]{1,0:T(8,128)S(1)} %add.28.here_ref, f32[128,128]{1,0:T(8,128)S(1)} %collective-permute-done.12.there_ref), custom_call_target="tpu_custom_call" | custom-call | tf_op jit(solution)/shard_map/second_rotation/pallas_call | solution.py:283
  96.4 1.8 %pad_maximum_fusion.own_ref = f32[4096,128]{1,0:T(8,128)S(1)} fusion(f32[1024,128]{1,0:T(8,128)} %copy-done.9, f32[1024,128]{1,0:T(8,128)} %copy-done.7, f32[1024,128]{1,0:T(8,128)} %copy-done.8, f32[1024,128]{1,0:T(8,128)} %copy-done.6), kind=kLoop, calls=%fused_computation | loop fusion | flops 1572864 | bytes 4194304 | tf_op jit(solution)/shard_map/concatenate | solution.py:389
  98.2 3.4 %last_product.2.rest_2_ = f32[2,4096,128]{2,1,0:T(8,128)} custom-call(s32[1]{0:T(128)} %bitcast.slot_ref, f32[4096,128]{1,0:T(8,128)S(1)} %product.9.own_ref, f32[1024,128]{1,0:T(8,128)S(1)} %collective-permute-done.9.far_ref.rest_0_, f32[1024,128]{1,0:T(8,128)S(1)} %collective-permute-done.8.far_ref.rest_1_, f32[1024,128]{1,0:T(8,128)S(1)} %copy-done.3, ...), custom_call_target="tpu_custom_call" | custom-call | flops 805306368 | bytes 8388608 | tf_op jit(solution)/shard_map/last_product/pallas_call | solution.py:326
  101.6 4.7 %last_product.3 = f32[2,4096,128]{2,1,0:T(8,128)} custom-call(s32[1]{0:T(128)S(6)} %sub.3.slot_ref, f32[4096,128]{1,0:T(8,128)S(1)} %pad_maximum_fusion.own_ref, f32[4096,128]{1,0:T(8,128)} %collective-permute-done.4.rest_0_, f32[256,128]{1,0:T(8,128)S(1)} %collective-permute-done.13.rest_1_, ...), custom_call_target="tpu_custom_call", output_to_operand_aliasing={{}: (4, {})} | custom-call | flops 805306368 | bytes 8388608 | tf_op jit(solution)/shard_map/last_product/pallas_call | solution.py:326
  (38 shorter events, 4.2 us)
Async XLA Ops:
  0.0 2.2 %copy-start = (f32[2,4096,128]{2,1,0:T(8,128)S(1)}, f32[2,4096,128]{2,1,0:T(8,128)}, u32[]{:S(2)}) copy-start(f32[2,4096,128]{2,1,0:T(8,128)} %matrix_ref.11) | copy-start | bytes 12582916
  4.7 1.4 %collective-permute-start = (f32[136,128]{1,0:T(8,128)S(1)}, f32[136,128]{1,0:T(8,128)S(1)}, u32[]{:S(2)}, u32[]{:S(2)}) collective-permute-start(f32[136,128]{1,0:T(8,128)S(1)} %get-tuple-element.13), channel_id=1, source_target_pairs={{0,1},{1,0},{2,3},{3,2},{4,5},{5,4},{6,7},{7,6},{8,9},{9,8},{10,11... | collective-permute-start | bytes 208904 | tf_op jit(solution)/shard_map/ppermute | solution.py:365
  6.1 5.5 %collective-permute-start.1 = (f32[136,128]{1,0:T(8,128)S(1)}, f32[136,128]{1,0:T(8,128)S(1)}, u32[]{:S(2)}, u32[]{:S(2)}) collective-permute-start(f32[136,128]{1,0:T(8,128)S(1)} %add.24), channel_id=1, source_target_pairs={{0,2},{1,3},{2,0},{3,1},{4,6},{5,7},{6,4},{7,5},{8,10},{9,11},{10,... | collective-permute-start | bytes 208904 | tf_op jit(solution)/shard_map/ppermute | solution.py:360
  11.6 5.4 %collective-permute-start.2 = (f32[136,128]{1,0:T(8,128)S(1)}, f32[136,128]{1,0:T(8,128)S(1)}, u32[]{:S(2)}, u32[]{:S(2)}) collective-permute-start(f32[136,128]{1,0:T(8,128)S(1)} %add.25), channel_id=1, source_target_pairs={{0,4},{1,5},{2,6},{3,7},{4,0},{5,1},{6,2},{7,3},{8,12},{9,13},{10,... | collective-permute-start | bytes 208904 | tf_op jit(solution)/shard_map/ppermute | solution.py:360
  17.1 1.3 %collective-permute-start.3 = (f32[136,128]{1,0:T(8,128)S(1)}, f32[136,128]{1,0:T(8,128)S(1)}, u32[]{:S(2)}, u32[]{:S(2)}) collective-permute-start(f32[136,128]{1,0:T(8,128)S(1)} %add.26.mine_ref), channel_id=1, source_target_pairs={{0,1},{1,0},{2,3},{3,2},{4,5},{5,4},{6,7},{7,6},{8,9},{9,8},{10,11... | collective-permute-start | bytes 208904 | tf_op jit(solution)/shard_map/ppermute | solution.py:366
  23.3 6.1 %copy-start.1 = (f32[2,4096,128]{2,1,0:T(8,128)S(1)}, f32[2,4096,128]{2,1,0:T(8,128)}, u32[]{:S(2)}) copy-start(f32[2,4096,128]{2,1,0:T(8,128)} %matrix_ref.11) | copy-start | bytes 12582916
  27.8 73.8 %collective-permute-start.4 = (f32[4096,128]{1,0:T(8,128)S(1)}, f32[4096,128]{1,0:T(8,128)}, u32[]{:S(2)}, u32[]{:S(2)}) collective-permute-start(f32[4096,128]{1,0:T(8,128)S(1)} %product.9.own_ref), channel_id=1, source_target_pairs={{0,16},{1,9},{2,18},{3,11},{4,20},{5,13},{6,22},{7,15},{8,0},{9,25... | collective-permute-start | bytes 6291464 | tf_op jit(solution)/shard_map/ppermute | solution.py:355
  30.0 1.1 %copy-start.6 = (f32[1024,128]{1,0:T(8,128)}, f32[1024,128]{1,0:T(8,128)S(1)}, u32[]{:S(2)}) copy-start(f32[1024,128]{1,0:T(8,128)S(1)} %product.5) | copy-start | bytes 1572868
  30.0 14.9 %collective-permute-start.9 = (f32[1024,128]{1,0:T(8,128)S(1)}, f32[1024,128]{1,0:T(8,128)S(1)}, u32[]{:S(2)}, u32[]{:S(2)}) collective-permute-start(f32[1024,128]{1,0:T(8,128)S(1)} %product.5), channel_id=1, source_target_pairs={{0,8},{1,17},{2,10},{3,19},{4,12},{5,21},{6,14},{7,23},{8,24},{9,1... | collective-permute-start | bytes 1572872 | tf_op jit(solution)/shard_map/ppermute | solution.py:355
  31.1 2.2 %copy-start.7 = (f32[1024,128]{1,0:T(8,128)}, f32[1024,128]{1,0:T(8,128)S(1)}, u32[]{:S(2)}) copy-start(f32[1024,128]{1,0:T(8,128)S(1)} %product.7) | copy-start | bytes 1572868
  31.7 3.7 %copy-start.8 = (f32[1024,128]{1,0:T(8,128)}, f32[1024,128]{1,0:T(8,128)S(1)}, u32[]{:S(2)}) copy-start(f32[1024,128]{1,0:T(8,128)S(1)} %product.6) | copy-start | bytes 1572868
  31.7 24.5 %collective-permute-start.8 = (f32[1024,128]{1,0:T(8,128)S(1)}, f32[1024,128]{1,0:T(8,128)S(1)}, u32[]{:S(2)}, u32[]{:S(2)}) collective-permute-start(f32[1024,128]{1,0:T(8,128)S(1)} %product.6), channel_id=1, source_target_pairs={{0,8},{1,17},{2,10},{3,19},{4,12},{5,21},{6,14},{7,23},{8,24},{9,1... | collective-permute-start | bytes 1572872 | tf_op jit(solution)/shard_map/ppermute | solution.py:355
  33.3 34.1 %collective-permute-start.7 = (f32[1024,128]{1,0:T(8,128)S(1)}, f32[1024,128]{1,0:T(8,128)S(1)}, u32[]{:S(2)}, u32[]{:S(2)}) collective-permute-start(f32[1024,128]{1,0:T(8,128)S(1)} %product.7), channel_id=1, source_target_pairs={{0,8},{1,17},{2,10},{3,19},{4,12},{5,21},{6,14},{7,23},{8,24},{9,1... | collective-permute-start | bytes 1572872 | tf_op jit(solution)/shard_map/ppermute | solution.py:355
  35.4 21.2 %copy-start.9 = (f32[1024,128]{1,0:T(8,128)}, f32[1024,128]{1,0:T(8,128)S(1)}, u32[]{:S(2)}) copy-start(f32[1024,128]{1,0:T(8,128)S(1)} %product.8) | copy-start | bytes 1572868
  35.4 40.1 %collective-permute-start.6 = (f32[1024,128]{1,0:T(8,128)S(1)}, f32[1024,128]{1,0:T(8,128)S(1)}, u32[]{:S(2)}, u32[]{:S(2)}) collective-permute-start(f32[1024,128]{1,0:T(8,128)S(1)} %product.8), channel_id=1, source_target_pairs={{0,8},{1,17},{2,10},{3,19},{4,12},{5,21},{6,14},{7,23},{8,24},{9,1... | collective-permute-start | bytes 1572872 | tf_op jit(solution)/shard_map/ppermute | solution.py:355
  67.4 8.6 %copy-start.2 = (f32[1024,128]{1,0:T(8,128)}, f32[1024,128]{1,0:T(8,128)S(1)}, u32[]{:S(2)}) copy-start(f32[1024,128]{1,0:T(8,128)S(1)} %collective-permute-done.7.far_ref.rest_2_) | copy-start | bytes 1572868
  75.5 9.2 %copy-start.4 = (f32[1024,128]{1,0:T(8,128)}, f32[1024,128]{1,0:T(8,128)S(1)}, u32[]{:S(2)}) copy-start(f32[1024,128]{1,0:T(8,128)S(1)} %collective-permute-done.6.far_ref.rest_3_) | copy-start | bytes 1572868
  76.0 4.7 %collective-permute-start.10 = (f32[128,128]{1,0:T(8,128)S(1)}, f32[128,128]{1,0:T(8,128)S(1)}, u32[]{:S(2)}, u32[]{:S(2)}) collective-permute-start(f32[128,128]{1,0:T(8,128)S(1)} %cross_gram.7), channel_id=1, source_target_pairs={{0,2},{1,3},{2,0},{3,1},{4,6},{5,7},{6,4},{7,5},{8,10},{9,11},{10,... | collective-permute-start | bytes 196616 | tf_op jit(solution)/shard_map/ppermute | solution.py:360
  80.7 6.9 %collective-permute-start.11 = (f32[128,128]{1,0:T(8,128)S(1)}, f32[128,128]{1,0:T(8,128)S(1)}, u32[]{:S(2)}, u32[]{:S(2)}) collective-permute-start(f32[128,128]{1,0:T(8,128)S(1)} %add.27), channel_id=1, source_target_pairs={{0,4},{1,5},{2,6},{3,7},{4,0},{5,1},{6,2},{7,3},{8,12},{9,13},{10,... | collective-permute-start | bytes 196616 | tf_op jit(solution)/shard_map/ppermute | solution.py:360
  84.7 4.5 %collective-permute-start.5 = (f32[128,128]{1,0:T(8,128)S(1)}, f32[128,128]{1,0:T(8,128)S(1)}, u32[]{:S(2)}, u32[]{:S(2)}) collective-permute-start(f32[128,128]{1,0:T(8,128)S(1)} %get-tuple-element.18), channel_id=1, source_target_pairs={{0,8},{1,17},{2,10},{3,19},{4,12},{5,21},{6,14},{7,23},{8,24},{9,1... | collective-permute-start | bytes 196616 | tf_op jit(solution)/shard_map/ppermute | solution.py:355
  87.6 3.8 %collective-permute-start.12 = (f32[128,128]{1,0:T(8,128)S(1)}, f32[128,128]{1,0:T(8,128)S(1)}, u32[]{:S(2)}, u32[]{:S(2)}) collective-permute-start(f32[128,128]{1,0:T(8,128)S(1)} %add.28.here_ref), channel_id=1, source_target_pairs={{0,17},{1,8},{2,19},{3,10},{4,21},{5,12},{6,23},{7,14},{8,1},{9,24... | collective-permute-start | bytes 196616 | tf_op jit(solution)/shard_map/ppermute | solution.py:355
  96.2 2.0 %copy-start.3 = (f32[1024,128]{1,0:T(8,128)S(1)}, f32[1024,128]{1,0:T(8,128)}, u32[]{:S(2)}) copy-start(f32[1024,128]{1,0:T(8,128)} %copy-done.2) | copy-start | bytes 1572868
  96.2 2.0 %copy-start.5 = (f32[1024,128]{1,0:T(8,128)S(1)}, f32[1024,128]{1,0:T(8,128)}, u32[]{:S(2)}) copy-start(f32[1024,128]{1,0:T(8,128)} %copy-done.4) | copy-start | bytes 1572868
  96.2 5.4 %collective-permute-start.13 = (f32[256,128]{1,0:T(8,128)S(1)}, f32[256,128]{1,0:T(8,128)S(1)}, u32[]{:S(2)}, u32[]{:S(2)}) collective-permute-start(f32[256,128]{1,0:T(8,128)S(1)} %second_rotation.1.rest_4_), channel_id=1, source_target_pairs={{0,1},{1,0},{2,3},{3,2},{4,5},{5,4},{6,7},{7,6},{8,9},{9,8},{10,11... | collective-permute-start | bytes 393224 | tf_op jit(solution)/shard_map/ppermute | solution.py:383

commit v2 on v0

v2 whole, which is shorter than its diff:
```python
import functools

import jax
import jax.numpy as jnp
from jax import lax
from jax.experimental import pallas as pl
from jax.experimental.pallas import tpu as pltpu
from jax.sharding import PartitionSpec as P


F32 = jnp.float32
BF16 = jnp.bfloat16
SCOPED = 16 * 1024 * 1024
WHOLE = 54 * 1024 * 1024

RAW = (5,)
LAST = 2
BULK = 12
STEP = 2


def after(p, n):
    if p == 0:
        return 1
    if p % 2:
        return n - 2 if p == n - 1 else p + 2
    return p - 2


def halves(x):
    high = x.astype(BF16)
    return high, (x - high.astype(F32)).astype(BF16)


def dot(left, right, contract=((1,), (0,))):
    return lax.dot_general(left, right, (contract, ((), ())), preferred_element_type=F32)


def product(left, right):
    width = right.shape[1]
    twice = jnp.concatenate(halves(right), 1)
    both = dot(jnp.concatenate(halves(left), 1), jnp.concatenate([twice, twice], 0))
    return both[:, :width] + both[:, width:]


def right_parts(right):
    high, low = halves(right)
    return jnp.concatenate([high, low], 1), high


def rows_product(left, parts):
    width = parts[1].shape[1]
    high, low = halves(left)
    both = dot(high, parts[0])
    return both[:, :width] + (both[:, width:] + dot(low, parts[1]))


def eye_of(width):
    rows = lax.broadcasted_iota(jnp.int32, (width, width), 0)
    cols = lax.broadcasted_iota(jnp.int32, (width, width), 1)
    return rows, cols


def polar(cross, sign):
    rows, cols = eye_of(cross.shape[0])
    unit = (rows == cols).astype(F32)
    flipped = cross.T
    s = [product(cross, flipped), product(flipped, cross)]
    s2 = [product(a, a) for a in s]
    e = [0.75 * b - 0.25 * product(b, a) for a, b in zip(s, s2)]
    e2 = [product(a, a) for a in e]
    z = [unit - 0.5 * a + 0.5 * b - 0.25 * product(a, b) for a, b in zip(s, e)]
    f = [0.75 * b + 0.25 * product(b, a) for a, b in zip(e, e2)]
    xz = product(cross, z[1])
    last = [a + 0.5 * product(a, b) for a, b in zip(z, f)]
    wide = sign * (xz + 0.5 * product(xz, f[1]))
    return jnp.concatenate(
        [jnp.concatenate([last[0], wide], 1), jnp.concatenate([-wide.T, last[1]], 1)], 0
    )


def scaled(cross, down, across):
    x = cross * lax.rsqrt(down + 1e-06) * lax.rsqrt(across + 1e-06)
    return x / (1.0 + jnp.sqrt(jnp.sum(x * x)))


def rotation_of(upper, cross, lower, sign):
    width = cross.shape[0]
    rows, cols = eye_of(width)
    same = rows == cols
    zero = jnp.zeros((width, width), F32)
    down = jnp.sum(jnp.where(same, upper, zero), 1, keepdims=True)
    across = jnp.sum(jnp.where(same, lower, zero), 0, keepdims=True)
    first = polar(scaled(cross, down, across), sign)
    gram = jnp.concatenate(
        [jnp.concatenate([upper, cross], 1), jnp.concatenate([cross.T, lower], 1)], 0
    )
    turned = rows_product(gram, right_parts(first))
    second_cross = rows_product(first[:, :width].T, right_parts(turned[:, width:]))
    diagonal = jnp.sum(first * turned, 0, keepdims=True)
    down = jnp.sum(jnp.where(same, diagonal[:, :width], zero), 1, keepdims=True)
    second = polar(scaled(second_cross, down, diagonal[:, width:]), sign)
    return gram, rows_product(first, right_parts(second))


def core_of():
    return lax.rem(lax.axis_index("row"), 2)


def first_is_upper():
    p = lax.axis_index("pair")
    clock_upper = (p == 0) | (lax.rem(p, 2) == 1)
    return (core_of() == 0) == clock_upper


def call(kernel, outs, args, name, flops=0, scratch=(), aliases=None, limit=SCOPED):
    places = [place for _, place in args]
    out_places = [place for _, place in outs]
    return pl.pallas_call(
        kernel,
        in_specs=[pl.BlockSpec(memory_space=place) for place in places],
        out_specs=[pl.BlockSpec(memory_space=place) for place in out_places],
        out_shape=[place(shape, F32) if place == pltpu.VMEM and PIN else jax.ShapeDtypeStruct(shape, F32) for shape, place in outs],
        scratch_shapes=list(scratch),
        input_output_aliases=aliases or {},
        compiler_params=pltpu.CompilerParams(vmem_limit_bytes=limit),
        cost_estimate=pl.CostEstimate(flops=flops if flops == LONG else 0, bytes_accessed=0, transcendentals=0),
        name=name,
    )(*[pltpu.with_memory_space_constraint(array, place) for array, place in args])


PIN = True
LONG = 11500000000
HERE = pltpu.VMEM
FAR = pltpu.HBM


class Rows:
    def __init__(self, *parts):
        self.parts = parts

    @classmethod
    def of(cls, refs, sizes):
        return cls(*[(ref, sum(sizes[:k]), sizes[k], 0) for k, ref in enumerate(refs)])

    def at(self, start, count):
        for ref, first, number, offset in self.parts:
            if first <= start and start + count <= first + number:
                return ref, pl.ds(offset + start - first, count)
        raise ValueError(start)

    def get(self, start, count):
        ref, rows = self.at(start, count)
        return ref[rows, :]

    def pair(self, start, count):
        ref, rows = self.at(start, count)
        return jnp.concatenate([ref[0, rows, :], ref[1, rows, :]], 1)


def spans(start, stop, step, *cuts):
    pieces = []
    while start < stop:
        count = min([step, stop - start] + [cut - start for cut in cuts if cut > start])
        pieces.append((start, count))
        start += count
    return pieces


def local_gram(matrix, sizes, step):
    rows, width = matrix.shape[1:]
    pieces = spans(0, rows, step, *[sum(sizes[:k]) for k in range(len(sizes))])

    def kernel(matrix_ref, *refs):
        part_refs, (keep_ref, give_ref, sems) = refs[: len(sizes)], refs[len(sizes) :]
        local = Rows.of(part_refs, sizes)
        copies = []
        for k, (start, count) in enumerate(pieces):
            ref, place = local.at(start, count)
            copies.append(pltpu.make_async_copy(matrix_ref.at[:, pl.ds(start, count)], ref.at[:, place], sems.at[k]))
            copies[-1].start()
        total = jnp.zeros((2 * width, 4 * width), F32)
        for copy, (start, count) in zip(copies, pieces):
            copy.wait()
            high, low = halves(local.pair(start, count))
            total = total + dot(high, jnp.concatenate([high, low], 1), ((0,), (0,)))
        rest = total[:, 2 * width :]
        total = total[:, : 2 * width] + (rest + rest.T)
        upper, cross, lower = total[:width, :width], total[:width, width:], total[width:, width:]
        r, c = eye_of(width)
        diagonal = jnp.sum(jnp.where(r == c, lower, jnp.zeros_like(lower)), 0, keepdims=True)
        packed = jnp.where(r <= c, upper, lower)
        pad = jnp.broadcast_to(diagonal, (8, width))
        mine = core_of() == 0
        keep_ref[:width] = jnp.where(mine, cross, packed)
        give_ref[:width] = jnp.where(mine, packed, cross)
        keep_ref[width:] = pad
        give_ref[width:] = pad

    outs = [((2, size, width), HERE) for size in sizes] + [((width + 8, width), HERE)] * 2
    return call(
        kernel,
        outs,
        [(matrix, FAR)],
        "gram",
        16 * rows * width * width,
        [pltpu.SemaphoreType.DMA((len(pieces),))],
        limit=WHOLE,
    )


def first_rotation(mine, other):
    width = mine.shape[1]

    def kernel(mine_ref, other_ref, first_ref, second_ref, gram_ref):
        holds_cross = core_of() == 0
        mine, other = mine_ref[...], other_ref[...]
        cross = jnp.where(holds_cross, mine[:width], other[:width])
        packed = jnp.where(holds_cross, other, mine)
        diagonal = packed[width : width + 1]
        packed = packed[:width]
        rows, cols = eye_of(width)
        flipped = packed.T
        upper = jnp.where(rows <= cols, packed, flipped)
        lower = jnp.where(rows > cols, packed, flipped)
        lower = jnp.where(rows == cols, diagonal, lower)
        gram, rotation = rotation_of(upper, cross, lower, 1.0)
        left, right = rotation[:, :width], rotation[:, width:]
        upper_first = first_is_upper()
        first_ref[...] = jnp.where(upper_first, left, right)
        second_ref[...] = jnp.where(upper_first, right, left)
        gram_ref[...] = gram

    half = ((2 * width, width), HERE)
    return call(kernel, [half, half, ((2 * width, 2 * width), HERE)], [(mine, HERE), (other, HERE)], "first_rotation")


def sent_parts(high, first, second, gram, early, last, step):
    width = first.shape[1]
    count = high.shape[1]

    def kernel(high_ref, first_ref, second_ref, gram_ref, main_ref, last_ref, second_gram_ref):
        local = Rows((high_ref, 0, count, 0))
        out = Rows((main_ref, 0, count - last, 2 * width), (last_ref, count - last, last, 0))
        main_ref[: 2 * width] = first_ref[...]
        parts = right_parts(first_ref[...])
        for start, number in spans(0, count, step, count - last):
            ref, place = out.at(start, number)
            ref[place, :] = rows_product(local.pair(start, number), parts)
        gram = gram_ref[...]
        for turn_ref, place in ((first_ref, last_ref.at[pl.ds(last, width), :]), (second_ref, second_gram_ref)):
            turn = turn_ref[...]
            place[...] = rows_product(turn.T, right_parts(rows_product(gram, right_parts(turn))))

    return call(
        kernel,
        [((2 * width + count - last, width), HERE), ((last + width, width), HERE), ((width, width), HERE)],
        [(high, HERE), (first, HERE), (second, HERE), (gram, HERE)],
        "sent_parts",
        12 * count * width * width,
    )


def rest_parts(local, first, second, bulk, early, step):
    width = first.shape[1]
    sizes = [part.shape[1] for part in local]
    rows = sum(sizes)

    def kernel(*refs):
        part_refs, (first_ref, second_ref, bulk_ref, tail_ref, raw_ref) = refs[: len(sizes)], refs[len(sizes) :]
        here = Rows.of(part_refs, sizes)
        out = Rows.of((bulk_ref, tail_ref), (bulk, rows - bulk))
        parts = right_parts(second_ref[...])
        for start, count in spans(0, rows, step, bulk, early):
            ref, place = out.at(start, count)
            ref[place, :] = rows_product(here.pair(start, count), parts)
        parts = right_parts(first_ref[...])
        for start, count in spans(0, early, step):
            raw_ref[pl.ds(start, count), :] = rows_product(here.pair(start, count), parts)

    return call(
        kernel,
        [((bulk, width), HERE), ((rows - bulk, width), HERE), ((early, width), HERE)],
        [(part, HERE) for part in local] + [(first, HERE), (second, HERE)],
        "rest_parts",
        12 * (rows + early) * width * width,
    )


def cross_term(own, far):
    return dot(jnp.concatenate(halves(own), 1), jnp.concatenate(halves(far), 1), ((0,), (0,)))


def cross_sum(total):
    width = total.shape[0] // 2
    return (total[:width, :width] + total[:width, width:]) + (total[width:, :width] + total[width:, width:])


def main_cross(far_raw, far_main, bulk, tail, step):
    width = bulk.shape[1]
    sizes = [part.shape[1] for part in far_raw]
    early, main = sum(sizes), far_main.shape[0] - 2 * width

    def kernel(*refs):
        raw_refs, (main_ref, bulk_ref, tail_ref, far_ref, out_ref) = refs[: len(sizes)], refs[len(sizes) :]
        own = Rows.of((bulk_ref, tail_ref), (bulk.shape[0], tail.shape[0]))
        raw = Rows.of(raw_refs, sizes)
        far = Rows((main_ref, early, main, 2 * width))
        parts = right_parts(main_ref[: 2 * width])
        total = jnp.zeros((2 * width, 2 * width), F32)
        for start, count in spans(0, early + main, step, early, bulk.shape[0]):
            if start < early:
                block = rows_product(raw.pair(start, count), parts)
                far_ref[pl.ds(start, count), :] = block
            else:
                block = far.get(start, count)
            total = total + cross_term(own.get(start, count), block)
        out_ref[...] = cross_sum(total)

    return call(
        kernel,
        [((early, width), HERE), ((width, width), HERE)],
        [(part, HERE) for part in far_raw] + [(far_main, HERE), (bulk, HERE), (tail, HERE)],
        "main_cross",
        12 * (early + main) * width * width,
    )


def last_cross(far_last, bulk, tail, so_far, step):
    width = bulk.shape[1]
    count = far_last.shape[0] - width
    rows = bulk.shape[0] + tail.shape[0]

    def kernel(far_ref, bulk_ref, tail_ref, total_ref, out_ref):
        own = Rows((bulk_ref, 0, bulk.shape[0], 0), (tail_ref, bulk.shape[0], tail.shape[0], 0))
        far = Rows((far_ref, rows - count, count, 0))
        total = jnp.zeros((2 * width, 2 * width), F32)
        for start, number in spans(rows - count, rows, step, bulk.shape[0]):
            total = total + cross_term(own.get(start, number), far.get(start, number))
        out_ref[...] = total_ref[...] + cross_sum(total)

    return call(
        kernel,
        [((width, width), HERE)],
        [(far_last, HERE), (bulk, HERE), (tail, HERE), (so_far, HERE)],
        "last_cross",
        6 * count * width * width,
    )[0]


def second_rotation(own_gram, far_sent, here, there):
    width = here.shape[1]
    place = far_sent.shape[0] - width

    def kernel(own_gram_ref, far_ref, here_ref, there_ref, out_ref):
        p, n = lax.axis_index("pair"), lax.axis_size("pair")
        odd = lax.rem(p, 2) == 1
        outward = core_of() == 1
        own_upper_out = (p == 0) | (odd & (p != n - 1))
        own_upper = (outward & own_upper_out) | (jnp.logical_not(outward) & jnp.logical_not(odd))
        sign = jnp.where(own_upper, 1.0, -1.0).astype(F32)
        cross = here_ref[...] + there_ref[...].T
        _, rotation = rotation_of(own_gram_ref[...], cross, far_ref[pl.ds(place, width), :], sign)
        keeps_own = (outward & (p == 0)) | (jnp.logical_not(outward) & (p == 1))
        out_ref[...] = jnp.where(keeps_own, rotation[:, :width], rotation[:, width:])

    return call(
        kernel,
        [((2 * width, width), HERE)],
        [(own_gram, HERE), (far_sent, HERE), (here, HERE), (there, HERE)],
        "second_rotation",
        LONG,
    )[0]


def last_product(own, far, turn, done, slot_of, start, count, rows, step, name):
    width = turn.shape[1]
    arrays = [array for array, *_ in own + far]
    pieces = spans(start, start + count, step, *[first for _, first, *_ in own + far])

    def kernel(*refs):
        n = len(arrays)
        turn_ref = refs[n]
        out_ref, stage_ref, sems = refs[-3], refs[-2], refs[-1]
        mine = Rows(*[(ref, *where) for ref, (_, *where) in zip(refs[: len(own)], own)])
        others = Rows(*[(ref, *where) for ref, (_, *where) in zip(refs[len(own) : n], far)])
        parts = right_parts(turn_ref[...])
        slot = slot_of()
        copies = []
        for k, (row, number) in enumerate(pieces):
            block = jnp.concatenate([mine.get(row, number), others.get(row, number)], 1)
            place = pl.ds(row - start, number)
            stage_ref[place, :] = rows_product(block, parts)
            copies.append(
                pltpu.make_async_copy(stage_ref.at[place, :], out_ref.at[slot, pl.ds(row, number), :], sems.at[k])
            )
            copies[-1].start()
        for copy in copies:
            copy.wait()

    args = [(array, HERE) for array in arrays] + [(turn, HERE)] + ([] if done is None else [(done, FAR)])
    return call(
        kernel,
        [((2, rows, width), FAR)],
        args,
        name,
        12 * count * width * width,
        [pltpu.VMEM((count, width), F32), pltpu.SemaphoreType.DMA((len(pieces),))],
        None if done is None else {len(args) - 1: 0},
    )[0]


def first_slot():
    return jnp.where(lax.rem(lax.axis_index("pair"), 2) == core_of(), 1, 0)


def body(pairs_count, rows_count, matrix):
    rows, width = matrix.shape[1:]
    unit = rows // 16
    last, bulk, step = LAST * unit, BULK * unit, STEP * unit
    raw_sizes = [part * unit for part in RAW if part]
    early = sum(raw_sizes)
    flat = [(p, r) for p in range(pairs_count) for r in range(rows_count)]
    ahead = {p: after(p, pairs_count) for p in range(pairs_count)}
    behind = {q: p for p, q in ahead.items()}

    def route(moves):
        return [(p * rows_count + r, q * rows_count + t) for (p, r) in flat for (q, t) in [moves(p, r)]]

    outward = route(lambda p, r: (ahead[p] if r % 2 == 0 else behind[p], r))
    inward = route(lambda p, r: (behind[p] if r % 2 == 0 else ahead[p], r))

    core = [(r, r ^ 1) for r in range(rows_count)]

    def travel(block, moves):
        return lax.ppermute(block, ("pair", "row"), moves)

    def chip_sum(block, flip=0):
        distance = 2
        while distance < rows_count:
            steps = [distance] if 2 * distance >= rows_count else [distance, 2 * distance, 3 * distance]
            hops = [d ^ flip for d in steps] + ([1] if flip else [])
            others = [lax.ppermute(block, "row", [(r, r ^ d) for r in range(rows_count)]) for d in hops]
            block = others.pop() if flip else block
            for other in others:
                block = block + other
            distance *= 1 + len(steps)
            flip = 0
        return block

    def other_sum(block):
        return chip_sum(block, 1)

    *local, keep, give = local_gram(matrix, raw_sizes + [rows - early], step)
    high = local[-1]
    far_raw = [travel(part, outward) for part in local[:-1]]
    mine = chip_sum(keep + lax.ppermute(give, "row", core))
    other = lax.ppermute(mine, "row", core)
    turn_first, turn_second, gram = first_rotation(mine, other)
    turn_first, *far_raw = lax.optimization_barrier((turn_first, *far_raw))

    sent_main, sent_last, second_gram = sent_parts(high, turn_first, turn_second, gram, early, last, step)
    far_main, far_last = travel(sent_main, outward), travel(sent_last, outward)
    turn_second, sent_main = lax.optimization_barrier((turn_second, sent_main))
    second_bulk, second_tail, first_raw = rest_parts(local, turn_first, turn_second, bulk, early, step)

    far_rotated, cross = main_cross(far_raw, far_main, second_bulk, second_tail, step)
    cross, later_bulk, later_tail = lax.optimization_barrier((cross, second_bulk, second_tail))
    far_bulk, far_tail = travel(later_bulk, inward), travel(later_tail, inward)
    cross = last_cross(far_last, second_bulk, second_tail, cross, step)

    total = other_sum(cross)
    there = travel(total, outward)
    here = lax.ppermute(total, "row", core)
    turn_here = second_rotation(second_gram, far_last, here, there)
    turn_there = lax.ppermute(turn_here, "row", core)

    main = rows - early - last
    first = [(first_raw, 0, early, 0), (sent_main, early, main, 2 * width), (sent_last, early + main, last, 0)]
    far_first = [(far_rotated, 0, early, 0), (far_main, early, main, 2 * width), (far_last, early + main, last, 0)]
    second = [(second_bulk, 0, bulk, 0), (second_tail, bulk, rows - bulk, 0)]
    done = last_product(second, far_first, turn_here, None, first_slot, 0, rows, rows, step, "here_product")

    def other_slot():
        return 1 - first_slot()

    done = last_product(first, [(far_bulk, 0, bulk, 0)], turn_there, done, other_slot, 0, bulk, rows, step, "bulk_product")
    return last_product(
        first, [(far_tail, bulk, rows - bulk, 0)], turn_there, done, other_slot, bulk, rows - bulk, rows, step, "tail_product"
    )


def solution(mesh):
    spec = P(None, "row", "pair")
    run = functools.partial(body, mesh.shape["pair"], mesh.shape["row"])
    return jax.shard_map(run, mesh=mesh, in_specs=(spec,), out_specs=spec, check_vma=False)
```

time: 395 us -> 72.9 us (0.18); the launches traced: 389 us -> 72.7 us
  waiting for transfers between devices: 288 us -> 33.3 us
  matrix products: 35.4 us -> 0 us
  local copies, waits for them, and re-layouts: 23.5 us -> 0 us
  Pallas kernels: 0 us -> 21.3 us
  between operations: 16.8 us -> 0.29 us
  other arithmetic: 15 us -> 0.05 us
  starting transfers between devices: 10.4 us -> 17.7 us
    ppermute x4 -> x17, waiting for transfers between devices: 176 us -> 33.3 us  [the longest x6 20 us: travel(): return lax.ppermute(block, ('pair', 'row'), moves)]
    psum x2 -> x0, waiting for transfers between devices: 112 us -> none  [body(): gram_matrix = lax.psum(gram_of(pair_cols, pair_cols), 'row')]
    dot_general x36 -> x0, matrix products: 35.4 us -> none  [the longest x16 19.7 us: gram_of(): lax.dot_general(left_cols, right_cols, (((0,), (0,)), ((), ())), precisio...]
    pallas_call x0 -> x10, Pallas kernels: none -> 21.3 us  [call(): pl.pallas_call(kernel, in_specs=[pl.BlockSpec(memory_space=place) for pla...]
    gather x4 -> x0, local copies, waits for them, and re-layouts: 10.2 us -> none  [polar_turn(): diagonal = jnp.diagonal(gram_matrix)]
    ppermute x4 -> x17, starting transfers between devices: 9.8 us -> 17.7 us  [the longest x7 8.74 us: chip_sum(): lax.ppermute(block, 'row', [(r, r ^ d) for r in range(rows_count)])]
    another operation x1 -> x0, local copies, waits for them, and re-layouts: 5.59 us -> none  [body(): return jnp.stack([upper_block, lower_block], 0)]
    select_n x3 -> x0, other arithmetic: 5.48 us -> none  [the longest x2 2.89 us: plain_move(): outgoing = jnp.where(position == 0, lower_block, upper_block)]
  transfers between devices with their start and end apart: 6 -> 17, of which waited for: 6 -> 10; matrix products, arithmetic and copies ran while one was open for 0% -> 0% of each run, Pallas kernels for 0% -> 20%
where the time goes in v2:
time: 72.9 us; the launch traced here: 72.7 us
  waiting for transfers between devices  33.3 us (46%)
  Pallas kernels  21.3 us (29%)
  starting transfers between devices  17.7 us (24%)
    pallas_call x10, Pallas kernels, call(): pl.pallas_call(kernel, in_specs=[pl.BlockSpec(memory_space=place) for pla...  21.3 us
    ppermute x6, waiting for transfers between devices, travel(): return lax.ppermute(block, ('pair', 'row'), moves)  20 us
    ppermute x7, waiting for transfers between devices, chip_sum(): lax.ppermute(block, 'row', [(r, r ^ d) for r in range(rows_count)])  10.8 us
    ppermute x7, starting transfers between devices, chip_sum(): lax.ppermute(block, 'row', [(r, r ^ d) for r in range(rows_count)])  8.74 us
    ppermute x6, starting transfers between devices, travel(): return lax.ppermute(block, ('pair', 'row'), moves)  8.66 us
  transfers between devices with their start and end apart: 17, of which 10 were waited for; matrix products, arithmetic and copies ran while one was open for 0% of the time, Pallas kernels for 20%

profile of v2, /device:TPU:0, one launch (start us, length us, event | category | flops | bytes accessed | tf_op | source)
XLA Modules:
  0.0 72.7 jit_solution(14153297451079294689)
XLA Ops:
  0.0 4.0 %gram.1 = (f32[2,1280,128]{2,1,0:T(8,128)S(1)}, f32[2,2816,128]{2,1,0:T(8,128)S(1)}, f32[136,128]{1,0:T(8,128)S(1)}, f32[136,128]{1,0:T(8,128)S(1)}) custom-call(f32[2,4096,128]{2,1,0:T(8,128)} %matrix_ref.1), custom_call_target="tpu_custom_call" | custom-call | tf_op jit(solution)/shard_map/gram/pallas_call | solution.py:119
  4.0 3.0 %collective-permute-start.5 = (f32[2,1280,128]{2,1,0:T(8,128)S(1)}, f32[2,1280,128]{2,1,0:T(8,128)S(1)}, u32[]{:S(2)}, u32[]{:S(2)}) collective-permute-start(f32[2,1280,128]{2,1,0:T(8,128)S(1)} %get-tuple-element.27.refs_0_), channel_id=1, source_target_pairs={{0,8},{1,17},{2,10},{3,19},{4,12},{5,21},{6,14},{7,23},{8,24},{9,1... | collective-permute-start | bytes 3932168 | tf_op jit(solution)/shard_map/ppermute | solution.py:436
  7.0 1.3 %collective-permute-done = f32[136,128]{1,0:T(8,128)S(1)} collective-permute-done((f32[136,128]{1,0:T(8,128)S(1)}, f32[136,128]{1,0:T(8,128)S(1)}, u32[]{:S(2)}, u32[]{:S(2)}) %collective-permute-start) | collective-permute-done | bytes 69664 | tf_op jit(solution)/shard_map/ppermute | solution.py:457
  8.2 1.6 %collective-permute-start.1 = (f32[136,128]{1,0:T(8,128)S(1)}, f32[136,128]{1,0:T(8,128)S(1)}, u32[]{:S(2)}, u32[]{:S(2)}) collective-permute-start(f32[136,128]{1,0:T(8,128)S(1)} %add.21), channel_id=1, source_target_pairs={{0,2},{1,3},{2,0},{3,1},{4,6},{5,7},{6,4},{7,5},{8,10},{9,11},{10,... | collective-permute-start | bytes 208904 | tf_op jit(solution)/shard_map/ppermute | solution.py:443
  9.9 2.6 %collective-permute-start.2 = (f32[136,128]{1,0:T(8,128)S(1)}, f32[136,128]{1,0:T(8,128)S(1)}, u32[]{:S(2)}, u32[]{:S(2)}) collective-permute-start(f32[136,128]{1,0:T(8,128)S(1)} %add.21), channel_id=1, source_target_pairs={{0,4},{1,5},{2,6},{3,7},{4,0},{5,1},{6,2},{7,3},{8,12},{9,13},{10,... | collective-permute-start | bytes 208904 | tf_op jit(solution)/shard_map/ppermute | solution.py:443
  12.5 0.2 collective-permute-start.3
  12.7 5.0 %collective-permute-done.2 = f32[136,128]{1,0:T(8,128)S(1)} collective-permute-done((f32[136,128]{1,0:T(8,128)S(1)}, f32[136,128]{1,0:T(8,128)S(1)}, u32[]{:S(2)}, u32[]{:S(2)}) %collective-permute-start.2) | collective-permute-done | bytes 69664 | tf_op jit(solution)/shard_map/ppermute | solution.py:443
  17.7 1.0 %collective-permute-done.3 = f32[136,128]{1,0:T(8,128)S(1)} collective-permute-done((f32[136,128]{1,0:T(8,128)S(1)}, f32[136,128]{1,0:T(8,128)S(1)}, u32[]{:S(2)}, u32[]{:S(2)}) %collective-permute-start.3) | collective-permute-done | bytes 69664 | tf_op jit(solution)/shard_map/ppermute | solution.py:443
  18.8 1.2 %collective-permute-done.4.other_ref = f32[136,128]{1,0:T(8,128)S(1)} collective-permute-done((f32[136,128]{1,0:T(8,128)S(1)}, f32[136,128]{1,0:T(8,128)S(1)}, u32[]{:S(2)}, u32[]{:S(2)}) %collective-permute-start.4) | collective-permute-done | bytes 69664 | tf_op jit(solution)/shard_map/ppermute | solution.py:458
  20.0 3.7 %first_rotation.1 = (f32[256,128]{1,0:T(8,128)S(1)}, f32[256,128]{1,0:T(8,128)S(1)}, f32[256,256]{1,0:T(8,128)S(1)}) custom-call(f32[136,128]{1,0:T(8,128)S(1)} %add_add_fusion.mine_ref, f32[136,128]{1,0:T(8,128)S(1)} %collective-permute-done.4.other_ref), custom_call_target="tpu_custom_call" | custom-call | tf_op jit(solution)/shard_map/first_rotation/pallas_call | solution.py:119
  23.7 1.4 %sent_parts.1 = (f32[2560,128]{1,0:T(8,128)S(1)}, f32[640,128]{1,0:T(8,128)S(1)}, f32[128,128]{1,0:T(8,128)S(1)}) custom-call(f32[2,2816,128]{2,1,0:T(8,128)S(1)} %get-tuple-element.28.high_ref.refs_1_, f32[256,128]{1,0:T(8,128)S(1)} %get-tuple-element.32.first_ref.refs_2_, f32[256,128]{1,0:T(8,128)S(1)} %get-tuple-element.36.second_ref.refs_3_, ...), custom_call_target="tpu_custom_call" | custom-call | tf_op jit(solution)/shard_map/sent_parts/pallas_call | solution.py:119
  25.1 1.6 %collective-permute-start.6 = (f32[2560,128]{1,0:T(8,128)S(1)}, f32[2560,128]{1,0:T(8,128)S(1)}, u32[]{:S(2)}, u32[]{:S(2)}) collective-permute-start(f32[2560,128]{1,0:T(8,128)S(1)} %get-tuple-element.38.refs_1_), channel_id=1, source_target_pairs={{0,8},{1,17},{2,10},{3,19},{4,12},{5,21},{6,14},{7,23},{8,24},{9,1... | collective-permute-start | bytes 3932168 | tf_op jit(solution)/shard_map/ppermute | solution.py:436
  26.7 0.8 %collective-permute-start.8 = (f32[640,128]{1,0:T(8,128)S(1)}, f32[640,128]{1,0:T(8,128)S(1)}, u32[]{:S(2)}, u32[]{:S(2)}) collective-permute-start(f32[640,128]{1,0:T(8,128)S(1)} %get-tuple-element.39.refs_2_), channel_id=1, source_target_pairs={{0,8},{1,17},{2,10},{3,19},{4,12},{5,21},{6,14},{7,23},{8,24},{9,1... | collective-permute-start | bytes 983048 | tf_op jit(solution)/shard_map/ppermute | solution.py:436
  27.6 1.6 %rest_parts.1 = (f32[3072,128]{1,0:T(8,128)S(1)}, f32[1024,128]{1,0:T(8,128)S(1)}, f32[1280,128]{1,0:T(8,128)S(1)}) custom-call(f32[2,1280,128]{2,1,0:T(8,128)S(1)} %get-tuple-element.27.refs_0_, f32[2,2816,128]{2,1,0:T(8,128)S(1)} %get-tuple-element.28.high_ref.refs_1_, f32[256,128]{1,0:T(8,128)S(1)} %get-tuple-element.32.first_ref.refs_2_, ...), custom_call_target="tpu_custom_call" | custom-call | tf_op jit(solution)/shard_map/rest_parts/pallas_call | solution.py:119
  29.2 13.6 %collective-permute-done.6.refs_1_.refs_3_ = f32[2560,128]{1,0:T(8,128)S(1)} collective-permute-done((f32[2560,128]{1,0:T(8,128)S(1)}, f32[2560,128]{1,0:T(8,128)S(1)}, u32[]{:S(2)}, u32[]{:S(2)}) %collective-permute-start.6) | collective-permute-done | bytes 1310752 | tf_op jit(solution)/shard_map/ppermute | solution.py:436
  42.8 1.8 %main_cross.1 = (f32[1280,128]{1,0:T(8,128)S(1)}, f32[128,128]{1,0:T(8,128)S(1)}) custom-call(f32[2,1280,128]{2,1,0:T(8,128)S(1)} %collective-permute-done.5.refs_0_, f32[2560,128]{1,0:T(8,128)S(1)} %collective-permute-done.6.refs_1_.refs_3_, f32[3072,128]{1,0:T(8,128)S(1)} %get-tuple-element.47.refs_2_.bulk_ref.refs_0_, ...), custom_call_target="tpu_custom_call" | custom-call | tf_op jit(solution)/shard_map/main_cross/pallas_call | solution.py:119
  44.6 0.9 %collective-permute-start.16 = (f32[3072,128]{1,0:T(8,128)S(1)}, f32[3072,128]{1,0:T(8,128)S(1)}, u32[]{:S(2)}, u32[]{:S(2)}) collective-permute-start(f32[3072,128]{1,0:T(8,128)S(1)} %get-tuple-element.47.refs_2_.bulk_ref.refs_0_), channel_id=1, source_target_pairs={{0,16},{1,9},{2,18},{3,11},{4,20},{5,13},{6,22},{7,15},{8,0},{9,25... | collective-permute-start | bytes 4718600 | tf_op jit(solution)/shard_map/ppermute | solution.py:436
  45.6 0.8 %collective-permute-done.8.far_ref.refs_4_ = f32[640,128]{1,0:T(8,128)S(1)} collective-permute-done((f32[640,128]{1,0:T(8,128)S(1)}, f32[640,128]{1,0:T(8,128)S(1)}, u32[]{:S(2)}, u32[]{:S(2)}) %collective-permute-start.8) | collective-permute-done | bytes 327712 | tf_op jit(solution)/shard_map/ppermute | solution.py:436
  46.3 0.3 last_cross.1
  46.7 3.5 %collective-permute-start.11 = (f32[128,128]{1,0:T(8,128)S(1)}, f32[128,128]{1,0:T(8,128)S(1)}, u32[]{:S(2)}, u32[]{:S(2)}) collective-permute-start(f32[128,128]{1,0:T(8,128)S(1)} %last_cross.1), channel_id=1, source_target_pairs={{0,5},{1,4},{2,7},{3,6},{4,1},{5,0},{6,3},{7,2},{8,13},{9,12},{10,... | collective-permute-start | bytes 196616 | tf_op jit(solution)/shard_map/ppermute | solution.py:443
  50.2 0.6 collective-permute-start.9
  50.9 1.9 %collective-permute-done.11 = f32[128,128]{1,0:T(8,128)S(1)} collective-permute-done((f32[128,128]{1,0:T(8,128)S(1)}, f32[128,128]{1,0:T(8,128)S(1)}, u32[]{:S(2)}, u32[]{:S(2)}) %collective-permute-start.11) | collective-permute-done | bytes 65568 | tf_op jit(solution)/shard_map/ppermute | solution.py:443
  52.7 3.0 %collective-permute-done.12 = f32[128,128]{1,0:T(8,128)S(1)} collective-permute-done((f32[128,128]{1,0:T(8,128)S(1)}, f32[128,128]{1,0:T(8,128)S(1)}, u32[]{:S(2)}, u32[]{:S(2)}) %collective-permute-start.12) | collective-permute-done | bytes 65568 | tf_op jit(solution)/shard_map/ppermute | solution.py:443
  55.8 0.2 collective-permute-start.13
  55.9 1.4 %collective-permute-start.14 = (f32[128,128]{1,0:T(8,128)S(1)}, f32[128,128]{1,0:T(8,128)S(1)}, u32[]{:S(2)}, u32[]{:S(2)}) collective-permute-start(f32[128,128]{1,0:T(8,128)S(1)} %add_add_fusion.1), channel_id=1, source_target_pairs={{0,8},{1,17},{2,10},{3,19},{4,12},{5,21},{6,14},{7,23},{8,24},{9,1... | collective-permute-start | bytes 196616 | tf_op jit(solution)/shard_map/ppermute | solution.py:436
  57.4 0.9 %collective-permute-start.7 = (f32[1024,128]{1,0:T(8,128)S(1)}, f32[1024,128]{1,0:T(8,128)S(1)}, u32[]{:S(2)}, u32[]{:S(2)}) collective-permute-start(f32[1024,128]{1,0:T(8,128)S(1)} %get-tuple-element.44.refs_3_.tail_ref.refs_1_), channel_id=1, source_target_pairs={{0,16},{1,9},{2,18},{3,11},{4,20},{5,13},{6,22},{7,15},{8,0},{9,25... | collective-permute-start | bytes 1572872 | tf_op jit(solution)/shard_map/ppermute | solution.py:436
  58.3 2.8 %collective-permute-done.14.there_ref = f32[128,128]{1,0:T(8,128)S(1)} collective-permute-done((f32[128,128]{1,0:T(8,128)S(1)}, f32[128,128]{1,0:T(8,128)S(1)}, u32[]{:S(2)}, u32[]{:S(2)}) %collective-permute-start.14) | collective-permute-done | bytes 65568 | tf_op jit(solution)/shard_map/ppermute | solution.py:436
  61.0 3.6 %second_rotation.1.refs_5_ = f32[256,128]{1,0:T(8,128)S(1)} custom-call(f32[128,128]{1,0:T(8,128)S(1)} %get-tuple-element.45.own_gram_ref, f32[640,128]{1,0:T(8,128)S(1)} %collective-permute-done.8.far_ref.refs_4_, f32[128,128]{1,0:T(8,128)S(1)} %collective-permute-done.13.here_ref, f32[128,128]{1,0:T(8,128)S(1)} %collective-permute-done.14.there_ref), custom_call_target="tpu_custom_call" | custom-call | flops 11500000256 | tf_op jit(solution)/shard_map/second_rotation/pallas_call | solution.py:119
  64.7 2.1 %here_product.1.refs_5_ = f32[2,4096,128]{2,1,0:T(8,128)} custom-call(f32[3072,128]{1,0:T(8,128)S(1)} %get-tuple-element.47.refs_2_.bulk_ref.refs_0_, f32[1024,128]{1,0:T(8,128)S(1)} %get-tuple-element.44.refs_3_.tail_ref.refs_1_, f32[1280,128]{1,0:T(8,128)S(1)} %get-tuple-element.48.refs_2_, f32[2560,128]{1,0:T(8,128)S(1)} %collective-permute-done.6.refs_1_.refs_3_, ...), custom_call_target="tpu_custom_call" | custom-call | tf_op jit(solution)/shard_map/here_product/pallas_call | solution.py:119
  66.8 1.7 %bulk_product.1.refs_5_ = f32[2,4096,128]{2,1,0:T(8,128)} custom-call(f32[1280,128]{1,0:T(8,128)S(1)} %get-tuple-element.37.refs_0_, f32[2560,128]{1,0:T(8,128)S(1)} %get-tuple-element.38.refs_1_, f32[640,128]{1,0:T(8,128)S(1)} %get-tuple-element.39.refs_2_, f32[3072,128]{1,0:T(8,128)S(1)} %collective-permute-done.16.refs_3_, ...), custom_call_target="tpu_custom_call", output_to_operand_aliasing={{}: (5, {})} | custom-call | tf_op jit(solution)/shard_map/bulk_product/pallas_call | solution.py:119
  68.6 2.8 %collective-permute-done.7.refs_3_ = f32[1024,128]{1,0:T(8,128)S(1)} collective-permute-done((f32[1024,128]{1,0:T(8,128)S(1)}, f32[1024,128]{1,0:T(8,128)S(1)}, u32[]{:S(2)}, u32[]{:S(2)}) %collective-permute-start.7) | collective-permute-done | bytes 524320 | tf_op jit(solution)/shard_map/ppermute | solution.py:436
  71.4 1.2 %tail_product.1 = f32[2,4096,128]{2,1,0:T(8,128)} custom-call(f32[1280,128]{1,0:T(8,128)S(1)} %get-tuple-element.37.refs_0_, f32[2560,128]{1,0:T(8,128)S(1)} %get-tuple-element.38.refs_1_, f32[640,128]{1,0:T(8,128)S(1)} %get-tuple-element.39.refs_2_, f32[1024,128]{1,0:T(8,128)S(1)} %collective-permute-done.7.refs_3_, ...), custom_call_target="tpu_custom_call", output_to_operand_aliasing={{}: (5, {})} | custom-call | tf_op jit(solution)/shard_map/tail_product/pallas_call | solution.py:119
  (15 shorter events, 0.4 us)
Async XLA Ops:
  4.0 19.7 %collective-permute-start.5 = (f32[2,1280,128]{2,1,0:T(8,128)S(1)}, f32[2,1280,128]{2,1,0:T(8,128)S(1)}, u32[]{:S(2)}, u32[]{:S(2)}) collective-permute-start(f32[2,1280,128]{2,1,0:T(8,128)S(1)} %get-tuple-element.27.refs_0_), channel_id=1, source_target_pairs={{0,8},{1,17},{2,10},{3,19},{4,12},{5,21},{6,14},{7,23},{8,24},{9,1... | collective-permute-start | bytes 3932168 | tf_op jit(solution)/shard_map/ppermute | solution.py:436
  7.0 1.3 %collective-permute-start = (f32[136,128]{1,0:T(8,128)S(1)}, f32[136,128]{1,0:T(8,128)S(1)}, u32[]{:S(2)}, u32[]{:S(2)}) collective-permute-start(f32[136,128]{1,0:T(8,128)S(1)} %get-tuple-element.30), channel_id=1, source_target_pairs={{0,1},{1,0},{2,3},{3,2},{4,5},{5,4},{6,7},{7,6},{8,9},{9,8},{10,11... | collective-permute-start | bytes 208904 | tf_op jit(solution)/shard_map/ppermute | solution.py:457
  8.2 4.5 %collective-permute-start.1 = (f32[136,128]{1,0:T(8,128)S(1)}, f32[136,128]{1,0:T(8,128)S(1)}, u32[]{:S(2)}, u32[]{:S(2)}) collective-permute-start(f32[136,128]{1,0:T(8,128)S(1)} %add.21), channel_id=1, source_target_pairs={{0,2},{1,3},{2,0},{3,1},{4,6},{5,7},{6,4},{7,5},{8,10},{9,11},{10,... | collective-permute-start | bytes 208904 | tf_op jit(solution)/shard_map/ppermute | solution.py:443
  9.9 7.8 %collective-permute-start.2 = (f32[136,128]{1,0:T(8,128)S(1)}, f32[136,128]{1,0:T(8,128)S(1)}, u32[]{:S(2)}, u32[]{:S(2)}) collective-permute-start(f32[136,128]{1,0:T(8,128)S(1)} %add.21), channel_id=1, source_target_pairs={{0,4},{1,5},{2,6},{3,7},{4,0},{5,1},{6,2},{7,3},{8,12},{9,13},{10,... | collective-permute-start | bytes 208904 | tf_op jit(solution)/shard_map/ppermute | solution.py:443
  12.5 6.2 %collective-permute-start.3 = (f32[136,128]{1,0:T(8,128)S(1)}, f32[136,128]{1,0:T(8,128)S(1)}, u32[]{:S(2)}, u32[]{:S(2)}) collective-permute-start(f32[136,128]{1,0:T(8,128)S(1)} %add.21), channel_id=1, source_target_pairs={{0,6},{1,7},{2,4},{3,5},{4,2},{5,3},{6,0},{7,1},{8,14},{9,15},{10,... | collective-permute-start | bytes 208904 | tf_op jit(solution)/shard_map/ppermute | solution.py:443
  18.7 1.3 %collective-permute-start.4 = (f32[136,128]{1,0:T(8,128)S(1)}, f32[136,128]{1,0:T(8,128)S(1)}, u32[]{:S(2)}, u32[]{:S(2)}) collective-permute-start(f32[136,128]{1,0:T(8,128)S(1)} %add_add_fusion.mine_ref), channel_id=1, source_target_pairs={{0,1},{1,0},{2,3},{3,2},{4,5},{5,4},{6,7},{7,6},{8,9},{9,8},{10,11... | collective-permute-start | bytes 208904 | tf_op jit(solution)/shard_map/ppermute | solution.py:458
  25.1 17.7 %collective-permute-start.6 = (f32[2560,128]{1,0:T(8,128)S(1)}, f32[2560,128]{1,0:T(8,128)S(1)}, u32[]{:S(2)}, u32[]{:S(2)}) collective-permute-start(f32[2560,128]{1,0:T(8,128)S(1)} %get-tuple-element.38.refs_1_), channel_id=1, source_target_pairs={{0,8},{1,17},{2,10},{3,19},{4,12},{5,21},{6,14},{7,23},{8,24},{9,1... | collective-permute-start | bytes 3932168 | tf_op jit(solution)/shard_map/ppermute | solution.py:436
  26.7 19.6 %collective-permute-start.8 = (f32[640,128]{1,0:T(8,128)S(1)}, f32[640,128]{1,0:T(8,128)S(1)}, u32[]{:S(2)}, u32[]{:S(2)}) collective-permute-start(f32[640,128]{1,0:T(8,128)S(1)} %get-tuple-element.39.refs_2_), channel_id=1, source_target_pairs={{0,8},{1,17},{2,10},{3,19},{4,12},{5,21},{6,14},{7,23},{8,24},{9,1... | collective-permute-start | bytes 983048 | tf_op jit(solution)/shard_map/ppermute | solution.py:436
  44.6 22.2 %collective-permute-start.16 = (f32[3072,128]{1,0:T(8,128)S(1)}, f32[3072,128]{1,0:T(8,128)S(1)}, u32[]{:S(2)}, u32[]{:S(2)}) collective-permute-start(f32[3072,128]{1,0:T(8,128)S(1)} %get-tuple-element.47.refs_2_.bulk_ref.refs_0_), channel_id=1, source_target_pairs={{0,16},{1,9},{2,18},{3,11},{4,20},{5,13},{6,22},{7,15},{8,0},{9,25... | collective-permute-start | bytes 4718600 | tf_op jit(solution)/shard_map/ppermute | solution.py:436
  46.6 4.3 %collective-permute-start.10 = (f32[128,128]{1,0:T(8,128)S(1)}, f32[128,128]{1,0:T(8,128)S(1)}, u32[]{:S(2)}, u32[]{:S(2)}) collective-permute-start(f32[128,128]{1,0:T(8,128)S(1)} %last_cross.1), channel_id=1, source_target_pairs={{0,3},{1,2},{2,1},{3,0},{4,7},{5,6},{6,5},{7,4},{8,11},{9,10},{10,... | collective-permute-start | bytes 196616 | tf_op jit(solution)/shard_map/ppermute | solution.py:443
  46.7 6.0 %collective-permute-start.11 = (f32[128,128]{1,0:T(8,128)S(1)}, f32[128,128]{1,0:T(8,128)S(1)}, u32[]{:S(2)}, u32[]{:S(2)}) collective-permute-start(f32[128,128]{1,0:T(8,128)S(1)} %last_cross.1), channel_id=1, source_target_pairs={{0,5},{1,4},{2,7},{3,6},{4,1},{5,0},{6,3},{7,2},{8,13},{9,12},{10,... | collective-permute-start | bytes 196616 | tf_op jit(solution)/shard_map/ppermute | solution.py:443
  50.2 5.5 %collective-permute-start.12 = (f32[128,128]{1,0:T(8,128)S(1)}, f32[128,128]{1,0:T(8,128)S(1)}, u32[]{:S(2)}, u32[]{:S(2)}) collective-permute-start(f32[128,128]{1,0:T(8,128)S(1)} %last_cross.1), channel_id=1, source_target_pairs={{0,7},{1,6},{2,5},{3,4},{4,3},{5,2},{6,1},{7,0},{8,15},{9,14},{10,... | collective-permute-start | bytes 196616 | tf_op jit(solution)/shard_map/ppermute | solution.py:443
  50.2 5.5 %collective-permute-start.9 = (f32[128,128]{1,0:T(8,128)S(1)}, f32[128,128]{1,0:T(8,128)S(1)}, u32[]{:S(2)}, u32[]{:S(2)}) collective-permute-start(f32[128,128]{1,0:T(8,128)S(1)} %last_cross.1), channel_id=1, source_target_pairs={{0,1},{1,0},{2,3},{3,2},{4,5},{5,4},{6,7},{7,6},{8,9},{9,8},{10,11... | collective-permute-start | bytes 196616 | tf_op jit(solution)/shard_map/ppermute | solution.py:443
  55.8 2.5 %collective-permute-start.13 = (f32[128,128]{1,0:T(8,128)S(1)}, f32[128,128]{1,0:T(8,128)S(1)}, u32[]{:S(2)}, u32[]{:S(2)}) collective-permute-start(f32[128,128]{1,0:T(8,128)S(1)} %add_add_fusion.1), channel_id=1, source_target_pairs={{0,1},{1,0},{2,3},{3,2},{4,5},{5,4},{6,7},{7,6},{8,9},{9,8},{10,11... | collective-permute-start | bytes 196616 | tf_op jit(solution)/shard_map/ppermute | solution.py:474
  55.9 5.1 %collective-permute-start.14 = (f32[128,128]{1,0:T(8,128)S(1)}, f32[128,128]{1,0:T(8,128)S(1)}, u32[]{:S(2)}, u32[]{:S(2)}) collective-permute-start(f32[128,128]{1,0:T(8,128)S(1)} %add_add_fusion.1), channel_id=1, source_target_pairs={{0,8},{1,17},{2,10},{3,19},{4,12},{5,21},{6,14},{7,23},{8,24},{9,1... | collective-permute-start | bytes 196616 | tf_op jit(solution)/shard_map/ppermute | solution.py:436
  57.4 14.0 %collective-permute-start.7 = (f32[1024,128]{1,0:T(8,128)S(1)}, f32[1024,128]{1,0:T(8,128)S(1)}, u32[]{:S(2)}, u32[]{:S(2)}) collective-permute-start(f32[1024,128]{1,0:T(8,128)S(1)} %get-tuple-element.44.refs_3_.tail_ref.refs_1_), channel_id=1, source_target_pairs={{0,16},{1,9},{2,18},{3,11},{4,20},{5,13},{6,22},{7,15},{8,0},{9,25... | collective-permute-start | bytes 1572872 | tf_op jit(solution)/shard_map/ppermute | solution.py:436
  64.7 2.1 %collective-permute-start.15 = (f32[256,128]{1,0:T(8,128)S(1)}, f32[256,128]{1,0:T(8,128)S(1)}, u32[]{:S(2)}, u32[]{:S(2)}) collective-permute-start(f32[256,128]{1,0:T(8,128)S(1)} %second_rotation.1.refs_5_), channel_id=1, source_target_pairs={{0,1},{1,0},{2,3},{3,2},{4,5},{5,4},{6,7},{7,6},{8,9},{9,8},{10,11... | collective-permute-start | bytes 393224 | tf_op jit(solution)/shard_map/ppermute | solution.py:476

commit v3 on v2

--- a/solution.py
+++ b/solution.py
@@ -13,9 +13,10 @@
 SCOPED = 16 * 1024 * 1024
 WHOLE = 54 * 1024 * 1024
 
-RAW = (5,)
+RAW = 6
+SMALL = 4
 LAST = 2
-BULK = 12
+BULK = 14
 STEP = 2
 
 
@@ -235,16 +236,30 @@
     return call(kernel, [half, half, ((2 * width, 2 * width), HERE)], [(mine, HERE), (other, HERE)], "first_rotation")
 
 
-def sent_parts(high, first, second, gram, early, last, step):
+def small_part(high, turn, small, step):
+    width = turn.shape[1]
+
+    def kernel(high_ref, turn_ref, out_ref):
+        local = Rows((high_ref, 0, high.shape[1], 0))
+        out_ref[: 2 * width] = turn_ref[...]
+        parts = right_parts(turn_ref[...])
+        for start, number in spans(0, small, step):
+            out_ref[pl.ds(2 * width + start, number), :] = rows_product(local.pair(start, number), parts)
+
+    return call(
+        kernel, [((2 * width + small, width), HERE)], [(high, HERE), (turn, HERE)], "small_part", 12 * small * width * width
+    )[0]
+
+
+def sent_parts(high, first, second, gram, small, last, step):
     width = first.shape[1]
     count = high.shape[1]
 
     def kernel(high_ref, first_ref, second_ref, gram_ref, main_ref, last_ref, second_gram_ref):
         local = Rows((high_ref, 0, count, 0))
-        out = Rows((main_ref, 0, count - last, 2 * width), (last_ref, count - last, last, 0))
-        main_ref[: 2 * width] = first_ref[...]
+        out = Rows((main_ref, small, count - small - last, 0), (last_ref, count - last, last, 0))
         parts = right_parts(first_ref[...])
-        for start, number in spans(0, count, step, count - last):
+        for start, number in spans(small, count, step, count - last):
             ref, place = out.at(start, number)
             ref[place, :] = rows_product(local.pair(start, number), parts)
         gram = gram_ref[...]
@@ -254,7 +269,7 @@
 
     return call(
         kernel,
-        [((2 * width + count - last, width), HERE), ((last + width, width), HERE), ((width, width), HERE)],
+        [((count - small - last, width), HERE), ((last + width, width), HERE), ((width, width), HERE)],
         [(high, HERE), (first, HERE), (second, HERE), (gram, HERE)],
         "sent_parts",
         12 * count * width * width,
@@ -296,19 +311,17 @@
     return (total[:width, :width] + total[:width, width:]) + (total[width:, :width] + total[width:, width:])
 
 
-def main_cross(far_raw, far_main, bulk, tail, step):
+def raw_cross(far_raw, far_small, bulk, tail, step):
     width = bulk.shape[1]
-    sizes = [part.shape[1] for part in far_raw]
-    early, main = sum(sizes), far_main.shape[0] - 2 * width
-
-    def kernel(*refs):
-        raw_refs, (main_ref, bulk_ref, tail_ref, far_ref, out_ref) = refs[: len(sizes)], refs[len(sizes) :]
+    early, small = far_raw.shape[1], far_small.shape[0] - 2 * width
+
+    def kernel(raw_ref, small_ref, bulk_ref, tail_ref, far_ref, out_ref):
         own = Rows.of((bulk_ref, tail_ref), (bulk.shape[0], tail.shape[0]))
-        raw = Rows.of(raw_refs, sizes)
-        far = Rows((main_ref, early, main, 2 * width))
-        parts = right_parts(main_ref[: 2 * width])
+        raw = Rows((raw_ref, 0, early, 0))
+        far = Rows((small_ref, early, small, 2 * width))
+        parts = right_parts(small_ref[: 2 * width])
         total = jnp.zeros((2 * width, 2 * width), F32)
-        for start, count in spans(0, early + main, step, early, bulk.shape[0]):
+        for start, count in spans(0, early + small, step, early, bulk.shape[0]):
             if start < early:
                 block = rows_product(raw.pair(start, count), parts)
                 far_ref[pl.ds(start, count), :] = block
@@ -320,30 +333,28 @@
     return call(
         kernel,
         [((early, width), HERE), ((width, width), HERE)],
-        [(part, HERE) for part in far_raw] + [(far_main, HERE), (bulk, HERE), (tail, HERE)],
-        "main_cross",
-        12 * (early + main) * width * width,
-    )
-
-
-def last_cross(far_last, bulk, tail, so_far, step):
+        [(far_raw, HERE), (far_small, HERE), (bulk, HERE), (tail, HERE)],
+        "raw_cross",
+        12 * (early + small) * width * width,
+    )
+
+
+def more_cross(far, first_row, count, bulk, tail, so_far, step, name):
     width = bulk.shape[1]
-    count = far_last.shape[0] - width
-    rows = bulk.shape[0] + tail.shape[0]
 
     def kernel(far_ref, bulk_ref, tail_ref, total_ref, out_ref):
-        own = Rows((bulk_ref, 0, bulk.shape[0], 0), (tail_ref, bulk.shape[0], tail.shape[0], 0))
-        far = Rows((far_ref, rows - count, count, 0))
+        own = Rows.of((bulk_ref, tail_ref), (bulk.shape[0], tail.shape[0]))
+        part = Rows((far_ref, first_row, count, 0))
         total = jnp.zeros((2 * width, 2 * width), F32)
-        for start, number in spans(rows - count, rows, step, bulk.shape[0]):
-            total = total + cross_term(own.get(start, number), far.get(start, number))
+        for start, number in spans(first_row, first_row + count, step, bulk.shape[0]):
+            total = total + cross_term(own.get(start, number), part.get(start, number))
         out_ref[...] = total_ref[...] + cross_sum(total)
 
     return call(
         kernel,
         [((width, width), HERE)],
-        [(far_last, HERE), (bulk, HERE), (tail, HERE), (so_far, HERE)],
-        "last_cross",
+        [(far, HERE), (bulk, HERE), (tail, HERE), (so_far, HERE)],
+        name,
         6 * count * width * width,
     )[0]
 
@@ -417,9 +428,8 @@
 def body(pairs_count, rows_count, matrix):
     rows, width = matrix.shape[1:]
     unit = rows // 16
-    last, bulk, step = LAST * unit, BULK * unit, STEP * unit
-    raw_sizes = [part * unit for part in RAW if part]
-    early = sum(raw_sizes)
+    early, small, last, bulk, step = (part * unit for part in (RAW, SMALL, LAST, BULK, STEP))
+    main = rows - early - small - last
     flat = [(p, r) for p in range(pairs_count) for r in range(rows_count)]
     ahead = {p: after(p, pairs_count) for p in range(pairs_count)}
     behind = {q: p for p, q in ahead.items()}
@@ -451,23 +461,26 @@
     def other_sum(block):
         return chip_sum(block, 1)
 
-    *local, keep, give = local_gram(matrix, raw_sizes + [rows - early], step)
-    high = local[-1]
-    far_raw = [travel(part, outward) for part in local[:-1]]
+    low, high, keep, give = local_gram(matrix, [early, rows - early], step)
+    far_raw = travel(low, outward)
     mine = chip_sum(keep + lax.ppermute(give, "row", core))
     other = lax.ppermute(mine, "row", core)
     turn_first, turn_second, gram = first_rotation(mine, other)
-    turn_first, *far_raw = lax.optimization_barrier((turn_first, *far_raw))
-
-    sent_main, sent_last, second_gram = sent_parts(high, turn_first, turn_second, gram, early, last, step)
+
+    sent_small = small_part(high, turn_first, small, step)
+    far_small = travel(sent_small, outward)
+    turn_main, sent_small, far_raw = lax.optimization_barrier((turn_first, sent_small, far_raw))
+    sent_main, sent_last, second_gram = sent_parts(high, turn_main, turn_second, gram, small, last, step)
     far_main, far_last = travel(sent_main, outward), travel(sent_last, outward)
     turn_second, sent_main = lax.optimization_barrier((turn_second, sent_main))
-    second_bulk, second_tail, first_raw = rest_parts(local, turn_first, turn_second, bulk, early, step)
-
-    far_rotated, cross = main_cross(far_raw, far_main, second_bulk, second_tail, step)
+    second_bulk, second_tail, first_raw = rest_parts([low, high], turn_first, turn_second, bulk, early, step)
+
+    far_rotated, cross = raw_cross(far_raw, far_small, second_bulk, second_tail, step)
+    far_main, cross = lax.optimization_barrier((far_main, cross))
+    cross = more_cross(far_main, early + small, main, second_bulk, second_tail, cross, step, "main_cross")
     cross, later_bulk, later_tail = lax.optimization_barrier((cross, second_bulk, second_tail))
     far_bulk, far_tail = travel(later_bulk, inward), travel(later_tail, inward)
-    cross = last_cross(far_last, second_bulk, second_tail, cross, step)
+    cross = more_cross(far_last, rows - last, last, second_bulk, second_tail, cross, step, "last_cross")
 
     total = other_sum(cross)
     there = travel(total, outward)
@@ -475,9 +488,9 @@
     turn_here = second_rotation(second_gram, far_last, here, there)
     turn_there = lax.ppermute(turn_here, "row", core)
 
-    main = rows - early - last
-    first = [(first_raw, 0, early, 0), (sent_main, early, main, 2 * width), (sent_last, early + main, last, 0)]
-    far_first = [(far_rotated, 0, early, 0), (far_main, early, main, 2 * width), (far_last, early + main, last, 0)]
+    parts = (0, early, 0), (early, small, 2 * width), (early + small, main, 0), (rows - last, last, 0)
+    first = [(array, *where) for array, where in zip((first_raw, sent_small, sent_main, sent_last), parts)]
+    far_first = [(array, *where) for array, where in zip((far_rotated, far_small, far_main, far_last), parts)]
     second = [(second_bulk, 0, bulk, 0), (second_tail, bulk, rows - bulk, 0)]
     done = last_product(second, far_first, turn_here, None, first_slot, 0, rows, rows, step, "here_product")
 

time: 72.9 us -> 68.9 us (0.945)
  waiting for transfers between devices: 33.3 us -> 27.3 us
  starting transfers between devices: 17.7 us -> 19.8 us
    ppermute x6 -> x7, waiting for transfers between devices: 20 us -> 13.9 us  [travel(): return lax.ppermute(block, ('pair', 'row'), moves)]
    ppermute x6 -> x7, starting transfers between devices: 8.66 us -> 10.5 us  [travel(): return lax.ppermute(block, ('pair', 'row'), moves)]
    pallas_call x10 -> x12, Pallas kernels: 21.3 us -> 21.2 us  [call(): pl.pallas_call(kernel, in_specs=[pl.BlockSpec(memory_space=place) for pla...]
  transfers between devices with their start and end apart: 17 -> 18, of which waited for: 10 -> 9; matrix products, arithmetic and copies ran while one was open for 0% -> 0% of each run, Pallas kernels for 20% -> 24%
where the time goes in v3:
time: 68.9 us; the launch traced here: 68.7 us
  waiting for transfers between devices  27.3 us (40%)
  Pallas kernels  21.2 us (31%)
  starting transfers between devices  19.8 us (29%)
    pallas_call x12, Pallas kernels, call(): pl.pallas_call(kernel, in_specs=[pl.BlockSpec(memory_space=place) for pla...  21.2 us
    ppermute x7, waiting for transfers between devices, travel(): return lax.ppermute(block, ('pair', 'row'), moves)  13.9 us
    ppermute x7, waiting for transfers between devices, chip_sum(): lax.ppermute(block, 'row', [(r, r ^ d) for r in range(rows_count)])  10.9 us
    ppermute x7, starting transfers between devices, travel(): return lax.ppermute(block, ('pair', 'row'), moves)  10.5 us
    ppermute x7, starting transfers between devices, chip_sum(): lax.ppermute(block, 'row', [(r, r ^ d) for r in range(rows_count)])  8.75 us
  transfers between devices with their start and end apart: 18, of which 9 were waited for; matrix products, arithmetic and copies ran while one was open for 0% of the time, Pallas kernels for 24%

profile of v3, /device:TPU:0, one launch (start us, length us, event | category | flops | bytes accessed | tf_op | source)
XLA Modules:
  0.0 68.7 jit_solution(16796927864872908167)
XLA Ops:
  0.0 3.8 %gram.1 = (f32[2,1536,128]{2,1,0:T(8,128)S(1)}, f32[2,2560,128]{2,1,0:T(8,128)S(1)}, f32[136,128]{1,0:T(8,128)S(1)}, f32[136,128]{1,0:T(8,128)S(1)}) custom-call(f32[2,4096,128]{2,1,0:T(8,128)} %matrix_ref.1), custom_call_target="tpu_custom_call" | custom-call | tf_op jit(solution)/shard_map/gram/pallas_call | solution.py:120
  3.8 3.0 %collective-permute-start.5 = (f32[2,1536,128]{2,1,0:T(8,128)S(1)}, f32[2,1536,128]{2,1,0:T(8,128)S(1)}, u32[]{:S(2)}, u32[]{:S(2)}) collective-permute-start(f32[2,1536,128]{2,1,0:T(8,128)S(1)} %get-tuple-element.30.refs_0_), channel_id=1, source_target_pairs={{0,8},{1,17},{2,10},{3,19},{4,12},{5,21},{6,14},{7,23},{8,24},{9,1... | collective-permute-start | bytes 4718600 | tf_op jit(solution)/shard_map/ppermute | solution.py:446
  6.8 1.3 %collective-permute-done = f32[136,128]{1,0:T(8,128)S(1)} collective-permute-done((f32[136,128]{1,0:T(8,128)S(1)}, f32[136,128]{1,0:T(8,128)S(1)}, u32[]{:S(2)}, u32[]{:S(2)}) %collective-permute-start) | collective-permute-done | bytes 69664 | tf_op jit(solution)/shard_map/ppermute | solution.py:466
  8.0 1.6 %collective-permute-start.1 = (f32[136,128]{1,0:T(8,128)S(1)}, f32[136,128]{1,0:T(8,128)S(1)}, u32[]{:S(2)}, u32[]{:S(2)}) collective-permute-start(f32[136,128]{1,0:T(8,128)S(1)} %add.21), channel_id=1, source_target_pairs={{0,2},{1,3},{2,0},{3,1},{4,6},{5,7},{6,4},{7,5},{8,10},{9,11},{10,... | collective-permute-start | bytes 208904 | tf_op jit(solution)/shard_map/ppermute | solution.py:453
  9.7 2.6 %collective-permute-start.2 = (f32[136,128]{1,0:T(8,128)S(1)}, f32[136,128]{1,0:T(8,128)S(1)}, u32[]{:S(2)}, u32[]{:S(2)}) collective-permute-start(f32[136,128]{1,0:T(8,128)S(1)} %add.21), channel_id=1, source_target_pairs={{0,4},{1,5},{2,6},{3,7},{4,0},{5,1},{6,2},{7,3},{8,12},{9,13},{10,... | collective-permute-start | bytes 208904 | tf_op jit(solution)/shard_map/ppermute | solution.py:453
  12.5 5.0 %collective-permute-done.2 = f32[136,128]{1,0:T(8,128)S(1)} collective-permute-done((f32[136,128]{1,0:T(8,128)S(1)}, f32[136,128]{1,0:T(8,128)S(1)}, u32[]{:S(2)}, u32[]{:S(2)}) %collective-permute-start.2) | collective-permute-done | bytes 69664 | tf_op jit(solution)/shard_map/ppermute | solution.py:453
  17.5 1.0 %collective-permute-done.3 = f32[136,128]{1,0:T(8,128)S(1)} collective-permute-done((f32[136,128]{1,0:T(8,128)S(1)}, f32[136,128]{1,0:T(8,128)S(1)}, u32[]{:S(2)}, u32[]{:S(2)}) %collective-permute-start.3) | collective-permute-done | bytes 69664 | tf_op jit(solution)/shard_map/ppermute | solution.py:453
  18.6 1.2 %collective-permute-done.4.other_ref = f32[136,128]{1,0:T(8,128)S(1)} collective-permute-done((f32[136,128]{1,0:T(8,128)S(1)}, f32[136,128]{1,0:T(8,128)S(1)}, u32[]{:S(2)}, u32[]{:S(2)}) %collective-permute-start.4) | collective-permute-done | bytes 69664 | tf_op jit(solution)/shard_map/ppermute | solution.py:467
  19.8 3.7 %first_rotation.1 = (f32[256,128]{1,0:T(8,128)S(1)}, f32[256,128]{1,0:T(8,128)S(1)}, f32[256,256]{1,0:T(8,128)S(1)}) custom-call(f32[136,128]{1,0:T(8,128)S(1)} %add_add_fusion.mine_ref, f32[136,128]{1,0:T(8,128)S(1)} %collective-permute-done.4.other_ref), custom_call_target="tpu_custom_call" | custom-call | tf_op jit(solution)/shard_map/first_rotation/pallas_call | solution.py:120
  23.5 0.5 small_part.1.refs_1_
  24.0 1.6 %collective-permute-start.7 = (f32[1280,128]{1,0:T(8,128)S(1)}, f32[1280,128]{1,0:T(8,128)S(1)}, u32[]{:S(2)}, u32[]{:S(2)}) collective-permute-start(f32[1280,128]{1,0:T(8,128)S(1)} %small_part.1.refs_1_), channel_id=1, source_target_pairs={{0,8},{1,17},{2,10},{3,19},{4,12},{5,21},{6,14},{7,23},{8,24},{9,1... | collective-permute-start | bytes 1966088 | tf_op jit(solution)/shard_map/ppermute | solution.py:446
  25.6 1.1 %sent_parts.1 = (f32[1024,128]{1,0:T(8,128)S(1)}, f32[640,128]{1,0:T(8,128)S(1)}, f32[128,128]{1,0:T(8,128)S(1)}) custom-call(f32[2,2560,128]{2,1,0:T(8,128)S(1)} %get-tuple-element.31.high_ref.refs_1_, f32[256,128]{1,0:T(8,128)S(1)} %get-tuple-element.36.turn_ref.first_ref.refs_2_, f32[256,128]{1,0:T(8,128)S(1)} %get-tuple-element.39.second_ref.refs_3_, ...), custom_call_target="tpu_custom_call" | custom-call | tf_op jit(solution)/shard_map/sent_parts/pallas_call | solution.py:120
  26.6 1.7 %collective-permute-start.6 = (f32[1024,128]{1,0:T(8,128)S(1)}, f32[1024,128]{1,0:T(8,128)S(1)}, u32[]{:S(2)}, u32[]{:S(2)}) collective-permute-start(f32[1024,128]{1,0:T(8,128)S(1)} %get-tuple-element.42.refs_2_), channel_id=1, source_target_pairs={{0,8},{1,17},{2,10},{3,19},{4,12},{5,21},{6,14},{7,23},{8,24},{9,1... | collective-permute-start | bytes 1572872 | tf_op jit(solution)/shard_map/ppermute | solution.py:446
  28.3 1.5 %collective-permute-start.9 = (f32[640,128]{1,0:T(8,128)S(1)}, f32[640,128]{1,0:T(8,128)S(1)}, u32[]{:S(2)}, u32[]{:S(2)}) collective-permute-start(f32[640,128]{1,0:T(8,128)S(1)} %get-tuple-element.43.refs_3_), channel_id=1, source_target_pairs={{0,8},{1,17},{2,10},{3,19},{4,12},{5,21},{6,14},{7,23},{8,24},{9,1... | collective-permute-start | bytes 983048 | tf_op jit(solution)/shard_map/ppermute | solution.py:446
  29.8 1.7 %rest_parts.1 = (f32[3584,128]{1,0:T(8,128)S(1)}, f32[512,128]{1,0:T(8,128)S(1)}, f32[1536,128]{1,0:T(8,128)S(1)}) custom-call(f32[2,1536,128]{2,1,0:T(8,128)S(1)} %get-tuple-element.30.refs_0_, f32[2,2560,128]{2,1,0:T(8,128)S(1)} %get-tuple-element.31.high_ref.refs_1_, f32[256,128]{1,0:T(8,128)S(1)} %get-tuple-element.36.turn_ref.first_ref.refs_2_, ...), custom_call_target="tpu_custom_call" | custom-call | tf_op jit(solution)/shard_map/rest_parts/pallas_call | solution.py:120
  31.5 3.1 %collective-permute-done.7.small_ref.refs_3_ = f32[1280,128]{1,0:T(8,128)S(1)} collective-permute-done((f32[1280,128]{1,0:T(8,128)S(1)}, f32[1280,128]{1,0:T(8,128)S(1)}, u32[]{:S(2)}, u32[]{:S(2)}) %collective-permute-start.7) | collective-permute-done | bytes 655392 | tf_op jit(solution)/shard_map/ppermute | solution.py:446
  34.6 1.4 %raw_cross.1 = (f32[1536,128]{1,0:T(8,128)S(1)}, f32[128,128]{1,0:T(8,128)S(1)}) custom-call(f32[2,1536,128]{2,1,0:T(8,128)S(1)} %collective-permute-done.5.raw_ref, f32[1280,128]{1,0:T(8,128)S(1)} %collective-permute-done.7.small_ref.refs_3_, f32[3584,128]{1,0:T(8,128)S(1)} %get-tuple-element.53.bulk_ref.refs_0_, ...), custom_call_target="tpu_custom_call" | custom-call | tf_op jit(solution)/shard_map/raw_cross/pallas_call | solution.py:120
  36.0 4.2 %collective-permute-done.6.far_ref.refs_4_ = f32[1024,128]{1,0:T(8,128)S(1)} collective-permute-done((f32[1024,128]{1,0:T(8,128)S(1)}, f32[1024,128]{1,0:T(8,128)S(1)}, u32[]{:S(2)}, u32[]{:S(2)}) %collective-permute-start.6) | collective-permute-done | bytes 524320 | tf_op jit(solution)/shard_map/ppermute | solution.py:446
  40.6 0.7 %collective-permute-start.17 = (f32[3584,128]{1,0:T(8,128)S(1)}, f32[3584,128]{1,0:T(8,128)S(1)}, u32[]{:S(2)}, u32[]{:S(2)}) collective-permute-start(f32[3584,128]{1,0:T(8,128)S(1)} %get-tuple-element.53.bulk_ref.refs_0_), channel_id=1, source_target_pairs={{0,16},{1,9},{2,18},{3,11},{4,20},{5,13},{6,22},{7,15},{8,0},{9,25... | collective-permute-start | bytes 5505032 | tf_op jit(solution)/shard_map/ppermute | solution.py:446
  41.3 3.6 %collective-permute-done.9.far_ref.refs_5_ = f32[640,128]{1,0:T(8,128)S(1)} collective-permute-done((f32[640,128]{1,0:T(8,128)S(1)}, f32[640,128]{1,0:T(8,128)S(1)}, u32[]{:S(2)}, u32[]{:S(2)}) %collective-permute-start.9) | collective-permute-done | bytes 327712 | tf_op jit(solution)/shard_map/ppermute | solution.py:446
  45.3 1.3 %collective-permute-start.11 = (f32[128,128]{1,0:T(8,128)S(1)}, f32[128,128]{1,0:T(8,128)S(1)}, u32[]{:S(2)}, u32[]{:S(2)}) collective-permute-start(f32[128,128]{1,0:T(8,128)S(1)} %last_cross.1), channel_id=1, source_target_pairs={{0,3},{1,2},{2,1},{3,0},{4,7},{5,6},{6,5},{7,4},{8,11},{9,10},{10,... | collective-permute-start | bytes 196616 | tf_op jit(solution)/shard_map/ppermute | solution.py:453
  46.5 1.3 %collective-permute-start.12 = (f32[128,128]{1,0:T(8,128)S(1)}, f32[128,128]{1,0:T(8,128)S(1)}, u32[]{:S(2)}, u32[]{:S(2)}) collective-permute-start(f32[128,128]{1,0:T(8,128)S(1)} %last_cross.1), channel_id=1, source_target_pairs={{0,5},{1,4},{2,7},{3,6},{4,1},{5,0},{6,3},{7,2},{8,13},{9,12},{10,... | collective-permute-start | bytes 196616 | tf_op jit(solution)/shard_map/ppermute | solution.py:453
  47.9 1.6 %collective-permute-start.13 = (f32[128,128]{1,0:T(8,128)S(1)}, f32[128,128]{1,0:T(8,128)S(1)}, u32[]{:S(2)}, u32[]{:S(2)}) collective-permute-start(f32[128,128]{1,0:T(8,128)S(1)} %last_cross.1), channel_id=1, source_target_pairs={{0,7},{1,6},{2,5},{3,4},{4,3},{5,2},{6,1},{7,0},{8,15},{9,14},{10,... | collective-permute-start | bytes 196616 | tf_op jit(solution)/shard_map/ppermute | solution.py:453
  49.5 4.9 %collective-permute-done.12 = f32[128,128]{1,0:T(8,128)S(1)} collective-permute-done((f32[128,128]{1,0:T(8,128)S(1)}, f32[128,128]{1,0:T(8,128)S(1)}, u32[]{:S(2)}, u32[]{:S(2)}) %collective-permute-start.12) | collective-permute-done | bytes 65568 | tf_op jit(solution)/shard_map/ppermute | solution.py:453
  54.4 0.4 collective-permute-start.14
  54.8 1.5 %collective-permute-start.15 = (f32[128,128]{1,0:T(8,128)S(1)}, f32[128,128]{1,0:T(8,128)S(1)}, u32[]{:S(2)}, u32[]{:S(2)}) collective-permute-start(f32[128,128]{1,0:T(8,128)S(1)} %add_add_fusion.1), channel_id=1, source_target_pairs={{0,8},{1,17},{2,10},{3,19},{4,12},{5,21},{6,14},{7,23},{8,24},{9,1... | collective-permute-start | bytes 196616 | tf_op jit(solution)/shard_map/ppermute | solution.py:446
  56.3 0.5 collective-permute-start.8
  56.8 3.0 %collective-permute-done.15.there_ref = f32[128,128]{1,0:T(8,128)S(1)} collective-permute-done((f32[128,128]{1,0:T(8,128)S(1)}, f32[128,128]{1,0:T(8,128)S(1)}, u32[]{:S(2)}, u32[]{:S(2)}) %collective-permute-start.15) | collective-permute-done | bytes 65568 | tf_op jit(solution)/shard_map/ppermute | solution.py:446
  59.8 3.6 %second_rotation.1.refs_6_ = f32[256,128]{1,0:T(8,128)S(1)} custom-call(f32[128,128]{1,0:T(8,128)S(1)} %get-tuple-element.51.own_gram_ref, f32[640,128]{1,0:T(8,128)S(1)} %collective-permute-done.9.far_ref.refs_5_, f32[128,128]{1,0:T(8,128)S(1)} %collective-permute-done.14.here_ref, f32[128,128]{1,0:T(8,128)S(1)} %collective-permute-done.15.there_ref), custom_call_target="tpu_custom_call" | custom-call | flops 11500000256 | tf_op jit(solution)/shard_map/second_rotation/pallas_call | solution.py:120
  63.5 2.0 %here_product.1.refs_6_ = f32[2,4096,128]{2,1,0:T(8,128)} custom-call(f32[3584,128]{1,0:T(8,128)S(1)} %get-tuple-element.53.bulk_ref.refs_0_, f32[512,128]{1,0:T(8,128)S(1)} %get-tuple-element.50.tail_ref.refs_1_, f32[1536,128]{1,0:T(8,128)S(1)} %get-tuple-element.54.refs_2_, f32[1280,128]{1,0:T(8,128)S(1)} %collective-permute-done.7.small_ref.refs_3_, ...), custom_call_target="tpu_custom_call" | custom-call | tf_op jit(solution)/shard_map/here_product/pallas_call | solution.py:120
  65.6 1.9 %bulk_product.1.refs_6_ = f32[2,4096,128]{2,1,0:T(8,128)} custom-call(f32[1536,128]{1,0:T(8,128)S(1)} %get-tuple-element.40.refs_0_, f32[1280,128]{1,0:T(8,128)S(1)} %small_part.1.refs_1_, f32[1024,128]{1,0:T(8,128)S(1)} %get-tuple-element.42.refs_2_, f32[640,128]{1,0:T(8,128)S(1)} %get-tuple-element.43.refs_3_, ...), custom_call_target="tpu_custom_call", output_to_operand_aliasing={{}: (6, {})} | custom-call | tf_op jit(solution)/shard_map/bulk_product/pallas_call | solution.py:120
  67.5 1.0 %tail_product.1 = f32[2,4096,128]{2,1,0:T(8,128)} custom-call(f32[1536,128]{1,0:T(8,128)S(1)} %get-tuple-element.40.refs_0_, f32[1280,128]{1,0:T(8,128)S(1)} %small_part.1.refs_1_, f32[1024,128]{1,0:T(8,128)S(1)} %get-tuple-element.42.refs_2_, f32[640,128]{1,0:T(8,128)S(1)} %get-tuple-element.43.refs_3_, ...), custom_call_target="tpu_custom_call", output_to_operand_aliasing={{}: (6, {})} | custom-call | tf_op jit(solution)/shard_map/tail_product/pallas_call | solution.py:120
  (19 shorter events, 1.1 us)
Async XLA Ops:
  3.8 21.8 %collective-permute-start.5 = (f32[2,1536,128]{2,1,0:T(8,128)S(1)}, f32[2,1536,128]{2,1,0:T(8,128)S(1)}, u32[]{:S(2)}, u32[]{:S(2)}) collective-permute-start(f32[2,1536,128]{2,1,0:T(8,128)S(1)} %get-tuple-element.30.refs_0_), channel_id=1, source_target_pairs={{0,8},{1,17},{2,10},{3,19},{4,12},{5,21},{6,14},{7,23},{8,24},{9,1... | collective-permute-start | bytes 4718600 | tf_op jit(solution)/shard_map/ppermute | solution.py:446
  6.8 1.3 %collective-permute-start = (f32[136,128]{1,0:T(8,128)S(1)}, f32[136,128]{1,0:T(8,128)S(1)}, u32[]{:S(2)}, u32[]{:S(2)}) collective-permute-start(f32[136,128]{1,0:T(8,128)S(1)} %get-tuple-element.33), channel_id=1, source_target_pairs={{0,1},{1,0},{2,3},{3,2},{4,5},{5,4},{6,7},{7,6},{8,9},{9,8},{10,11... | collective-permute-start | bytes 208904 | tf_op jit(solution)/shard_map/ppermute | solution.py:466
  8.0 4.5 %collective-permute-start.1 = (f32[136,128]{1,0:T(8,128)S(1)}, f32[136,128]{1,0:T(8,128)S(1)}, u32[]{:S(2)}, u32[]{:S(2)}) collective-permute-start(f32[136,128]{1,0:T(8,128)S(1)} %add.21), channel_id=1, source_target_pairs={{0,2},{1,3},{2,0},{3,1},{4,6},{5,7},{6,4},{7,5},{8,10},{9,11},{10,... | collective-permute-start | bytes 208904 | tf_op jit(solution)/shard_map/ppermute | solution.py:453
  9.7 7.8 %collective-permute-start.2 = (f32[136,128]{1,0:T(8,128)S(1)}, f32[136,128]{1,0:T(8,128)S(1)}, u32[]{:S(2)}, u32[]{:S(2)}) collective-permute-start(f32[136,128]{1,0:T(8,128)S(1)} %add.21), channel_id=1, source_target_pairs={{0,4},{1,5},{2,6},{3,7},{4,0},{5,1},{6,2},{7,3},{8,12},{9,13},{10,... | collective-permute-start | bytes 208904 | tf_op jit(solution)/shard_map/ppermute | solution.py:453
  12.3 6.2 %collective-permute-start.3 = (f32[136,128]{1,0:T(8,128)S(1)}, f32[136,128]{1,0:T(8,128)S(1)}, u32[]{:S(2)}, u32[]{:S(2)}) collective-permute-start(f32[136,128]{1,0:T(8,128)S(1)} %add.21), channel_id=1, source_target_pairs={{0,6},{1,7},{2,4},{3,5},{4,2},{5,3},{6,0},{7,1},{8,14},{9,15},{10,... | collective-permute-start | bytes 208904 | tf_op jit(solution)/shard_map/ppermute | solution.py:453
  18.5 1.3 %collective-permute-start.4 = (f32[136,128]{1,0:T(8,128)S(1)}, f32[136,128]{1,0:T(8,128)S(1)}, u32[]{:S(2)}, u32[]{:S(2)}) collective-permute-start(f32[136,128]{1,0:T(8,128)S(1)} %add_add_fusion.mine_ref), channel_id=1, source_target_pairs={{0,1},{1,0},{2,3},{3,2},{4,5},{5,4},{6,7},{7,6},{8,9},{9,8},{10,11... | collective-permute-start | bytes 208904 | tf_op jit(solution)/shard_map/ppermute | solution.py:467
  24.0 10.6 %collective-permute-start.7 = (f32[1280,128]{1,0:T(8,128)S(1)}, f32[1280,128]{1,0:T(8,128)S(1)}, u32[]{:S(2)}, u32[]{:S(2)}) collective-permute-start(f32[1280,128]{1,0:T(8,128)S(1)} %small_part.1.refs_1_), channel_id=1, source_target_pairs={{0,8},{1,17},{2,10},{3,19},{4,12},{5,21},{6,14},{7,23},{8,24},{9,1... | collective-permute-start | bytes 1966088 | tf_op jit(solution)/shard_map/ppermute | solution.py:446
  26.6 13.6 %collective-permute-start.6 = (f32[1024,128]{1,0:T(8,128)S(1)}, f32[1024,128]{1,0:T(8,128)S(1)}, u32[]{:S(2)}, u32[]{:S(2)}) collective-permute-start(f32[1024,128]{1,0:T(8,128)S(1)} %get-tuple-element.42.refs_2_), channel_id=1, source_target_pairs={{0,8},{1,17},{2,10},{3,19},{4,12},{5,21},{6,14},{7,23},{8,24},{9,1... | collective-permute-start | bytes 1572872 | tf_op jit(solution)/shard_map/ppermute | solution.py:446
  28.3 16.6 %collective-permute-start.9 = (f32[640,128]{1,0:T(8,128)S(1)}, f32[640,128]{1,0:T(8,128)S(1)}, u32[]{:S(2)}, u32[]{:S(2)}) collective-permute-start(f32[640,128]{1,0:T(8,128)S(1)} %get-tuple-element.43.refs_3_), channel_id=1, source_target_pairs={{0,8},{1,17},{2,10},{3,19},{4,12},{5,21},{6,14},{7,23},{8,24},{9,1... | collective-permute-start | bytes 983048 | tf_op jit(solution)/shard_map/ppermute | solution.py:446
  40.6 25.0 %collective-permute-start.17 = (f32[3584,128]{1,0:T(8,128)S(1)}, f32[3584,128]{1,0:T(8,128)S(1)}, u32[]{:S(2)}, u32[]{:S(2)}) collective-permute-start(f32[3584,128]{1,0:T(8,128)S(1)} %get-tuple-element.53.bulk_ref.refs_0_), channel_id=1, source_target_pairs={{0,16},{1,9},{2,18},{3,11},{4,20},{5,13},{6,22},{7,15},{8,0},{9,25... | collective-permute-start | bytes 5505032 | tf_op jit(solution)/shard_map/ppermute | solution.py:446
  45.2 4.3 %collective-permute-start.10 = (f32[128,128]{1,0:T(8,128)S(1)}, f32[128,128]{1,0:T(8,128)S(1)}, u32[]{:S(2)}, u32[]{:S(2)}) collective-permute-start(f32[128,128]{1,0:T(8,128)S(1)} %last_cross.1), channel_id=1, source_target_pairs={{0,1},{1,0},{2,3},{3,2},{4,5},{5,4},{6,7},{7,6},{8,9},{9,8},{10,11... | collective-permute-start | bytes 196616 | tf_op jit(solution)/shard_map/ppermute | solution.py:453
  45.3 4.2 %collective-permute-start.11 = (f32[128,128]{1,0:T(8,128)S(1)}, f32[128,128]{1,0:T(8,128)S(1)}, u32[]{:S(2)}, u32[]{:S(2)}) collective-permute-start(f32[128,128]{1,0:T(8,128)S(1)} %last_cross.1), channel_id=1, source_target_pairs={{0,3},{1,2},{2,1},{3,0},{4,7},{5,6},{6,5},{7,4},{8,11},{9,10},{10,... | collective-permute-start | bytes 196616 | tf_op jit(solution)/shard_map/ppermute | solution.py:453
  46.5 7.9 %collective-permute-start.12 = (f32[128,128]{1,0:T(8,128)S(1)}, f32[128,128]{1,0:T(8,128)S(1)}, u32[]{:S(2)}, u32[]{:S(2)}) collective-permute-start(f32[128,128]{1,0:T(8,128)S(1)} %last_cross.1), channel_id=1, source_target_pairs={{0,5},{1,4},{2,7},{3,6},{4,1},{5,0},{6,3},{7,2},{8,13},{9,12},{10,... | collective-permute-start | bytes 196616 | tf_op jit(solution)/shard_map/ppermute | solution.py:453
  47.9 6.5 %collective-permute-start.13 = (f32[128,128]{1,0:T(8,128)S(1)}, f32[128,128]{1,0:T(8,128)S(1)}, u32[]{:S(2)}, u32[]{:S(2)}) collective-permute-start(f32[128,128]{1,0:T(8,128)S(1)} %last_cross.1), channel_id=1, source_target_pairs={{0,7},{1,6},{2,5},{3,4},{4,3},{5,2},{6,1},{7,0},{8,15},{9,14},{10,... | collective-permute-start | bytes 196616 | tf_op jit(solution)/shard_map/ppermute | solution.py:453
  54.4 2.4 %collective-permute-start.14 = (f32[128,128]{1,0:T(8,128)S(1)}, f32[128,128]{1,0:T(8,128)S(1)}, u32[]{:S(2)}, u32[]{:S(2)}) collective-permute-start(f32[128,128]{1,0:T(8,128)S(1)} %add_add_fusion.1), channel_id=1, source_target_pairs={{0,1},{1,0},{2,3},{3,2},{4,5},{5,4},{6,7},{7,6},{8,9},{9,8},{10,11... | collective-permute-start | bytes 196616 | tf_op jit(solution)/shard_map/ppermute | solution.py:487
  54.8 5.0 %collective-permute-start.15 = (f32[128,128]{1,0:T(8,128)S(1)}, f32[128,128]{1,0:T(8,128)S(1)}, u32[]{:S(2)}, u32[]{:S(2)}) collective-permute-start(f32[128,128]{1,0:T(8,128)S(1)} %add_add_fusion.1), channel_id=1, source_target_pairs={{0,8},{1,17},{2,10},{3,19},{4,12},{5,21},{6,14},{7,23},{8,24},{9,1... | collective-permute-start | bytes 196616 | tf_op jit(solution)/shard_map/ppermute | solution.py:446
  56.3 11.2 %collective-permute-start.8 = (f32[512,128]{1,0:T(8,128)S(1)}, f32[512,128]{1,0:T(8,128)S(1)}, u32[]{:S(2)}, u32[]{:S(2)}) collective-permute-start(f32[512,128]{1,0:T(8,128)S(1)} %get-tuple-element.50.tail_ref.refs_1_), channel_id=1, source_target_pairs={{0,16},{1,9},{2,18},{3,11},{4,20},{5,13},{6,22},{7,15},{8,0},{9,25... | collective-permute-start | bytes 786440 | tf_op jit(solution)/shard_map/ppermute | solution.py:446
  63.5 2.1 %collective-permute-start.16 = (f32[256,128]{1,0:T(8,128)S(1)}, f32[256,128]{1,0:T(8,128)S(1)}, u32[]{:S(2)}, u32[]{:S(2)}) collective-permute-start(f32[256,128]{1,0:T(8,128)S(1)} %second_rotation.1.refs_6_), channel_id=1, source_target_pairs={{0,1},{1,0},{2,3},{3,2},{4,5},{5,4},{6,7},{7,6},{8,9},{9,8},{10,11... | collective-permute-start | bytes 393224 | tf_op jit(solution)/shard_map/ppermute | solution.py:489

commit v4 on v3

v4 whole, which is shorter than its diff:
```python
import functools

import jax
import jax.numpy as jnp
from jax import lax
from jax.experimental import pallas as pl
from jax.experimental.pallas import tpu as pltpu
from jax.sharding import PartitionSpec as P


F32 = jnp.float32
BF16 = jnp.bfloat16
SCOPED = 16 * 1024 * 1024
WHOLE = 54 * 1024 * 1024

RAW = 13
SMALL = 8
LAST = 4
BULK = 28
STEP = 4


def after(p, n):
    if p == 0:
        return 1
    if p % 2:
        return n - 2 if p == n - 1 else p + 2
    return p - 2


def halves(x):
    high = x.astype(BF16)
    return high, (x - high.astype(F32)).astype(BF16)


def dot(left, right, contract=((1,), (0,))):
    return lax.dot_general(left, right, (contract, ((), ())), preferred_element_type=F32)


def spread(x):
    twice = jnp.concatenate(halves(x), 1)
    return twice, jnp.concatenate([twice, twice], 0)


def product(left, right):
    width = right.shape[1] // 2
    both = dot(left, right)
    return both[:, :width] + both[:, width:]


def right_parts(right):
    high, low = halves(right)
    return jnp.concatenate([high, low], 1), high


def rows_product(left, parts):
    return halves_product(*halves(left), parts)


def halves_product(high, low, parts):
    width = parts[1].shape[1]
    both = dot(high, parts[0])
    return both[:, :width] + (both[:, width:] + dot(low, parts[1]))


def eye_of(width):
    rows = lax.broadcasted_iota(jnp.int32, (width, width), 0)
    cols = lax.broadcasted_iota(jnp.int32, (width, width), 1)
    return rows, cols


def polar(cross, sign):
    rows, cols = eye_of(cross.shape[0])
    unit = (rows == cols).astype(F32)
    damp = 1.0 / (1.0 + jnp.sqrt(jnp.sum(cross * cross, keepdims=True)))
    left, right = spread(cross)
    left_t, right_t = spread(cross.T)
    s = [product(left, right_t) * (damp * damp), product(left_t, right) * (damp * damp)]
    x = cross * (damp * sign)
    x_left = spread(x)[0]
    s_spread = [spread(a) for a in s]
    s2 = [product(*a) for a in s_spread]
    xs = product(x_left, s_spread[1][1])
    s2_spread = [spread(a) for a in s2]
    s3 = [product(a[0], b[1]) for a, b in zip(s2_spread, s_spread)]
    s4 = [product(*a) for a in s2_spread]
    xs2, xs3 = product(x_left, s2_spread[1][1]), product(spread(xs)[0], s2_spread[1][1])
    e = [0.75 * a - 0.25 * b for a, b in zip(s2, s3)]
    z = [unit - 0.5 * a + 0.5 * b - 0.25 * (0.75 * c - 0.25 * d) for a, b, c, d in zip(s, e, s3, s4)]
    w = [0.75 * unit + 0.25 * a for a in e]
    xw = 0.75 * x + 0.25 * (0.75 * xs2 - 0.25 * xs3)
    e2 = [product(*spread(a)) for a in e]
    zw = [product(spread(a)[0], spread(b)[1]) for a, b in zip(z, w)]
    z_right = spread(z[1])[1]
    xz, xwz = product(x_left, z_right), product(spread(xw)[0], z_right)
    e2_right = [spread(a)[1] for a in e2]
    upper, lower = [a + 0.5 * product(spread(b)[0], c) for a, b, c in zip(z, zw, e2_right)]
    return upper, xz + 0.5 * product(spread(xwz)[0], e2_right[1]), lower


def scaled(cross, down, across):
    return cross * lax.rsqrt(down + 1e-06) * lax.rsqrt(across + 1e-06)


def rotation_of(upper, cross, lower, sign):
    width = cross.shape[0]
    rows, cols = eye_of(width)
    same = rows == cols
    zero = jnp.zeros((width, width), F32)
    down = jnp.sum(jnp.where(same, upper, zero), 1, keepdims=True)
    across = jnp.sum(jnp.where(same, lower, zero), 0, keepdims=True)
    top, wide, bottom = polar(scaled(cross, down, across), sign)
    first = jnp.concatenate([jnp.concatenate([top, wide], 1), jnp.concatenate([-wide.T, bottom], 1)], 0)
    gram = jnp.concatenate(
        [jnp.concatenate([upper, cross], 1), jnp.concatenate([cross.T, lower], 1)], 0
    )
    turned = rows_product(gram, right_parts(first))
    second_cross = rows_product(first[:, :width].T, right_parts(turned[:, width:]))
    diagonal = jnp.sum(first * turned, 0, keepdims=True)
    down = jnp.sum(jnp.where(same, diagonal[:, :width], zero), 1, keepdims=True)
    top, wide, bottom = polar(scaled(second_cross, down, diagonal[:, width:]), sign)
    return gram, first, jnp.concatenate([top, -wide.T], 0), jnp.concatenate([wide, bottom], 0)


def core_of():
    return lax.rem(lax.axis_index("row"), 2)


def first_is_upper():
    p = lax.axis_index("pair")
    clock_upper = (p == 0) | (lax.rem(p, 2) == 1)
    return (core_of() == 0) == clock_upper


def call(kernel, outs, args, name, flops=0, scratch=(), aliases=None, limit=SCOPED):
    places = [place for _, place in args]
    outs = [(*out, F32)[:3] for out in outs]
    out_places = [place for _, place, _ in outs]
    return pl.pallas_call(
        kernel,
        in_specs=[pl.BlockSpec(memory_space=place) for place in places],
        out_specs=[pl.BlockSpec(memory_space=place) for place in out_places],
        out_shape=[
            place(shape, dtype) if place == HERE else jax.ShapeDtypeStruct(shape, dtype) for shape, place, dtype in outs
        ],
        scratch_shapes=list(scratch),
        input_output_aliases=aliases or {},
        compiler_params=pltpu.CompilerParams(vmem_limit_bytes=limit),
        cost_estimate=pl.CostEstimate(flops=flops if flops == LONG else 0, bytes_accessed=0, transcendentals=0),
        name=name,
    )(*[pltpu.with_memory_space_constraint(array, place) for array, place in args])


LONG = 11500000000
HERE = pltpu.VMEM
FAR = pltpu.HBM


class Rows:
    def __init__(self, *parts):
        self.parts = parts

    @classmethod
    def of(cls, refs, sizes):
        return cls(*[(ref, sum(sizes[:k]), sizes[k], 0) for k, ref in enumerate(refs)])

    def at(self, start, count):
        for ref, first, number, offset in self.parts:
            if first <= start and start + count <= first + number:
                return ref, pl.ds(offset + start - first, count)
        raise ValueError(start)

    def get(self, start, count):
        ref, rows = self.at(start, count)
        return ref[rows, :]

    def pair(self, start, count):
        ref, rows = self.at(start, count)
        return jnp.concatenate([ref[0, rows, :], ref[1, rows, :]], 1)


def spans(start, stop, step, *cuts):
    pieces = []
    while start < stop:
        count = min([step, stop - start] + [cut - start for cut in cuts if cut > start])
        pieces.append((start, count))
        start += count
    return pieces


def raw_rows(matrix, count):
    width = matrix.shape[2]

    def kernel(matrix_ref, out_ref, sems):
        copies = [
            pltpu.make_async_copy(matrix_ref.at[k, pl.ds(0, count)], out_ref.at[k], sems.at[k]) for k in range(2)
        ]
        for copy in copies:
            copy.start()
        for copy in copies:
            copy.wait()

    return call(
        kernel,
        [((2, count, width), HERE)],
        [(matrix, FAR)],
        "raw_rows",
        0,
        [pltpu.SemaphoreType.DMA((2,))],
        limit=WHOLE,
    )[0]


def local_gram(matrix, low, step):
    rows, width = matrix.shape[1:]
    early = low.shape[1]

    def kernel(matrix_ref, low_ref, high_ref, keep_ref, give_ref, sems):
        copies = []
        for k, (start, count) in enumerate(spans(early, rows, step)):
            place = pl.ds(start - early, count)
            copies.append(pltpu.make_async_copy(matrix_ref.at[:, pl.ds(start, count)], high_ref.at[:, place], sems.at[k]))
            copies[-1].start()
        local = Rows.of((low_ref, high_ref), (early, rows - early))
        total = jnp.zeros((2 * width, 4 * width), F32)
        for start, count in spans(0, rows, step, early):
            if start >= early:
                copies.pop(0).wait()
            high, low = halves(local.pair(start, count))
            total = total + dot(high, jnp.concatenate([high, low], 1), ((0,), (0,)))
        rest = total[:, 2 * width :]
        total = total[:, : 2 * width] + (rest + rest.T)
        upper, cross, lower = total[:width, :width], total[:width, width:], total[width:, width:]
        r, c = eye_of(width)
        diagonal = jnp.sum(jnp.where(r == c, lower, jnp.zeros_like(lower)), 0, keepdims=True)
        packed = jnp.where(r <= c, upper, lower)
        pad = jnp.broadcast_to(diagonal, (8, width))
        mine = core_of() == 0
        keep_ref[:width] = jnp.where(mine, cross, packed)
        give_ref[:width] = jnp.where(mine, packed, cross)
        keep_ref[width:] = pad
        give_ref[width:] = pad

    outs = [((2, rows - early, width), HERE)] + [((width + 8, width), HERE)] * 2
    return call(
        kernel,
        outs,
        [(matrix, FAR), (low, HERE)],
        "gram",
        16 * rows * width * width,
        [pltpu.SemaphoreType.DMA((len(spans(early, rows, step)),))],
        limit=WHOLE,
    )


def first_rotation(mine, other):
    width = mine.shape[1]

    def kernel(mine_ref, other_ref, first_ref, second_ref, gram_ref):
        holds_cross = core_of() == 0
        mine, other = mine_ref[...], other_ref[...]
        cross = jnp.where(holds_cross, mine[:width], other[:width])
        packed = jnp.where(holds_cross, other, mine)
        diagonal = packed[width : width + 1]
        packed = packed[:width]
        rows, cols = eye_of(width)
        flipped = packed.T
        upper = jnp.where(rows <= cols, packed, flipped)
        lower = jnp.where(rows > cols, packed, flipped)
        lower = jnp.where(rows == cols, diagonal, lower)
        gram, first, left, right = rotation_of(upper, cross, lower, 1.0)
        upper_first = first_is_upper()
        gram_ref[...] = gram
        first_ref[...] = rows_product(first, right_parts(jnp.where(upper_first, left, right)))
        second_ref[...] = rows_product(first, right_parts(jnp.where(upper_first, right, left)))

    half = ((2 * width, width), HERE)
    return call(kernel, [half, half, ((2 * width, 2 * width), HERE)], [(mine, HERE), (other, HERE)], "first_rotation")


def small_part(high, turn, small, step):
    width = turn.shape[1]

    def kernel(high_ref, turn_ref, out_ref):
        local = Rows((high_ref, 0, high.shape[1], 0))
        out_ref[: 2 * width] = turn_ref[...]
        parts = right_parts(turn_ref[...])
        for start, number in spans(0, small, step):
            out_ref[pl.ds(2 * width + start, number), :] = rows_product(local.pair(start, number), parts)

    return call(
        kernel, [((2 * width + small, width), HERE)], [(high, HERE), (turn, HERE)], "small_part", 12 * small * width * width
    )[0]


def sent_parts(high, first, second, gram, small, last, step):
    width = first.shape[1]
    count = high.shape[1]

    def kernel(high_ref, first_ref, second_ref, gram_ref, main_ref, last_ref, second_gram_ref):
        local = Rows((high_ref, 0, count, 0))
        out = Rows((main_ref, small, count - small - last, 0), (last_ref, count - last, last, 0))
        parts = right_parts(first_ref[...])
        for start, number in spans(small, count, step, count - last):
            ref, place = out.at(start, number)
            ref[place, :] = rows_product(local.pair(start, number), parts)
        gram = gram_ref[...]
        for turn_ref, place in ((first_ref, last_ref.at[pl.ds(last, width), :]), (second_ref, second_gram_ref)):
            turn = turn_ref[...]
            place[...] = rows_product(turn.T, right_parts(rows_product(gram, right_parts(turn))))

    return call(
        kernel,
        [((count - small - last, width), HERE), ((last + width, width), HERE), ((width, width), HERE)],
        [(high, HERE), (first, HERE), (second, HERE), (gram, HERE)],
        "sent_parts",
        12 * count * width * width,
    )


def rest_parts(low, high, first, second, sent, bulk, step):
    width = first.shape[1]
    sizes = low.shape[1], high.shape[1]
    early, rows = sizes[0], sum(sizes)
    arrays = [array for array, *_ in sent]

    def kernel(low_ref, high_ref, first_ref, second_ref, *refs):
        bulk_ref, tail_ref, high_half_ref, low_half_ref = refs[len(sent) :]
        here = Rows.of((low_ref, high_ref), sizes)
        there = Rows(*[(ref, *where) for ref, (_, *where) in zip(refs, sent)])
        out = Rows.of((bulk_ref, tail_ref), (bulk, rows - bulk))
        parts = right_parts(second_ref[...])
        for start, count in spans(0, rows, step, bulk, early):
            ref, place = out.at(start, count)
            ref[place, :] = rows_product(here.pair(start, count), parts)
        parts = right_parts(first_ref[...])
        for start, count in spans(0, rows, step, early, *[first for _, first, *_ in sent]):
            block = rows_product(here.pair(start, count), parts) if start < early else there.get(start, count)
            place = pl.ds(start, count)
            high_half_ref[place, :], low_half_ref[place, :] = halves(block)

    return call(
        kernel,
        [((bulk, width), HERE), ((rows - bulk, width), HERE)] + [((rows, width), HERE, BF16)] * 2,
        [(part, HERE) for part in (low, high, first, second, *arrays)],
        "rest_parts",
        12 * (rows + early) * width * width,
    )


def cross_term(high, low):
    width = high.shape[1] // 2
    own = jnp.concatenate([high[:, :width], low[:, :width]], 1)
    far = jnp.concatenate([high[:, width:], low[:, width:]], 1)
    return dot(own, far, ((0,), (0,)))


def cross_sum(total):
    width = total.shape[0] // 2
    return (total[:width, :width] + total[:width, width:]) + (total[width:, :width] + total[width:, width:])


def raw_cross(far_raw, far_small, bulk, tail, step):
    width = bulk.shape[1]
    early, small = far_raw.shape[1], far_small.shape[0] - 2 * width

    def kernel(raw_ref, small_ref, bulk_ref, tail_ref, high_ref, low_ref, out_ref):
        own = Rows.of((bulk_ref, tail_ref), (bulk.shape[0], tail.shape[0]))
        raw = Rows((raw_ref, 0, early, 0))
        far = Rows((small_ref, early, small, 2 * width))
        parts = right_parts(small_ref[: 2 * width])
        total = jnp.zeros((2 * width, 2 * width), F32)
        for start, count in spans(0, early + small, step, early, bulk.shape[0]):
            block = rows_product(raw.pair(start, count), parts) if start < early else far.get(start, count)
            high, low = halves(jnp.concatenate([own.get(start, count), block], 1))
            place = pl.ds(start, count)
            high_ref[place, :], low_ref[place, :] = high, low
            total = total + cross_term(high, low)
        out_ref[...] = cross_sum(total)

    return call(
        kernel,
        [((early + small, 2 * width), HERE, BF16)] * 2 + [((width, width), HERE)],
        [(far_raw, HERE), (far_small, HERE), (bulk, HERE), (tail, HERE)],
        "raw_cross",
        12 * (early + small) * width * width,
    )


def more_cross(far, first_row, count, bulk, tail, so_far, step, name):
    width = bulk.shape[1]

    def kernel(far_ref, bulk_ref, tail_ref, total_ref, high_ref, low_ref, out_ref):
        own = Rows.of((bulk_ref, tail_ref), (bulk.shape[0], tail.shape[0]))
        part = Rows((far_ref, first_row, count, 0))
        total = jnp.zeros((2 * width, 2 * width), F32)
        for start, number in spans(first_row, first_row + count, step, bulk.shape[0]):
            high, low = halves(jnp.concatenate([own.get(start, number), part.get(start, number)], 1))
            place = pl.ds(start - first_row, number)
            high_ref[place, :], low_ref[place, :] = high, low
            total = total + cross_term(high, low)
        out_ref[...] = total_ref[...] + cross_sum(total)

    return call(
        kernel,
        [((count, 2 * width), HERE, BF16)] * 2 + [((width, width), HERE)],
        [(far, HERE), (bulk, HERE), (tail, HERE), (so_far, HERE)],
        name,
        6 * count * width * width,
    )


def second_rotation(own_gram, far_sent, here, there):
    width = here.shape[1]
    place = far_sent.shape[0] - width

    def kernel(own_gram_ref, far_ref, here_ref, there_ref, out_ref):
        p, n = lax.axis_index("pair"), lax.axis_size("pair")
        odd = lax.rem(p, 2) == 1
        outward = core_of() == 1
        own_upper_out = (p == 0) | (odd & (p != n - 1))
        own_upper = (outward & own_upper_out) | (jnp.logical_not(outward) & jnp.logical_not(odd))
        sign = jnp.where(own_upper, 1.0, -1.0).astype(F32)
        cross = here_ref[...] + there_ref[...].T
        _, first, left, right = rotation_of(own_gram_ref[...], cross, far_ref[pl.ds(place, width), :], sign)
        keeps_own = (outward & (p == 0)) | (jnp.logical_not(outward) & (p == 1))
        out_ref[...] = rows_product(first, right_parts(jnp.where(keeps_own, left, right)))

    return call(
        kernel,
        [((2 * width, width), HERE)],
        [(own_gram, HERE), (far_sent, HERE), (here, HERE), (there, HERE)],
        "second_rotation",
        LONG,
    )[0]


def last_product(load, arrays, turn, done, slot_of, start, count, rows, step, cuts, name):
    width = turn.shape[1]
    pieces = spans(start, start + count, step, *cuts)

    def kernel(*refs):
        turn_ref = refs[len(arrays)]
        out_ref, stage_ref, sems = refs[-3:]
        parts = right_parts(turn_ref[...])
        slot = slot_of()
        copies = []
        for k, (row, number) in enumerate(pieces):
            place = pl.ds(row - start, number)
            stage_ref[place, :] = halves_product(*load(refs, row, number), parts)
            copies.append(
                pltpu.make_async_copy(stage_ref.at[place, :], out_ref.at[slot, pl.ds(row, number), :], sems.at[k])
            )
            copies[-1].start()
        for copy in copies:
            copy.wait()

    args = [(array, HERE) for array in (*arrays, turn)] + ([] if done is None else [(done, FAR)])
    return call(
        kernel,
        [((2, rows, width), FAR)],
        args,
        name,
        12 * count * width * width,
        [pltpu.VMEM((count, width), F32), pltpu.SemaphoreType.DMA((len(pieces),))],
        None if done is None else {len(args) - 1: 0},
    )[0]


def first_slot():
    return jnp.where(lax.rem(lax.axis_index("pair"), 2) == core_of(), 1, 0)


def body(pairs_count, rows_count, matrix):
    rows, width = matrix.shape[1:]
    unit = rows // 32
    early, small, last, bulk, step = (part * unit for part in (RAW, SMALL, LAST, BULK, STEP))
    main = rows - early - small - last
    flat = [(p, r) for p in range(pairs_count) for r in range(rows_count)]
    ahead = {p: after(p, pairs_count) for p in range(pairs_count)}
    behind = {q: p for p, q in ahead.items()}

    def route(moves):
        return [(p * rows_count + r, q * rows_count + t) for (p, r) in flat for (q, t) in [moves(p, r)]]

    outward = route(lambda p, r: (ahead[p] if r % 2 == 0 else behind[p], r))
    inward = route(lambda p, r: (behind[p] if r % 2 == 0 else ahead[p], r))

    core = [(r, r ^ 1) for r in range(rows_count)]

    def travel(block, moves):
        return lax.ppermute(block, ("pair", "row"), moves)

    def chip_sum(block, radix, flip=0):
        distance = 2
        while distance < rows_count:
            steps = [distance] if radix == 2 or 2 * distance >= rows_count else [distance, 2 * distance, 3 * distance]
            hops = [d ^ flip for d in steps] + ([1] if flip else [])
            others = [lax.ppermute(block, "row", [(r, r ^ d) for r in range(rows_count)]) for d in hops]
            block = others.pop() if flip else block
            for other in others:
                block = block + other
            distance *= 1 + len(steps)
            flip = 0
        return block

    def other_sum(block):
        return chip_sum(block, 4, 1)

    low = raw_rows(matrix, early)
    far_raw = travel(low, outward)
    high, keep, give = local_gram(matrix, low, step)
    mine = chip_sum(keep + lax.ppermute(give, "row", core), 4)
    other = lax.ppermute(mine, "row", core)
    turn_first, turn_second, gram = first_rotation(mine, other)

    sent_small = small_part(high, turn_first, small, step)
    far_small = travel(sent_small, outward)
    turn_main, sent_small, far_raw = lax.optimization_barrier((turn_first, sent_small, far_raw))
    sent_main, sent_last, second_gram = sent_parts(high, turn_main, turn_second, gram, small, last, step)
    far_main, far_last = travel(sent_main, outward), travel(sent_last, outward)
    turn_second, sent_main = lax.optimization_barrier((turn_second, sent_main))
    sent = [(sent_small, early, small, 2 * width), (sent_main, early + small, main, 0), (sent_last, rows - last, last, 0)]
    second_bulk, second_tail, *first_halves = rest_parts(low, high, turn_first, turn_second, sent, bulk, step)

    *raw_halves, cross = raw_cross(far_raw, far_small, second_bulk, second_tail, step)
    far_main, cross = lax.optimization_barrier((far_main, cross))
    *main_halves, cross = more_cross(
        far_main, early + small, main, second_bulk, second_tail, cross, step, "main_cross"
    )
    cross, later_bulk, later_tail = lax.optimization_barrier((cross, second_bulk, second_tail))
    far_bulk, far_tail = travel(later_bulk, inward), travel(later_tail, inward)
    *last_halves, cross = more_cross(far_last, rows - last, last, second_bulk, second_tail, cross, step, "last_cross")

    total = other_sum(cross)
    there = travel(total, outward)
    here = lax.ppermute(total, "row", core)
    turn_here = second_rotation(second_gram, far_last, here, there)
    turn_there = lax.ppermute(turn_here, "row", core)

    sizes = early + small, main, last

    def load_here(refs, row, number):
        return [Rows.of(refs[k : 6 : 2], sizes).get(row, number) for k in (0, 1)]

    def other_slot():
        return 1 - first_slot()

    def load_there(refs, row, number):
        place = pl.ds(row, number)
        far = halves(Rows.of(refs[2:4], (bulk, rows - bulk)).get(row, number))
        return [jnp.concatenate([ref[place, :], half], 1) for ref, half in zip(refs, far)]

    cuts = early + small, rows - last
    done = last_product(
        load_here, raw_halves + main_halves + last_halves, turn_here, None, first_slot, 0, rows, rows, step, cuts, "here_product"
    )

    def load_tail(refs, row, number):
        place = pl.ds(row, number)
        far = halves(Rows((refs[2], bulk, rows - bulk, 0)).get(row, number))
        return [jnp.concatenate([ref[place, :], half], 1) for ref, half in zip(refs, far)]

    done = last_product(
        load_there, [*first_halves, far_bulk, far_bulk], turn_there, done, other_slot, 0, bulk, rows, step, [], "bulk_product"
    )
    return last_product(
        load_tail, [*first_halves, far_tail], turn_there, done, other_slot, bulk, rows - bulk, rows, step, [], "tail_product"
    )


def solution(mesh):
    spec = P(None, "row", "pair")
    run = functools.partial(body, mesh.shape["pair"], mesh.shape["row"])
    return jax.shard_map(run, mesh=mesh, in_specs=(spec,), out_specs=spec, check_vma=False)
```

time: 68.9 us -> 67.3 us (0.977)
    ppermute x7, waiting for transfers between devices: 10.9 us -> 9.57 us  [chip_sum(): lax.ppermute(block, 'row', [(r, r ^ d) for r in range(rows_count)])]
    ppermute x7, waiting for transfers between devices: 13.9 us -> 14.8 us  [travel(): return lax.ppermute(block, ('pair', 'row'), moves)]
    pallas_call x12 -> x13, Pallas kernels: 21.2 us -> 20.6 us  [call(): pl.pallas_call(kernel, in_specs=[pl.BlockSpec(memory_space=place) for pla...]
  transfers between devices with their start and end apart: 18 -> 18, of which waited for: 9 -> 12; matrix products, arithmetic and copies ran while one was open for 0% -> 0% of each run, Pallas kernels for 24% -> 27%
where the time goes in v4:
time: 67.3 us; the launch traced here: 67.2 us
  waiting for transfers between devices  26.8 us (40%)
  Pallas kernels  20.6 us (31%)
  starting transfers between devices  19.4 us (29%)
    pallas_call x13, Pallas kernels, call(): pl.pallas_call(kernel, in_specs=[pl.BlockSpec(memory_space=place) for pla...  20.6 us
    ppermute x7, waiting for transfers between devices, travel(): return lax.ppermute(block, ('pair', 'row'), moves)  14.8 us
    ppermute x7, starting transfers between devices, travel(): return lax.ppermute(block, ('pair', 'row'), moves)  10.5 us
    ppermute x7, waiting for transfers between devices, chip_sum(): lax.ppermute(block, 'row', [(r, r ^ d) for r in range(rows_count)])  9.57 us
    ppermute x7, starting transfers between devices, chip_sum(): lax.ppermute(block, 'row', [(r, r ^ d) for r in range(rows_count)])  8.74 us
  transfers between devices with their start and end apart: 18, of which 12 were waited for; matrix products, arithmetic and copies ran while one was open for 0% of the time, Pallas kernels for 27%

profile of v4, /device:TPU:0, one launch (start us, length us, event | category | flops | bytes accessed | tf_op | source)
XLA Modules:
  0.0 67.2 jit_solution(10531391199656277638)
XLA Ops:
  0.0 1.4 %raw_rows.1.low_ref = f32[2,1664,128]{2,1,0:T(8,128)S(1)} custom-call(f32[2,4096,128]{2,1,0:T(8,128)} %matrix_ref.3), custom_call_target="tpu_custom_call" | custom-call | tf_op jit(solution)/shard_map/raw_rows/pallas_call | solution.py:139
  1.4 3.0 %collective-permute-start.5 = (f32[2,1664,128]{2,1,0:T(8,128)S(1)}, f32[2,1664,128]{2,1,0:T(8,128)S(1)}, u32[]{:S(2)}, u32[]{:S(2)}) collective-permute-start(f32[2,1664,128]{2,1,0:T(8,128)S(1)} %raw_rows.1.low_ref), channel_id=1, source_target_pairs={{0,8},{1,17},{2,10},{3,19},{4,12},{5,21},{6,14},{7,23},{8,24},{9,1... | collective-permute-start | bytes 5111816 | tf_op jit(solution)/shard_map/ppermute | solution.py:492
  4.4 2.8 %gram.1 = (f32[2,2432,128]{2,1,0:T(8,128)S(1)}, f32[136,128]{1,0:T(8,128)S(1)}, f32[136,128]{1,0:T(8,128)S(1)}) custom-call(f32[2,4096,128]{2,1,0:T(8,128)} %matrix_ref.3, f32[2,1664,128]{2,1,0:T(8,128)S(1)} %raw_rows.1.low_ref), custom_call_target="tpu_custom_call" | custom-call | tf_op jit(solution)/shard_map/gram/pallas_call | solution.py:139
  7.3 1.2 %collective-permute-done = f32[136,128]{1,0:T(8,128)S(1)} collective-permute-done((f32[136,128]{1,0:T(8,128)S(1)}, f32[136,128]{1,0:T(8,128)S(1)}, u32[]{:S(2)}, u32[]{:S(2)}) %collective-permute-start) | collective-permute-done | bytes 69664 | tf_op jit(solution)/shard_map/ppermute | solution.py:513
  8.6 3.7 %collective-permute-start.3 = (f32[136,128]{1,0:T(8,128)S(1)}, f32[136,128]{1,0:T(8,128)S(1)}, u32[]{:S(2)}, u32[]{:S(2)}) collective-permute-start(f32[136,128]{1,0:T(8,128)S(1)} %add.21), channel_id=1, source_target_pairs={{0,6},{1,7},{2,4},{3,5},{4,2},{5,3},{6,0},{7,1},{8,14},{9,15},{10,... | collective-permute-start | bytes 208904 | tf_op jit(solution)/shard_map/ppermute | solution.py:499
  12.3 0.8 %collective-permute-start.1 = (f32[136,128]{1,0:T(8,128)S(1)}, f32[136,128]{1,0:T(8,128)S(1)}, u32[]{:S(2)}, u32[]{:S(2)}) collective-permute-start(f32[136,128]{1,0:T(8,128)S(1)} %add.21), channel_id=1, source_target_pairs={{0,2},{1,3},{2,0},{3,1},{4,6},{5,7},{6,4},{7,5},{8,10},{9,11},{10,... | collective-permute-start | bytes 208904 | tf_op jit(solution)/shard_map/ppermute | solution.py:499
  13.0 2.1 %collective-permute-done.3 = f32[136,128]{1,0:T(8,128)S(1)} collective-permute-done((f32[136,128]{1,0:T(8,128)S(1)}, f32[136,128]{1,0:T(8,128)S(1)}, u32[]{:S(2)}, u32[]{:S(2)}) %collective-permute-start.3) | collective-permute-done | bytes 69664 | tf_op jit(solution)/shard_map/ppermute | solution.py:499
  15.1 3.3 %collective-permute-done.2 = f32[136,128]{1,0:T(8,128)S(1)} collective-permute-done((f32[136,128]{1,0:T(8,128)S(1)}, f32[136,128]{1,0:T(8,128)S(1)}, u32[]{:S(2)}, u32[]{:S(2)}) %collective-permute-start.2) | collective-permute-done | bytes 69664 | tf_op jit(solution)/shard_map/ppermute | solution.py:499
  18.6 1.2 %collective-permute-done.4.other_ref = f32[136,128]{1,0:T(8,128)S(1)} collective-permute-done((f32[136,128]{1,0:T(8,128)S(1)}, f32[136,128]{1,0:T(8,128)S(1)}, u32[]{:S(2)}, u32[]{:S(2)}) %collective-permute-start.4) | collective-permute-done | bytes 69664 | tf_op jit(solution)/shard_map/ppermute | solution.py:514
  19.8 3.1 %first_rotation.1 = (f32[256,128]{1,0:T(8,128)S(1)}, f32[256,128]{1,0:T(8,128)S(1)}, f32[256,256]{1,0:T(8,128)S(1)}) custom-call(f32[136,128]{1,0:T(8,128)S(1)} %add_add_fusion.mine_ref, f32[136,128]{1,0:T(8,128)S(1)} %collective-permute-done.4.other_ref), custom_call_target="tpu_custom_call" | custom-call | tf_op jit(solution)/shard_map/first_rotation/pallas_call | solution.py:139
  23.3 1.6 %collective-permute-start.7 = (f32[1280,128]{1,0:T(8,128)S(1)}, f32[1280,128]{1,0:T(8,128)S(1)}, u32[]{:S(2)}, u32[]{:S(2)}) collective-permute-start(f32[1280,128]{1,0:T(8,128)S(1)} %small_part.1.refs_0_), channel_id=1, source_target_pairs={{0,8},{1,17},{2,10},{3,19},{4,12},{5,21},{6,14},{7,23},{8,24},{9,1... | collective-permute-start | bytes 1966088 | tf_op jit(solution)/shard_map/ppermute | solution.py:492
  24.9 1.0 %sent_parts.1 = (f32[896,128]{1,0:T(8,128)S(1)}, f32[640,128]{1,0:T(8,128)S(1)}, f32[128,128]{1,0:T(8,128)S(1)}) custom-call(f32[2,2432,128]{2,1,0:T(8,128)S(1)} %get-tuple-element.37.high_ref, f32[256,128]{1,0:T(8,128)S(1)} %get-tuple-element.42.turn_ref.first_ref, f32[256,128]{1,0:T(8,128)S(1)} %get-tuple-element.45.second_ref, ...), custom_call_target="tpu_custom_call" | custom-call | tf_op jit(solution)/shard_map/sent_parts/pallas_call | solution.py:139
  25.9 1.4 %collective-permute-start.6 = (f32[896,128]{1,0:T(8,128)S(1)}, f32[896,128]{1,0:T(8,128)S(1)}, u32[]{:S(2)}, u32[]{:S(2)}) collective-permute-start(f32[896,128]{1,0:T(8,128)S(1)} %get-tuple-element.47.refs_1_), channel_id=1, source_target_pairs={{0,8},{1,17},{2,10},{3,19},{4,12},{5,21},{6,14},{7,23},{8,24},{9,1... | collective-permute-start | bytes 1376264 | tf_op jit(solution)/shard_map/ppermute | solution.py:492
  27.3 1.5 %collective-permute-start.9 = (f32[640,128]{1,0:T(8,128)S(1)}, f32[640,128]{1,0:T(8,128)S(1)}, u32[]{:S(2)}, u32[]{:S(2)}) collective-permute-start(f32[640,128]{1,0:T(8,128)S(1)} %get-tuple-element.48.refs_2_), channel_id=1, source_target_pairs={{0,8},{1,17},{2,10},{3,19},{4,12},{5,21},{6,14},{7,23},{8,24},{9,1... | collective-permute-start | bytes 983048 | tf_op jit(solution)/shard_map/ppermute | solution.py:492
  28.8 1.9 %rest_parts.1 = (f32[3584,128]{1,0:T(8,128)S(1)}, f32[512,128]{1,0:T(8,128)S(1)}, bf16[4096,128]{1,0:T(8,128)(2,1)S(1)}, bf16[4096,128]{1,0:T(8,128)(2,1)S(1)}) custom-call(f32[2,1664,128]{2,1,0:T(8,128)S(1)} %raw_rows.1.low_ref, f32[2,2432,128]{2,1,0:T(8,128)S(1)} %get-tuple-element.37.high_ref, f32[256,128]{1,0:T(8,128)S(1)} %get-tuple-element.42.turn_ref.first_ref, ...), custom_call_target="tpu_custom_call" | custom-call | tf_op jit(solution)/shard_map/rest_parts/pallas_call | solution.py:139
  30.7 3.2 %collective-permute-done.7.small_ref = f32[1280,128]{1,0:T(8,128)S(1)} collective-permute-done((f32[1280,128]{1,0:T(8,128)S(1)}, f32[1280,128]{1,0:T(8,128)S(1)}, u32[]{:S(2)}, u32[]{:S(2)}) %collective-permute-start.7) | collective-permute-done | bytes 655392 | tf_op jit(solution)/shard_map/ppermute | solution.py:492
  34.0 1.4 %raw_cross.1 = (bf16[2688,256]{1,0:T(8,128)(2,1)S(1)}, bf16[2688,256]{1,0:T(8,128)(2,1)S(1)}, f32[128,128]{1,0:T(8,128)S(1)}) custom-call(f32[2,1664,128]{2,1,0:T(8,128)S(1)} %collective-permute-done.5.raw_ref, f32[1280,128]{1,0:T(8,128)S(1)} %collective-permute-done.7.small_ref, f32[3584,128]{1,0:T(8,128)S(1)} %get-tuple-element.62.bulk_ref, ...), custom_call_target="tpu_custom_call" | custom-call | tf_op jit(solution)/shard_map/raw_cross/pallas_call | solution.py:139
  35.4 3.5 %collective-permute-done.6.far_ref = f32[896,128]{1,0:T(8,128)S(1)} collective-permute-done((f32[896,128]{1,0:T(8,128)S(1)}, f32[896,128]{1,0:T(8,128)S(1)}, u32[]{:S(2)}, u32[]{:S(2)}) %collective-permute-start.6) | collective-permute-done | bytes 458784 | tf_op jit(solution)/shard_map/ppermute | solution.py:492
  39.2 0.9 %collective-permute-start.17 = (f32[3584,128]{1,0:T(8,128)S(1)}, f32[3584,128]{1,0:T(8,128)S(1)}, u32[]{:S(2)}, u32[]{:S(2)}) collective-permute-start(f32[3584,128]{1,0:T(8,128)S(1)} %get-tuple-element.62.bulk_ref), channel_id=1, source_target_pairs={{0,16},{1,9},{2,18},{3,11},{4,20},{5,13},{6,22},{7,15},{8,0},{9,25... | collective-permute-start | bytes 5505032 | tf_op jit(solution)/shard_map/ppermute | solution.py:492
  40.1 3.4 %collective-permute-done.9.far_ref = f32[640,128]{1,0:T(8,128)S(1)} collective-permute-done((f32[640,128]{1,0:T(8,128)S(1)}, f32[640,128]{1,0:T(8,128)S(1)}, u32[]{:S(2)}, u32[]{:S(2)}) %collective-permute-start.9) | collective-permute-done | bytes 327712 | tf_op jit(solution)/shard_map/ppermute | solution.py:492
  44.1 2.0 %collective-permute-start.12 = (f32[128,128]{1,0:T(8,128)S(1)}, f32[128,128]{1,0:T(8,128)S(1)}, u32[]{:S(2)}, u32[]{:S(2)}) collective-permute-start(f32[128,128]{1,0:T(8,128)S(1)} %get-tuple-element.61), channel_id=1, source_target_pairs={{0,5},{1,4},{2,7},{3,6},{4,1},{5,0},{6,3},{7,2},{8,13},{9,12},{10,... | collective-permute-start | bytes 196616 | tf_op jit(solution)/shard_map/ppermute | solution.py:499
  46.7 1.4 %collective-permute-start.10 = (f32[128,128]{1,0:T(8,128)S(1)}, f32[128,128]{1,0:T(8,128)S(1)}, u32[]{:S(2)}, u32[]{:S(2)}) collective-permute-start(f32[128,128]{1,0:T(8,128)S(1)} %get-tuple-element.61), channel_id=1, source_target_pairs={{0,1},{1,0},{2,3},{3,2},{4,5},{5,4},{6,7},{7,6},{8,9},{9,8},{10,11... | collective-permute-start | bytes 196616 | tf_op jit(solution)/shard_map/ppermute | solution.py:499
  48.1 1.5 %collective-permute-done.13 = f32[128,128]{1,0:T(8,128)S(1)} collective-permute-done((f32[128,128]{1,0:T(8,128)S(1)}, f32[128,128]{1,0:T(8,128)S(1)}, u32[]{:S(2)}, u32[]{:S(2)}) %collective-permute-start.13) | collective-permute-done | bytes 65568 | tf_op jit(solution)/shard_map/ppermute | solution.py:499
  49.6 2.7 %collective-permute-done.12 = f32[128,128]{1,0:T(8,128)S(1)} collective-permute-done((f32[128,128]{1,0:T(8,128)S(1)}, f32[128,128]{1,0:T(8,128)S(1)}, u32[]{:S(2)}, u32[]{:S(2)}) %collective-permute-start.12) | collective-permute-done | bytes 65568 | tf_op jit(solution)/shard_map/ppermute | solution.py:499
  52.3 1.6 %collective-permute-start.15 = (f32[128,128]{1,0:T(8,128)S(1)}, f32[128,128]{1,0:T(8,128)S(1)}, u32[]{:S(2)}, u32[]{:S(2)}) collective-permute-start(f32[128,128]{1,0:T(8,128)S(1)} %add_add_fusion.1), channel_id=1, source_target_pairs={{0,8},{1,17},{2,10},{3,19},{4,12},{5,21},{6,14},{7,23},{8,24},{9,1... | collective-permute-start | bytes 196616 | tf_op jit(solution)/shard_map/ppermute | solution.py:492
  54.4 3.0 %collective-permute-done.15.there_ref = f32[128,128]{1,0:T(8,128)S(1)} collective-permute-done((f32[128,128]{1,0:T(8,128)S(1)}, f32[128,128]{1,0:T(8,128)S(1)}, u32[]{:S(2)}, u32[]{:S(2)}) %collective-permute-start.15) | collective-permute-done | bytes 65568 | tf_op jit(solution)/shard_map/ppermute | solution.py:492
  57.4 2.9 %second_rotation.1.refs_6_ = f32[256,128]{1,0:T(8,128)S(1)} custom-call(f32[128,128]{1,0:T(8,128)S(1)} %get-tuple-element.59.own_gram_ref, f32[640,128]{1,0:T(8,128)S(1)} %collective-permute-done.9.far_ref, f32[128,128]{1,0:T(8,128)S(1)} %collective-permute-done.14.here_ref, f32[128,128]{1,0:T(8,128)S(1)} %collective-permute-done.15.there_ref), custom_call_target="tpu_custom_call" | custom-call | flops 11500000256 | tf_op jit(solution)/shard_map/second_rotation/pallas_call | solution.py:139
  60.4 2.0 %here_product.1.refs_5_ = f32[2,4096,128]{2,1,0:T(8,128)} custom-call(bf16[2688,256]{1,0:T(8,128)(2,1)S(1)} %get-tuple-element.63.refs_0_, bf16[2688,256]{1,0:T(8,128)(2,1)S(1)} %get-tuple-element.64.refs_1_, bf16[896,256]{1,0:T(8,128)(2,1)S(1)} %get-tuple-element.65.refs_2_, bf16[896,256]{1,0:T(8,128)(2,1)S(1)} %get-tuple-element.66.refs_3_, ...), custom_call_target="tpu_custom_call" | custom-call | tf_op jit(solution)/shard_map/here_product/pallas_call | solution.py:139
  62.5 0.8 %collective-permute-done.17.refs_2_.refs_3_ = f32[3584,128]{1,0:T(8,128)S(1)} collective-permute-done((f32[3584,128]{1,0:T(8,128)S(1)}, f32[3584,128]{1,0:T(8,128)S(1)}, u32[]{:S(2)}, u32[]{:S(2)}) %collective-permute-start.17) | collective-permute-done | bytes 1835040 | tf_op jit(solution)/shard_map/ppermute | solution.py:492
  63.2 1.9 %bulk_product.1.refs_4_ = f32[2,4096,128]{2,1,0:T(8,128)} custom-call(bf16[4096,128]{1,0:T(8,128)(2,1)S(1)} %get-tuple-element.49.refs_0_, bf16[4096,128]{1,0:T(8,128)(2,1)S(1)} %get-tuple-element.50.refs_1_, f32[3584,128]{1,0:T(8,128)S(1)} %collective-permute-done.17.refs_2_.refs_3_, ...), custom_call_target="tpu_custom_call", output_to_operand_aliasing={{}: (5, {})} | custom-call | tf_op jit(solution)/shard_map/bulk_product/pallas_call | solution.py:139
  65.1 0.9 %collective-permute-done.8.refs_2_ = f32[512,128]{1,0:T(8,128)S(1)} collective-permute-done((f32[512,128]{1,0:T(8,128)S(1)}, f32[512,128]{1,0:T(8,128)S(1)}, u32[]{:S(2)}, u32[]{:S(2)}) %collective-permute-start.8) | collective-permute-done | bytes 262176 | tf_op jit(solution)/shard_map/ppermute | solution.py:492
  66.0 1.0 %tail_product.1 = f32[2,4096,128]{2,1,0:T(8,128)} custom-call(bf16[4096,128]{1,0:T(8,128)(2,1)S(1)} %get-tuple-element.49.refs_0_, bf16[4096,128]{1,0:T(8,128)(2,1)S(1)} %get-tuple-element.50.refs_1_, f32[512,128]{1,0:T(8,128)S(1)} %collective-permute-done.8.refs_2_, ...), custom_call_target="tpu_custom_call", output_to_operand_aliasing={{}: (4, {})} | custom-call | tf_op jit(solution)/shard_map/tail_product/pallas_call | solution.py:139
  (20 shorter events, 2.8 us)
Async XLA Ops:
  1.4 23.5 %collective-permute-start.5 = (f32[2,1664,128]{2,1,0:T(8,128)S(1)}, f32[2,1664,128]{2,1,0:T(8,128)S(1)}, u32[]{:S(2)}, u32[]{:S(2)}) collective-permute-start(f32[2,1664,128]{2,1,0:T(8,128)S(1)} %raw_rows.1.low_ref), channel_id=1, source_target_pairs={{0,8},{1,17},{2,10},{3,19},{4,12},{5,21},{6,14},{7,23},{8,24},{9,1... | collective-permute-start | bytes 5111816 | tf_op jit(solution)/shard_map/ppermute | solution.py:492
  7.2 1.3 %collective-permute-start = (f32[136,128]{1,0:T(8,128)S(1)}, f32[136,128]{1,0:T(8,128)S(1)}, u32[]{:S(2)}, u32[]{:S(2)}) collective-permute-start(f32[136,128]{1,0:T(8,128)S(1)} %get-tuple-element.39), channel_id=1, source_target_pairs={{0,1},{1,0},{2,3},{3,2},{4,5},{5,4},{6,7},{7,6},{8,9},{9,8},{10,11... | collective-permute-start | bytes 208904 | tf_op jit(solution)/shard_map/ppermute | solution.py:513
  8.6 6.5 %collective-permute-start.3 = (f32[136,128]{1,0:T(8,128)S(1)}, f32[136,128]{1,0:T(8,128)S(1)}, u32[]{:S(2)}, u32[]{:S(2)}) collective-permute-start(f32[136,128]{1,0:T(8,128)S(1)} %add.21), channel_id=1, source_target_pairs={{0,6},{1,7},{2,4},{3,5},{4,2},{5,3},{6,0},{7,1},{8,14},{9,15},{10,... | collective-permute-start | bytes 208904 | tf_op jit(solution)/shard_map/ppermute | solution.py:499
  12.3 6.2 %collective-permute-start.2 = (f32[136,128]{1,0:T(8,128)S(1)}, f32[136,128]{1,0:T(8,128)S(1)}, u32[]{:S(2)}, u32[]{:S(2)}) collective-permute-start(f32[136,128]{1,0:T(8,128)S(1)} %add.21), channel_id=1, source_target_pairs={{0,4},{1,5},{2,6},{3,7},{4,0},{5,1},{6,2},{7,3},{8,12},{9,13},{10,... | collective-permute-start | bytes 208904 | tf_op jit(solution)/shard_map/ppermute | solution.py:499
  12.3 6.2 %collective-permute-start.1 = (f32[136,128]{1,0:T(8,128)S(1)}, f32[136,128]{1,0:T(8,128)S(1)}, u32[]{:S(2)}, u32[]{:S(2)}) collective-permute-start(f32[136,128]{1,0:T(8,128)S(1)} %add.21), channel_id=1, source_target_pairs={{0,2},{1,3},{2,0},{3,1},{4,6},{5,7},{6,4},{7,5},{8,10},{9,11},{10,... | collective-permute-start | bytes 208904 | tf_op jit(solution)/shard_map/ppermute | solution.py:499
  18.5 1.3 %collective-permute-start.4 = (f32[136,128]{1,0:T(8,128)S(1)}, f32[136,128]{1,0:T(8,128)S(1)}, u32[]{:S(2)}, u32[]{:S(2)}) collective-permute-start(f32[136,128]{1,0:T(8,128)S(1)} %add_add_fusion.mine_ref), channel_id=1, source_target_pairs={{0,1},{1,0},{2,3},{3,2},{4,5},{5,4},{6,7},{7,6},{8,9},{9,8},{10,11... | collective-permute-start | bytes 208904 | tf_op jit(solution)/shard_map/ppermute | solution.py:514
  23.3 10.6 %collective-permute-start.7 = (f32[1280,128]{1,0:T(8,128)S(1)}, f32[1280,128]{1,0:T(8,128)S(1)}, u32[]{:S(2)}, u32[]{:S(2)}) collective-permute-start(f32[1280,128]{1,0:T(8,128)S(1)} %small_part.1.refs_0_), channel_id=1, source_target_pairs={{0,8},{1,17},{2,10},{3,19},{4,12},{5,21},{6,14},{7,23},{8,24},{9,1... | collective-permute-start | bytes 1966088 | tf_op jit(solution)/shard_map/ppermute | solution.py:492
  25.9 12.9 %collective-permute-start.6 = (f32[896,128]{1,0:T(8,128)S(1)}, f32[896,128]{1,0:T(8,128)S(1)}, u32[]{:S(2)}, u32[]{:S(2)}) collective-permute-start(f32[896,128]{1,0:T(8,128)S(1)} %get-tuple-element.47.refs_1_), channel_id=1, source_target_pairs={{0,8},{1,17},{2,10},{3,19},{4,12},{5,21},{6,14},{7,23},{8,24},{9,1... | collective-permute-start | bytes 1376264 | tf_op jit(solution)/shard_map/ppermute | solution.py:492
  27.3 16.2 %collective-permute-start.9 = (f32[640,128]{1,0:T(8,128)S(1)}, f32[640,128]{1,0:T(8,128)S(1)}, u32[]{:S(2)}, u32[]{:S(2)}) collective-permute-start(f32[640,128]{1,0:T(8,128)S(1)} %get-tuple-element.48.refs_2_), channel_id=1, source_target_pairs={{0,8},{1,17},{2,10},{3,19},{4,12},{5,21},{6,14},{7,23},{8,24},{9,1... | collective-permute-start | bytes 983048 | tf_op jit(solution)/shard_map/ppermute | solution.py:492
  39.2 24.0 %collective-permute-start.17 = (f32[3584,128]{1,0:T(8,128)S(1)}, f32[3584,128]{1,0:T(8,128)S(1)}, u32[]{:S(2)}, u32[]{:S(2)}) collective-permute-start(f32[3584,128]{1,0:T(8,128)S(1)} %get-tuple-element.62.bulk_ref), channel_id=1, source_target_pairs={{0,16},{1,9},{2,18},{3,11},{4,20},{5,13},{6,22},{7,15},{8,0},{9,25... | collective-permute-start | bytes 5505032 | tf_op jit(solution)/shard_map/ppermute | solution.py:492
  43.8 5.8 %collective-permute-start.13 = (f32[128,128]{1,0:T(8,128)S(1)}, f32[128,128]{1,0:T(8,128)S(1)}, u32[]{:S(2)}, u32[]{:S(2)}) collective-permute-start(f32[128,128]{1,0:T(8,128)S(1)} %get-tuple-element.61), channel_id=1, source_target_pairs={{0,7},{1,6},{2,5},{3,4},{4,3},{5,2},{6,1},{7,0},{8,15},{9,14},{10,... | collective-permute-start | bytes 196616 | tf_op jit(solution)/shard_map/ppermute | solution.py:499
  44.1 8.1 %collective-permute-start.12 = (f32[128,128]{1,0:T(8,128)S(1)}, f32[128,128]{1,0:T(8,128)S(1)}, u32[]{:S(2)}, u32[]{:S(2)}) collective-permute-start(f32[128,128]{1,0:T(8,128)S(1)} %get-tuple-element.61), channel_id=1, source_target_pairs={{0,5},{1,4},{2,7},{3,6},{4,1},{5,0},{6,3},{7,2},{8,13},{9,12},{10,... | collective-permute-start | bytes 196616 | tf_op jit(solution)/shard_map/ppermute | solution.py:499
  46.1 6.1 %collective-permute-start.11 = (f32[128,128]{1,0:T(8,128)S(1)}, f32[128,128]{1,0:T(8,128)S(1)}, u32[]{:S(2)}, u32[]{:S(2)}) collective-permute-start(f32[128,128]{1,0:T(8,128)S(1)} %get-tuple-element.61), channel_id=1, source_target_pairs={{0,3},{1,2},{2,1},{3,0},{4,7},{5,6},{6,5},{7,4},{8,11},{9,10},{10,... | collective-permute-start | bytes 196616 | tf_op jit(solution)/shard_map/ppermute | solution.py:499
  46.7 5.5 %collective-permute-start.10 = (f32[128,128]{1,0:T(8,128)S(1)}, f32[128,128]{1,0:T(8,128)S(1)}, u32[]{:S(2)}, u32[]{:S(2)}) collective-permute-start(f32[128,128]{1,0:T(8,128)S(1)} %get-tuple-element.61), channel_id=1, source_target_pairs={{0,1},{1,0},{2,3},{3,2},{4,5},{5,4},{6,7},{7,6},{8,9},{9,8},{10,11... | collective-permute-start | bytes 196616 | tf_op jit(solution)/shard_map/ppermute | solution.py:499
  52.3 5.1 %collective-permute-start.15 = (f32[128,128]{1,0:T(8,128)S(1)}, f32[128,128]{1,0:T(8,128)S(1)}, u32[]{:S(2)}, u32[]{:S(2)}) collective-permute-start(f32[128,128]{1,0:T(8,128)S(1)} %add_add_fusion.1), channel_id=1, source_target_pairs={{0,8},{1,17},{2,10},{3,19},{4,12},{5,21},{6,14},{7,23},{8,24},{9,1... | collective-permute-start | bytes 196616 | tf_op jit(solution)/shard_map/ppermute | solution.py:492
  53.9 3.5 %collective-permute-start.14 = (f32[128,128]{1,0:T(8,128)S(1)}, f32[128,128]{1,0:T(8,128)S(1)}, u32[]{:S(2)}, u32[]{:S(2)}) collective-permute-start(f32[128,128]{1,0:T(8,128)S(1)} %add_add_fusion.1), channel_id=1, source_target_pairs={{0,1},{1,0},{2,3},{3,2},{4,5},{5,4},{6,7},{7,6},{8,9},{9,8},{10,11... | collective-permute-start | bytes 196616 | tf_op jit(solution)/shard_map/ppermute | solution.py:537
  53.9 12.2 %collective-permute-start.8 = (f32[512,128]{1,0:T(8,128)S(1)}, f32[512,128]{1,0:T(8,128)S(1)}, u32[]{:S(2)}, u32[]{:S(2)}) collective-permute-start(f32[512,128]{1,0:T(8,128)S(1)} %get-tuple-element.58.tail_ref), channel_id=1, source_target_pairs={{0,16},{1,9},{2,18},{3,11},{4,20},{5,13},{6,22},{7,15},{8,0},{9,25... | collective-permute-start | bytes 786440 | tf_op jit(solution)/shard_map/ppermute | solution.py:492
  60.3 2.1 %collective-permute-start.16 = (f32[256,128]{1,0:T(8,128)S(1)}, f32[256,128]{1,0:T(8,128)S(1)}, u32[]{:S(2)}, u32[]{:S(2)}) collective-permute-start(f32[256,128]{1,0:T(8,128)S(1)} %second_rotation.1.refs_6_), channel_id=1, source_target_pairs={{0,1},{1,0},{2,3},{3,2},{4,5},{5,4},{6,7},{7,6},{8,9},{9,8},{10,11... | collective-permute-start | bytes 393224 | tf_op jit(solution)/shard_map/ppermute | solution.py:539

commit v5 on v4

--- a/solution.py
+++ b/solution.py
@@ -13,11 +13,12 @@
 SCOPED = 16 * 1024 * 1024
 WHOLE = 54 * 1024 * 1024
 
-RAW = 13
-SMALL = 8
+RAW = 14
+SMALL = 7
 LAST = 4
 BULK = 28
 STEP = 4
+SHARE = 3
 
 
 def after(p, n):
@@ -278,18 +279,37 @@
     return call(kernel, [half, half, ((2 * width, 2 * width), HERE)], [(mine, HERE), (other, HERE)], "first_rotation")
 
 
-def small_part(high, turn, small, step):
+def share_of():
+    return lax.rem(lax.div(lax.axis_index("row"), 2), 2)
+
+
+def rotated_gram(gram, turn):
+    return rows_product(turn.T, right_parts(rows_product(gram, right_parts(turn))))
+
+
+def small_part(high, turn, gram, small, step):
     width = turn.shape[1]
-
-    def kernel(high_ref, turn_ref, out_ref):
+    turn_share, gram_share = width, width // 2
+
+    def kernel(high_ref, turn_ref, gram_ref, out_ref, square_ref):
+        place = share_of()
         local = Rows((high_ref, 0, high.shape[1], 0))
-        out_ref[: 2 * width] = turn_ref[...]
         parts = right_parts(turn_ref[...])
         for start, number in spans(0, small, step):
-            out_ref[pl.ds(2 * width + start, number), :] = rows_product(local.pair(start, number), parts)
-
-    return call(
-        kernel, [((2 * width + small, width), HERE)], [(high, HERE), (turn, HERE)], "small_part", 12 * small * width * width
+            out_ref[pl.ds(SHARE * width // 2 + start, number), :] = rows_product(local.pair(start, number), parts)
+        square_ref[...] = rotated_gram(gram_ref[...], turn_ref[...])
+        out_ref[:turn_share] = turn_ref[pl.ds(pl.multiple_of(place * turn_share, turn_share), turn_share), :]
+        out_ref[turn_share : turn_share + gram_share] = square_ref[
+            pl.ds(pl.multiple_of(place * gram_share, gram_share), gram_share), :
+        ]
+
+    return call(
+        kernel,
+        [((SHARE * width // 2 + small, width), HERE)],
+        [(high, HERE), (turn, HERE), (gram, HERE)],
+        "small_part",
+        12 * small * width * width,
+        [pltpu.VMEM((width, width), F32)],
     )[0]
 
 
@@ -304,14 +324,11 @@
         for start, number in spans(small, count, step, count - last):
             ref, place = out.at(start, number)
             ref[place, :] = rows_product(local.pair(start, number), parts)
-        gram = gram_ref[...]
-        for turn_ref, place in ((first_ref, last_ref.at[pl.ds(last, width), :]), (second_ref, second_gram_ref)):
-            turn = turn_ref[...]
-            place[...] = rows_product(turn.T, right_parts(rows_product(gram, right_parts(turn))))
-
-    return call(
-        kernel,
-        [((count - small - last, width), HERE), ((last + width, width), HERE), ((width, width), HERE)],
+        second_gram_ref[...] = rotated_gram(gram_ref[...], second_ref[...])
+
+    return call(
+        kernel,
+        [((count - small - last, width), HERE), ((last, width), HERE), ((width, width), HERE)],
         [(high, HERE), (first, HERE), (second, HERE), (gram, HERE)],
         "sent_parts",
         12 * count * width * width,
@@ -360,15 +377,24 @@
     return (total[:width, :width] + total[:width, width:]) + (total[width:, :width] + total[width:, width:])
 
 
-def raw_cross(far_raw, far_small, bulk, tail, step):
+def raw_cross(far_raw, far_small, share, bulk, tail, step):
     width = bulk.shape[1]
-    early, small = far_raw.shape[1], far_small.shape[0] - 2 * width
-
-    def kernel(raw_ref, small_ref, bulk_ref, tail_ref, high_ref, low_ref, out_ref):
+    offset = SHARE * width // 2
+    early, small = far_raw.shape[1], far_small.shape[0] - offset
+    turn_share, gram_share = width, width // 2
+
+    def kernel(
+        raw_ref, small_ref, share_ref, bulk_ref, tail_ref, high_ref, low_ref, gram_ref, out_ref, turn_ref
+    ):
+        for place, ref in ((share_of(), small_ref), (1 - share_of(), share_ref)):
+            turn_ref[pl.ds(pl.multiple_of(place * turn_share, turn_share), turn_share), :] = ref[:turn_share]
+            gram_ref[pl.ds(pl.multiple_of(place * gram_share, gram_share), gram_share), :] = ref[
+                turn_share : turn_share + gram_share
+            ]
         own = Rows.of((bulk_ref, tail_ref), (bulk.shape[0], tail.shape[0]))
         raw = Rows((raw_ref, 0, early, 0))
-        far = Rows((small_ref, early, small, 2 * width))
-        parts = right_parts(small_ref[: 2 * width])
+        far = Rows((small_ref, early, small, offset))
+        parts = right_parts(turn_ref[...])
         total = jnp.zeros((2 * width, 2 * width), F32)
         for start, count in spans(0, early + small, step, early, bulk.shape[0]):
             block = rows_product(raw.pair(start, count), parts) if start < early else far.get(start, count)
@@ -380,10 +406,11 @@
 
     return call(
         kernel,
-        [((early + small, 2 * width), HERE, BF16)] * 2 + [((width, width), HERE)],
-        [(far_raw, HERE), (far_small, HERE), (bulk, HERE), (tail, HERE)],
+        [((early + small, 2 * width), HERE, BF16)] * 2 + [((width, width), HERE)] * 2,
+        [(part, HERE) for part in (far_raw, far_small, share, bulk, tail)],
         "raw_cross",
         12 * (early + small) * width * width,
+        [pltpu.VMEM((2 * width, width), F32)],
     )
 
 
@@ -410,9 +437,8 @@
     )
 
 
-def second_rotation(own_gram, far_sent, here, there):
+def second_rotation(own_gram, far_gram, here, there):
     width = here.shape[1]
-    place = far_sent.shape[0] - width
 
     def kernel(own_gram_ref, far_ref, here_ref, there_ref, out_ref):
         p, n = lax.axis_index("pair"), lax.axis_size("pair")
@@ -422,14 +448,14 @@
         own_upper = (outward & own_upper_out) | (jnp.logical_not(outward) & jnp.logical_not(odd))
         sign = jnp.where(own_upper, 1.0, -1.0).astype(F32)
         cross = here_ref[...] + there_ref[...].T
-        _, first, left, right = rotation_of(own_gram_ref[...], cross, far_ref[pl.ds(place, width), :], sign)
+        _, first, left, right = rotation_of(own_gram_ref[...], cross, far_ref[...], sign)
         keeps_own = (outward & (p == 0)) | (jnp.logical_not(outward) & (p == 1))
         out_ref[...] = rows_product(first, right_parts(jnp.where(keeps_own, left, right)))
 
     return call(
         kernel,
         [((2 * width, width), HERE)],
-        [(own_gram, HERE), (far_sent, HERE), (here, HERE), (there, HERE)],
+        [(own_gram, HERE), (far_gram, HERE), (here, HERE), (there, HERE)],
         "second_rotation",
         LONG,
     )[0]
@@ -476,6 +502,7 @@
     unit = rows // 32
     early, small, last, bulk, step = (part * unit for part in (RAW, SMALL, LAST, BULK, STEP))
     main = rows - early - small - last
+    offset = SHARE * width // 2
     flat = [(p, r) for p in range(pairs_count) for r in range(rows_count)]
     ahead = {p: after(p, pairs_count) for p in range(pairs_count)}
     behind = {q: p for p, q in ahead.items()}
@@ -514,28 +541,30 @@
     other = lax.ppermute(mine, "row", core)
     turn_first, turn_second, gram = first_rotation(mine, other)
 
-    sent_small = small_part(high, turn_first, small, step)
+    sent_small = small_part(high, turn_first, gram, small, step)
     far_small = travel(sent_small, outward)
     turn_main, sent_small, far_raw = lax.optimization_barrier((turn_first, sent_small, far_raw))
     sent_main, sent_last, second_gram = sent_parts(high, turn_main, turn_second, gram, small, last, step)
     far_main, far_last = travel(sent_main, outward), travel(sent_last, outward)
     turn_second, sent_main = lax.optimization_barrier((turn_second, sent_main))
-    sent = [(sent_small, early, small, 2 * width), (sent_main, early + small, main, 0), (sent_last, rows - last, last, 0)]
+    sent = [(sent_small, early, small, offset), (sent_main, early + small, main, 0), (sent_last, rows - last, last, 0)]
     second_bulk, second_tail, *first_halves = rest_parts(low, high, turn_first, turn_second, sent, bulk, step)
 
-    *raw_halves, cross = raw_cross(far_raw, far_small, second_bulk, second_tail, step)
+    far_small, second_bulk = lax.optimization_barrier((far_small, second_bulk))
+    share = lax.ppermute(far_small[:offset], "row", [(r, r ^ 2) for r in range(rows_count)])
+    share, later_bulk, later_tail = lax.optimization_barrier((share, second_bulk, second_tail))
+    *raw_halves, far_gram, cross = raw_cross(far_raw, far_small, share, second_bulk, second_tail, step)
     far_main, cross = lax.optimization_barrier((far_main, cross))
     *main_halves, cross = more_cross(
         far_main, early + small, main, second_bulk, second_tail, cross, step, "main_cross"
     )
-    cross, later_bulk, later_tail = lax.optimization_barrier((cross, second_bulk, second_tail))
     far_bulk, far_tail = travel(later_bulk, inward), travel(later_tail, inward)
     *last_halves, cross = more_cross(far_last, rows - last, last, second_bulk, second_tail, cross, step, "last_cross")
 
     total = other_sum(cross)
     there = travel(total, outward)
     here = lax.ppermute(total, "row", core)
-    turn_here = second_rotation(second_gram, far_last, here, there)
+    turn_here = second_rotation(second_gram, far_gram, here, there)
     turn_there = lax.ppermute(turn_here, "row", core)
 
     sizes = early + small, main, last

time: 67.3 us -> 65.8 us (0.978)
  waiting for transfers between devices: 26.8 us -> 22.4 us
  starting transfers between devices: 19.4 us -> 22.3 us
    ppermute x7, waiting for transfers between devices: 14.8 us -> 8.27 us  [travel(): return lax.ppermute(block, ('pair', 'row'), moves)]
    ppermute x0 -> x1, waiting for transfers between devices: none -> 2.03 us  [body(): lax.ppermute(far_small[:offset], 'row', [(r, r ^ 2) for r in range(rows_c...]
    ppermute x7, starting transfers between devices: 10.5 us -> 12.2 us  [travel(): return lax.ppermute(block, ('pair', 'row'), moves)]
    ppermute x0 -> x1, starting transfers between devices: none -> 1.14 us  [body(): lax.ppermute(far_small[:offset], 'row', [(r, r ^ 2) for r in range(rows_c...]
  transfers between devices with their start and end apart: 18 -> 19, of which waited for: 12 -> 12; matrix products, arithmetic and copies ran while one was open for 0% -> 0% of each run, Pallas kernels for 27% -> 28%
where the time goes in v5:
time: 65.8 us; the launch traced here: 65.7 us
  waiting for transfers between devices  22.4 us (34%)
  starting transfers between devices  22.3 us (34%)
  Pallas kernels  20.6 us (31%)
    pallas_call x13, Pallas kernels, call(): pl.pallas_call(kernel, in_specs=[pl.BlockSpec(memory_space=place) for pla...  20.6 us
    ppermute x7, starting transfers between devices, travel(): return lax.ppermute(block, ('pair', 'row'), moves)  12.2 us
    ppermute x7, waiting for transfers between devices, chip_sum(): lax.ppermute(block, 'row', [(r, r ^ d) for r in range(rows_count)])  9.62 us
    ppermute x7, starting transfers between devices, chip_sum(): lax.ppermute(block, 'row', [(r, r ^ d) for r in range(rows_count)])  8.73 us
    ppermute x7, waiting for transfers between devices, travel(): return lax.ppermute(block, ('pair', 'row'), moves)  8.27 us
    ppermute x1, waiting for transfers between devices, body(): lax.ppermute(far_small[:offset], 'row', [(r, r ^ 2) for r in range(rows_c...  2.03 us
  transfers between devices with their start and end apart: 19, of which 12 were waited for; matrix products, arithmetic and copies ran while one was open for 0% of the time, Pallas kernels for 28%

profile of v5, /device:TPU:0, one launch (start us, length us, event | category | flops | bytes accessed | tf_op | source)
XLA Modules:
  0.0 65.7 jit_solution(1719877157814323963)
XLA Ops:
  0.0 1.5 %raw_rows.1.low_ref = f32[2,1792,128]{2,1,0:T(8,128)S(1)} custom-call(f32[2,4096,128]{2,1,0:T(8,128)} %matrix_ref.3), custom_call_target="tpu_custom_call" | custom-call | tf_op jit(solution)/shard_map/raw_rows/pallas_call | solution.py:140
  1.5 3.0 %collective-permute-start.5 = (f32[2,1792,128]{2,1,0:T(8,128)S(1)}, f32[2,1792,128]{2,1,0:T(8,128)S(1)}, u32[]{:S(2)}, u32[]{:S(2)}) collective-permute-start(f32[2,1792,128]{2,1,0:T(8,128)S(1)} %raw_rows.1.low_ref), channel_id=1, source_target_pairs={{0,8},{1,17},{2,10},{3,19},{4,12},{5,21},{6,14},{7,23},{8,24},{9,1... | collective-permute-start | bytes 5505032 | tf_op jit(solution)/shard_map/ppermute | solution.py:519
  4.5 2.7 %gram.1 = (f32[2,2304,128]{2,1,0:T(8,128)S(1)}, f32[136,128]{1,0:T(8,128)S(1)}, f32[136,128]{1,0:T(8,128)S(1)}) custom-call(f32[2,4096,128]{2,1,0:T(8,128)} %matrix_ref.3, f32[2,1792,128]{2,1,0:T(8,128)S(1)} %raw_rows.1.low_ref), custom_call_target="tpu_custom_call" | custom-call | tf_op jit(solution)/shard_map/gram/pallas_call | solution.py:140
  7.3 1.2 %collective-permute-done = f32[136,128]{1,0:T(8,128)S(1)} collective-permute-done((f32[136,128]{1,0:T(8,128)S(1)}, f32[136,128]{1,0:T(8,128)S(1)}, u32[]{:S(2)}, u32[]{:S(2)}) %collective-permute-start) | collective-permute-done | bytes 69664 | tf_op jit(solution)/shard_map/ppermute | solution.py:540
  8.6 3.7 %collective-permute-start.3 = (f32[136,128]{1,0:T(8,128)S(1)}, f32[136,128]{1,0:T(8,128)S(1)}, u32[]{:S(2)}, u32[]{:S(2)}) collective-permute-start(f32[136,128]{1,0:T(8,128)S(1)} %add.21), channel_id=1, source_target_pairs={{0,6},{1,7},{2,4},{3,5},{4,2},{5,3},{6,0},{7,1},{8,14},{9,15},{10,... | collective-permute-start | bytes 208904 | tf_op jit(solution)/shard_map/ppermute | solution.py:526
  13.0 2.1 %collective-permute-done.3 = f32[136,128]{1,0:T(8,128)S(1)} collective-permute-done((f32[136,128]{1,0:T(8,128)S(1)}, f32[136,128]{1,0:T(8,128)S(1)}, u32[]{:S(2)}, u32[]{:S(2)}) %collective-permute-start.3) | collective-permute-done | bytes 69664 | tf_op jit(solution)/shard_map/ppermute | solution.py:526
  15.1 3.3 %collective-permute-done.2 = f32[136,128]{1,0:T(8,128)S(1)} collective-permute-done((f32[136,128]{1,0:T(8,128)S(1)}, f32[136,128]{1,0:T(8,128)S(1)}, u32[]{:S(2)}, u32[]{:S(2)}) %collective-permute-start.2) | collective-permute-done | bytes 69664 | tf_op jit(solution)/shard_map/ppermute | solution.py:526
  18.5 1.2 %collective-permute-done.4.other_ref = f32[136,128]{1,0:T(8,128)S(1)} collective-permute-done((f32[136,128]{1,0:T(8,128)S(1)}, f32[136,128]{1,0:T(8,128)S(1)}, u32[]{:S(2)}, u32[]{:S(2)}) %collective-permute-start.4) | collective-permute-done | bytes 69664 | tf_op jit(solution)/shard_map/ppermute | solution.py:541
  19.8 3.1 %first_rotation.1 = (f32[256,128]{1,0:T(8,128)S(1)}, f32[256,128]{1,0:T(8,128)S(1)}, f32[256,256]{1,0:T(8,128)S(1)}) custom-call(f32[136,128]{1,0:T(8,128)S(1)} %add_add_fusion.mine_ref, f32[136,128]{1,0:T(8,128)S(1)} %collective-permute-done.4.other_ref), custom_call_target="tpu_custom_call" | custom-call | tf_op jit(solution)/shard_map/first_rotation/pallas_call | solution.py:140
  23.5 1.6 %collective-permute-start.6 = (f32[1088,128]{1,0:T(8,128)S(1)}, f32[1088,128]{1,0:T(8,128)S(1)}, u32[]{:S(2)}, u32[]{:S(2)}) collective-permute-start(f32[1088,128]{1,0:T(8,128)S(1)} %small_part.1.refs_0_), channel_id=1, source_target_pairs={{0,8},{1,17},{2,10},{3,19},{4,12},{5,21},{6,14},{7,23},{8,24},{9,1... | collective-permute-start | bytes 1671176 | tf_op jit(solution)/shard_map/ppermute | solution.py:519
  26.5 2.0 %collective-permute-start.10 = (f32[896,128]{1,0:T(8,128)S(1)}, f32[896,128]{1,0:T(8,128)S(1)}, u32[]{:S(2)}, u32[]{:S(2)}) collective-permute-start(f32[896,128]{1,0:T(8,128)S(1)} %get-tuple-element.50.refs_1_), channel_id=1, source_target_pairs={{0,8},{1,17},{2,10},{3,19},{4,12},{5,21},{6,14},{7,23},{8,24},{9,1... | collective-permute-start | bytes 1376264 | tf_op jit(solution)/shard_map/ppermute | solution.py:519
  28.5 1.9 %rest_parts.1 = (f32[3584,128]{1,0:T(8,128)S(1)}, f32[512,128]{1,0:T(8,128)S(1)}, bf16[4096,128]{1,0:T(8,128)(2,1)S(1)}, bf16[4096,128]{1,0:T(8,128)(2,1)S(1)}) custom-call(f32[2,1792,128]{2,1,0:T(8,128)S(1)} %raw_rows.1.low_ref, f32[2,2304,128]{2,1,0:T(8,128)S(1)} %get-tuple-element.40.high_ref, f32[256,128]{1,0:T(8,128)S(1)} %get-tuple-element.46.turn_ref.first_ref, ...), custom_call_target="tpu_custom_call" | custom-call | tf_op jit(solution)/shard_map/rest_parts/pallas_call | solution.py:140
  30.4 2.6 %collective-permute-done.6.small_ref = f32[1088,128]{1,0:T(8,128)S(1)} collective-permute-done((f32[1088,128]{1,0:T(8,128)S(1)}, f32[1088,128]{1,0:T(8,128)S(1)}, u32[]{:S(2)}, u32[]{:S(2)}) %collective-permute-start.6) | collective-permute-done | bytes 557088 | tf_op jit(solution)/shard_map/ppermute | solution.py:519
  33.1 1.1 %collective-permute-start.7 = (f32[192,128]{1,0:T(8,128)S(1)}, f32[192,128]{1,0:T(8,128)S(1)}, u32[]{:S(2)}, u32[]{:S(2)}) collective-permute-start(f32[192,128]{1,0:T(8,128)S(1)} %slice.3), channel_id=1, source_target_pairs={{0,2},{1,3},{2,0},{3,1},{4,6},{5,7},{6,4},{7,5},{8,10},{9,11},{10,... | collective-permute-start | bytes 294920 | tf_op jit(solution)/shard_map/ppermute | solution.py:554
  34.2 1.5 %collective-permute-start.9 = (f32[512,128]{1,0:T(8,128)S(1)}, f32[512,128]{1,0:T(8,128)S(1)}, u32[]{:S(2)}, u32[]{:S(2)}) collective-permute-start(f32[512,128]{1,0:T(8,128)S(1)} %get-tuple-element.51.refs_2_), channel_id=1, source_target_pairs={{0,8},{1,17},{2,10},{3,19},{4,12},{5,21},{6,14},{7,23},{8,24},{9,1... | collective-permute-start | bytes 786440 | tf_op jit(solution)/shard_map/ppermute | solution.py:519
  35.7 2.0 %collective-permute-done.7.share_ref = f32[192,128]{1,0:T(8,128)S(1)} collective-permute-done((f32[192,128]{1,0:T(8,128)S(1)}, f32[192,128]{1,0:T(8,128)S(1)}, u32[]{:S(2)}, u32[]{:S(2)}) %collective-permute-start.7) | collective-permute-done | bytes 98336 | tf_op jit(solution)/shard_map/ppermute | solution.py:554
  37.8 0.9 %collective-permute-start.18 = (f32[3584,128]{1,0:T(8,128)S(1)}, f32[3584,128]{1,0:T(8,128)S(1)}, u32[]{:S(2)}, u32[]{:S(2)}) collective-permute-start(f32[3584,128]{1,0:T(8,128)S(1)} %get-tuple-element.68.bulk_ref), channel_id=1, source_target_pairs={{0,16},{1,9},{2,18},{3,11},{4,20},{5,13},{6,22},{7,15},{8,0},{9,25... | collective-permute-start | bytes 5505032 | tf_op jit(solution)/shard_map/ppermute | solution.py:519
  38.6 1.5 %raw_cross.1 = (bf16[2688,256]{1,0:T(8,128)(2,1)S(1)}, bf16[2688,256]{1,0:T(8,128)(2,1)S(1)}, f32[128,128]{1,0:T(8,128)S(1)}, f32[128,128]{1,0:T(8,128)S(1)}) custom-call(f32[2,1792,128]{2,1,0:T(8,128)S(1)} %collective-permute-done.5.raw_ref, f32[1088,128]{1,0:T(8,128)S(1)} %collective-permute-done.6.small_ref, ...), custom_call_target="tpu_custom_call" | custom-call | tf_op jit(solution)/shard_map/raw_cross/pallas_call | solution.py:140
  40.5 2.2 %collective-permute-done.9.far_ref = f32[512,128]{1,0:T(8,128)S(1)} collective-permute-done((f32[512,128]{1,0:T(8,128)S(1)}, f32[512,128]{1,0:T(8,128)S(1)}, u32[]{:S(2)}, u32[]{:S(2)}) %collective-permute-start.9) | collective-permute-done | bytes 262176 | tf_op jit(solution)/shard_map/ppermute | solution.py:519
  43.1 2.2 %collective-permute-start.13 = (f32[128,128]{1,0:T(8,128)S(1)}, f32[128,128]{1,0:T(8,128)S(1)}, u32[]{:S(2)}, u32[]{:S(2)}) collective-permute-start(f32[128,128]{1,0:T(8,128)S(1)} %get-tuple-element.67), channel_id=1, source_target_pairs={{0,5},{1,4},{2,7},{3,6},{4,1},{5,0},{6,3},{7,2},{8,13},{9,12},{10,... | collective-permute-start | bytes 196616 | tf_op jit(solution)/shard_map/ppermute | solution.py:526
  45.3 1.0 %collective-permute-start.12 = (f32[128,128]{1,0:T(8,128)S(1)}, f32[128,128]{1,0:T(8,128)S(1)}, u32[]{:S(2)}, u32[]{:S(2)}) collective-permute-start(f32[128,128]{1,0:T(8,128)S(1)} %get-tuple-element.67), channel_id=1, source_target_pairs={{0,3},{1,2},{2,1},{3,0},{4,7},{5,6},{6,5},{7,4},{8,11},{9,10},{10,... | collective-permute-start | bytes 196616 | tf_op jit(solution)/shard_map/ppermute | solution.py:526
  46.4 0.9 %collective-permute-start.11 = (f32[128,128]{1,0:T(8,128)S(1)}, f32[128,128]{1,0:T(8,128)S(1)}, u32[]{:S(2)}, u32[]{:S(2)}) collective-permute-start(f32[128,128]{1,0:T(8,128)S(1)} %get-tuple-element.67), channel_id=1, source_target_pairs={{0,1},{1,0},{2,3},{3,2},{4,5},{5,4},{6,7},{7,6},{8,9},{9,8},{10,11... | collective-permute-start | bytes 196616 | tf_op jit(solution)/shard_map/ppermute | solution.py:526
  47.3 1.8 %collective-permute-done.14 = f32[128,128]{1,0:T(8,128)S(1)} collective-permute-done((f32[128,128]{1,0:T(8,128)S(1)}, f32[128,128]{1,0:T(8,128)S(1)}, u32[]{:S(2)}, u32[]{:S(2)}) %collective-permute-start.14) | collective-permute-done | bytes 65568 | tf_op jit(solution)/shard_map/ppermute | solution.py:526
  49.1 2.4 %collective-permute-done.13 = f32[128,128]{1,0:T(8,128)S(1)} collective-permute-done((f32[128,128]{1,0:T(8,128)S(1)}, f32[128,128]{1,0:T(8,128)S(1)}, u32[]{:S(2)}, u32[]{:S(2)}) %collective-permute-start.13) | collective-permute-done | bytes 65568 | tf_op jit(solution)/shard_map/ppermute | solution.py:526
  51.5 1.6 %collective-permute-start.16 = (f32[128,128]{1,0:T(8,128)S(1)}, f32[128,128]{1,0:T(8,128)S(1)}, u32[]{:S(2)}, u32[]{:S(2)}) collective-permute-start(f32[128,128]{1,0:T(8,128)S(1)} %add_add_fusion.1), channel_id=1, source_target_pairs={{0,8},{1,17},{2,10},{3,19},{4,12},{5,21},{6,14},{7,23},{8,24},{9,1... | collective-permute-start | bytes 196616 | tf_op jit(solution)/shard_map/ppermute | solution.py:519
  53.1 1.6 %collective-permute-start.8 = (f32[512,128]{1,0:T(8,128)S(1)}, f32[512,128]{1,0:T(8,128)S(1)}, u32[]{:S(2)}, u32[]{:S(2)}) collective-permute-start(f32[512,128]{1,0:T(8,128)S(1)} %get-tuple-element.58.tail_ref), channel_id=1, source_target_pairs={{0,16},{1,9},{2,18},{3,11},{4,20},{5,13},{6,22},{7,15},{8,0},{9,25... | collective-permute-start | bytes 786440 | tf_op jit(solution)/shard_map/ppermute | solution.py:519
  54.7 1.9 %collective-permute-done.16.there_ref = f32[128,128]{1,0:T(8,128)S(1)} collective-permute-done((f32[128,128]{1,0:T(8,128)S(1)}, f32[128,128]{1,0:T(8,128)S(1)}, u32[]{:S(2)}, u32[]{:S(2)}) %collective-permute-start.16) | collective-permute-done | bytes 65568 | tf_op jit(solution)/shard_map/ppermute | solution.py:519
  56.6 2.9 %second_rotation.1.refs_6_ = f32[256,128]{1,0:T(8,128)S(1)} custom-call(f32[128,128]{1,0:T(8,128)S(1)} %get-tuple-element.59.own_gram_ref, f32[128,128]{1,0:T(8,128)S(1)} %get-tuple-element.62.far_ref, f32[128,128]{1,0:T(8,128)S(1)} %collective-permute-done.15.here_ref, f32[128,128]{1,0:T(8,128)S(1)} %collective-permute-done.16.there_ref), custom_call_target="tpu_custom_call" | custom-call | flops 11500000256 | tf_op jit(solution)/shard_map/second_rotation/pallas_call | solution.py:140
  59.6 2.0 %here_product.1.refs_5_ = f32[2,4096,128]{2,1,0:T(8,128)} custom-call(bf16[2688,256]{1,0:T(8,128)(2,1)S(1)} %get-tuple-element.69.refs_0_, bf16[2688,256]{1,0:T(8,128)(2,1)S(1)} %get-tuple-element.70.refs_1_, bf16[896,256]{1,0:T(8,128)(2,1)S(1)} %get-tuple-element.71.refs_2_, bf16[896,256]{1,0:T(8,128)(2,1)S(1)} %get-tuple-element.72.refs_3_, ...), custom_call_target="tpu_custom_call" | custom-call | tf_op jit(solution)/shard_map/here_product/pallas_call | solution.py:140
  61.7 1.9 %bulk_product.1.refs_4_ = f32[2,4096,128]{2,1,0:T(8,128)} custom-call(bf16[4096,128]{1,0:T(8,128)(2,1)S(1)} %get-tuple-element.52.refs_0_, bf16[4096,128]{1,0:T(8,128)(2,1)S(1)} %get-tuple-element.53.refs_1_, f32[3584,128]{1,0:T(8,128)S(1)} %collective-permute-done.18.refs_2_.refs_3_, ...), custom_call_target="tpu_custom_call", output_to_operand_aliasing={{}: (5, {})} | custom-call | tf_op jit(solution)/shard_map/bulk_product/pallas_call | solution.py:140
  63.6 0.9 %collective-permute-done.8.refs_2_ = f32[512,128]{1,0:T(8,128)S(1)} collective-permute-done((f32[512,128]{1,0:T(8,128)S(1)}, f32[512,128]{1,0:T(8,128)S(1)}, u32[]{:S(2)}, u32[]{:S(2)}) %collective-permute-start.8) | collective-permute-done | bytes 262176 | tf_op jit(solution)/shard_map/ppermute | solution.py:519
  64.5 1.0 %tail_product.1 = f32[2,4096,128]{2,1,0:T(8,128)} custom-call(bf16[4096,128]{1,0:T(8,128)(2,1)S(1)} %get-tuple-element.52.refs_0_, bf16[4096,128]{1,0:T(8,128)(2,1)S(1)} %get-tuple-element.53.refs_1_, f32[512,128]{1,0:T(8,128)S(1)} %collective-permute-done.8.refs_2_, ...), custom_call_target="tpu_custom_call", output_to_operand_aliasing={{}: (4, {})} | custom-call | tf_op jit(solution)/shard_map/tail_product/pallas_call | solution.py:140
  (23 shorter events, 3.8 us)
Async XLA Ops:
  1.5 24.2 %collective-permute-start.5 = (f32[2,1792,128]{2,1,0:T(8,128)S(1)}, f32[2,1792,128]{2,1,0:T(8,128)S(1)}, u32[]{:S(2)}, u32[]{:S(2)}) collective-permute-start(f32[2,1792,128]{2,1,0:T(8,128)S(1)} %raw_rows.1.low_ref), channel_id=1, source_target_pairs={{0,8},{1,17},{2,10},{3,19},{4,12},{5,21},{6,14},{7,23},{8,24},{9,1... | collective-permute-start | bytes 5505032 | tf_op jit(solution)/shard_map/ppermute | solution.py:519
  7.2 1.3 %collective-permute-start = (f32[136,128]{1,0:T(8,128)S(1)}, f32[136,128]{1,0:T(8,128)S(1)}, u32[]{:S(2)}, u32[]{:S(2)}) collective-permute-start(f32[136,128]{1,0:T(8,128)S(1)} %get-tuple-element.42), channel_id=1, source_target_pairs={{0,1},{1,0},{2,3},{3,2},{4,5},{5,4},{6,7},{7,6},{8,9},{9,8},{10,11... | collective-permute-start | bytes 208904 | tf_op jit(solution)/shard_map/ppermute | solution.py:540
  8.6 6.5 %collective-permute-start.3 = (f32[136,128]{1,0:T(8,128)S(1)}, f32[136,128]{1,0:T(8,128)S(1)}, u32[]{:S(2)}, u32[]{:S(2)}) collective-permute-start(f32[136,128]{1,0:T(8,128)S(1)} %add.21), channel_id=1, source_target_pairs={{0,6},{1,7},{2,4},{3,5},{4,2},{5,3},{6,0},{7,1},{8,14},{9,15},{10,... | collective-permute-start | bytes 208904 | tf_op jit(solution)/shard_map/ppermute | solution.py:526
  12.2 6.2 %collective-permute-start.2 = (f32[136,128]{1,0:T(8,128)S(1)}, f32[136,128]{1,0:T(8,128)S(1)}, u32[]{:S(2)}, u32[]{:S(2)}) collective-permute-start(f32[136,128]{1,0:T(8,128)S(1)} %add.21), channel_id=1, source_target_pairs={{0,4},{1,5},{2,6},{3,7},{4,0},{5,1},{6,2},{7,3},{8,12},{9,13},{10,... | collective-permute-start | bytes 208904 | tf_op jit(solution)/shard_map/ppermute | solution.py:526
  12.2 6.2 %collective-permute-start.1 = (f32[136,128]{1,0:T(8,128)S(1)}, f32[136,128]{1,0:T(8,128)S(1)}, u32[]{:S(2)}, u32[]{:S(2)}) collective-permute-start(f32[136,128]{1,0:T(8,128)S(1)} %add.21), channel_id=1, source_target_pairs={{0,2},{1,3},{2,0},{3,1},{4,6},{5,7},{6,4},{7,5},{8,10},{9,11},{10,... | collective-permute-start | bytes 208904 | tf_op jit(solution)/shard_map/ppermute | solution.py:526
  18.4 1.3 %collective-permute-start.4 = (f32[136,128]{1,0:T(8,128)S(1)}, f32[136,128]{1,0:T(8,128)S(1)}, u32[]{:S(2)}, u32[]{:S(2)}) collective-permute-start(f32[136,128]{1,0:T(8,128)S(1)} %add_add_fusion.mine_ref), channel_id=1, source_target_pairs={{0,1},{1,0},{2,3},{3,2},{4,5},{5,4},{6,7},{7,6},{8,9},{9,8},{10,11... | collective-permute-start | bytes 208904 | tf_op jit(solution)/shard_map/ppermute | solution.py:541
  23.5 9.6 %collective-permute-start.6 = (f32[1088,128]{1,0:T(8,128)S(1)}, f32[1088,128]{1,0:T(8,128)S(1)}, u32[]{:S(2)}, u32[]{:S(2)}) collective-permute-start(f32[1088,128]{1,0:T(8,128)S(1)} %small_part.1.refs_0_), channel_id=1, source_target_pairs={{0,8},{1,17},{2,10},{3,19},{4,12},{5,21},{6,14},{7,23},{8,24},{9,1... | collective-permute-start | bytes 1671176 | tf_op jit(solution)/shard_map/ppermute | solution.py:519
  26.5 13.6 %collective-permute-start.10 = (f32[896,128]{1,0:T(8,128)S(1)}, f32[896,128]{1,0:T(8,128)S(1)}, u32[]{:S(2)}, u32[]{:S(2)}) collective-permute-start(f32[896,128]{1,0:T(8,128)S(1)} %get-tuple-element.50.refs_1_), channel_id=1, source_target_pairs={{0,8},{1,17},{2,10},{3,19},{4,12},{5,21},{6,14},{7,23},{8,24},{9,1... | collective-permute-start | bytes 1376264 | tf_op jit(solution)/shard_map/ppermute | solution.py:519
  33.1 4.7 %collective-permute-start.7 = (f32[192,128]{1,0:T(8,128)S(1)}, f32[192,128]{1,0:T(8,128)S(1)}, u32[]{:S(2)}, u32[]{:S(2)}) collective-permute-start(f32[192,128]{1,0:T(8,128)S(1)} %slice.3), channel_id=1, source_target_pairs={{0,2},{1,3},{2,0},{3,1},{4,6},{5,7},{6,4},{7,5},{8,10},{9,11},{10,... | collective-permute-start | bytes 294920 | tf_op jit(solution)/shard_map/ppermute | solution.py:554
  34.2 8.5 %collective-permute-start.9 = (f32[512,128]{1,0:T(8,128)S(1)}, f32[512,128]{1,0:T(8,128)S(1)}, u32[]{:S(2)}, u32[]{:S(2)}) collective-permute-start(f32[512,128]{1,0:T(8,128)S(1)} %get-tuple-element.51.refs_2_), channel_id=1, source_target_pairs={{0,8},{1,17},{2,10},{3,19},{4,12},{5,21},{6,14},{7,23},{8,24},{9,1... | collective-permute-start | bytes 786440 | tf_op jit(solution)/shard_map/ppermute | solution.py:519
  37.8 23.9 %collective-permute-start.18 = (f32[3584,128]{1,0:T(8,128)S(1)}, f32[3584,128]{1,0:T(8,128)S(1)}, u32[]{:S(2)}, u32[]{:S(2)}) collective-permute-start(f32[3584,128]{1,0:T(8,128)S(1)} %get-tuple-element.68.bulk_ref), channel_id=1, source_target_pairs={{0,16},{1,9},{2,18},{3,11},{4,20},{5,13},{6,22},{7,15},{8,0},{9,25... | collective-permute-start | bytes 5505032 | tf_op jit(solution)/shard_map/ppermute | solution.py:519
  43.0 6.1 %collective-permute-start.14 = (f32[128,128]{1,0:T(8,128)S(1)}, f32[128,128]{1,0:T(8,128)S(1)}, u32[]{:S(2)}, u32[]{:S(2)}) collective-permute-start(f32[128,128]{1,0:T(8,128)S(1)} %get-tuple-element.67), channel_id=1, source_target_pairs={{0,7},{1,6},{2,5},{3,4},{4,3},{5,2},{6,1},{7,0},{8,15},{9,14},{10,... | collective-permute-start | bytes 196616 | tf_op jit(solution)/shard_map/ppermute | solution.py:526
  43.1 8.4 %collective-permute-start.13 = (f32[128,128]{1,0:T(8,128)S(1)}, f32[128,128]{1,0:T(8,128)S(1)}, u32[]{:S(2)}, u32[]{:S(2)}) collective-permute-start(f32[128,128]{1,0:T(8,128)S(1)} %get-tuple-element.67), channel_id=1, source_target_pairs={{0,5},{1,4},{2,7},{3,6},{4,1},{5,0},{6,3},{7,2},{8,13},{9,12},{10,... | collective-permute-start | bytes 196616 | tf_op jit(solution)/shard_map/ppermute | solution.py:526
  45.3 6.2 %collective-permute-start.12 = (f32[128,128]{1,0:T(8,128)S(1)}, f32[128,128]{1,0:T(8,128)S(1)}, u32[]{:S(2)}, u32[]{:S(2)}) collective-permute-start(f32[128,128]{1,0:T(8,128)S(1)} %get-tuple-element.67), channel_id=1, source_target_pairs={{0,3},{1,2},{2,1},{3,0},{4,7},{5,6},{6,5},{7,4},{8,11},{9,10},{10,... | collective-permute-start | bytes 196616 | tf_op jit(solution)/shard_map/ppermute | solution.py:526
  46.4 5.1 %collective-permute-start.11 = (f32[128,128]{1,0:T(8,128)S(1)}, f32[128,128]{1,0:T(8,128)S(1)}, u32[]{:S(2)}, u32[]{:S(2)}) collective-permute-start(f32[128,128]{1,0:T(8,128)S(1)} %get-tuple-element.67), channel_id=1, source_target_pairs={{0,1},{1,0},{2,3},{3,2},{4,5},{5,4},{6,7},{7,6},{8,9},{9,8},{10,11... | collective-permute-start | bytes 196616 | tf_op jit(solution)/shard_map/ppermute | solution.py:526
  51.5 5.1 %collective-permute-start.16 = (f32[128,128]{1,0:T(8,128)S(1)}, f32[128,128]{1,0:T(8,128)S(1)}, u32[]{:S(2)}, u32[]{:S(2)}) collective-permute-start(f32[128,128]{1,0:T(8,128)S(1)} %add_add_fusion.1), channel_id=1, source_target_pairs={{0,8},{1,17},{2,10},{3,19},{4,12},{5,21},{6,14},{7,23},{8,24},{9,1... | collective-permute-start | bytes 196616 | tf_op jit(solution)/shard_map/ppermute | solution.py:519
  53.1 3.5 %collective-permute-start.15 = (f32[128,128]{1,0:T(8,128)S(1)}, f32[128,128]{1,0:T(8,128)S(1)}, u32[]{:S(2)}, u32[]{:S(2)}) collective-permute-start(f32[128,128]{1,0:T(8,128)S(1)} %add_add_fusion.1), channel_id=1, source_target_pairs={{0,1},{1,0},{2,3},{3,2},{4,5},{5,4},{6,7},{7,6},{8,9},{9,8},{10,11... | collective-permute-start | bytes 196616 | tf_op jit(solution)/shard_map/ppermute | solution.py:566
  53.1 11.4 %collective-permute-start.8 = (f32[512,128]{1,0:T(8,128)S(1)}, f32[512,128]{1,0:T(8,128)S(1)}, u32[]{:S(2)}, u32[]{:S(2)}) collective-permute-start(f32[512,128]{1,0:T(8,128)S(1)} %get-tuple-element.58.tail_ref), channel_id=1, source_target_pairs={{0,16},{1,9},{2,18},{3,11},{4,20},{5,13},{6,22},{7,15},{8,0},{9,25... | collective-permute-start | bytes 786440 | tf_op jit(solution)/shard_map/ppermute | solution.py:519
  59.5 2.1 %collective-permute-start.17 = (f32[256,128]{1,0:T(8,128)S(1)}, f32[256,128]{1,0:T(8,128)S(1)}, u32[]{:S(2)}, u32[]{:S(2)}) collective-permute-start(f32[256,128]{1,0:T(8,128)S(1)} %second_rotation.1.refs_6_), channel_id=1, source_target_pairs={{0,1},{1,0},{2,3},{3,2},{4,5},{5,4},{6,7},{7,6},{8,9},{9,8},{10,11... | collective-permute-start | bytes 393224 | tf_op jit(solution)/shard_map/ppermute | solution.py:568

commit v6 on v5

--- a/solution.py
+++ b/solution.py
@@ -212,21 +212,13 @@
     )[0]
 
 
-def local_gram(matrix, low, step):
+def local_gram(matrix, step):
     rows, width = matrix.shape[1:]
-    early = low.shape[1]
-
-    def kernel(matrix_ref, low_ref, high_ref, keep_ref, give_ref, sems):
-        copies = []
-        for k, (start, count) in enumerate(spans(early, rows, step)):
-            place = pl.ds(start - early, count)
-            copies.append(pltpu.make_async_copy(matrix_ref.at[:, pl.ds(start, count)], high_ref.at[:, place], sems.at[k]))
-            copies[-1].start()
-        local = Rows.of((low_ref, high_ref), (early, rows - early))
+
+    def kernel(matrix_ref, keep_ref, give_ref):
+        local = Rows((matrix_ref, 0, rows, 0))
         total = jnp.zeros((2 * width, 4 * width), F32)
-        for start, count in spans(0, rows, step, early):
-            if start >= early:
-                copies.pop(0).wait()
+        for start, count in spans(0, rows, step):
             high, low = halves(local.pair(start, count))
             total = total + dot(high, jnp.concatenate([high, low], 1), ((0,), (0,)))
         rest = total[:, 2 * width :]
@@ -242,15 +234,8 @@
         keep_ref[width:] = pad
         give_ref[width:] = pad
 
-    outs = [((2, rows - early, width), HERE)] + [((width + 8, width), HERE)] * 2
-    return call(
-        kernel,
-        outs,
-        [(matrix, FAR), (low, HERE)],
-        "gram",
-        16 * rows * width * width,
-        [pltpu.SemaphoreType.DMA((len(spans(early, rows, step)),))],
-        limit=WHOLE,
+    return call(
+        kernel, [((width + 8, width), HERE)] * 2, [(matrix, HERE)], "gram", 16 * rows * width * width
     )
 
 
@@ -287,13 +272,13 @@
     return rows_product(turn.T, right_parts(rows_product(gram, right_parts(turn))))
 
 
-def small_part(high, turn, gram, small, step):
+def small_part(matrix, early, turn, gram, small, step):
     width = turn.shape[1]
     turn_share, gram_share = width, width // 2
 
-    def kernel(high_ref, turn_ref, gram_ref, out_ref, square_ref):
+    def kernel(matrix_ref, turn_ref, gram_ref, out_ref, square_ref):
         place = share_of()
-        local = Rows((high_ref, 0, high.shape[1], 0))
+        local = Rows((matrix_ref, -early, matrix.shape[1], 0))
         parts = right_parts(turn_ref[...])
         for start, number in spans(0, small, step):
             out_ref[pl.ds(SHARE * width // 2 + start, number), :] = rows_product(local.pair(start, number), parts)
@@ -306,19 +291,19 @@
     return call(
         kernel,
         [((SHARE * width // 2 + small, width), HERE)],
-        [(high, HERE), (turn, HERE), (gram, HERE)],
+        [(matrix, HERE), (turn, HERE), (gram, HERE)],
         "small_part",
         12 * small * width * width,
         [pltpu.VMEM((width, width), F32)],
     )[0]
 
 
-def sent_parts(high, first, second, gram, small, last, step):
+def sent_parts(matrix, early, first, second, gram, small, last, step):
     width = first.shape[1]
-    count = high.shape[1]
-
-    def kernel(high_ref, first_ref, second_ref, gram_ref, main_ref, last_ref, second_gram_ref):
-        local = Rows((high_ref, 0, count, 0))
+    count = matrix.shape[1] - early
+
+    def kernel(matrix_ref, first_ref, second_ref, gram_ref, main_ref, last_ref, second_gram_ref):
+        local = Rows((matrix_ref, -early, matrix.shape[1], 0))
         out = Rows((main_ref, small, count - small - last, 0), (last_ref, count - last, last, 0))
         parts = right_parts(first_ref[...])
         for start, number in spans(small, count, step, count - last):
@@ -329,21 +314,20 @@
     return call(
         kernel,
         [((count - small - last, width), HERE), ((last, width), HERE), ((width, width), HERE)],
-        [(high, HERE), (first, HERE), (second, HERE), (gram, HERE)],
+        [(matrix, HERE), (first, HERE), (second, HERE), (gram, HERE)],
         "sent_parts",
         12 * count * width * width,
     )
 
 
-def rest_parts(low, high, first, second, sent, bulk, step):
+def rest_parts(matrix, early, first, second, sent, bulk, step):
     width = first.shape[1]
-    sizes = low.shape[1], high.shape[1]
-    early, rows = sizes[0], sum(sizes)
+    rows = matrix.shape[1]
     arrays = [array for array, *_ in sent]
 
-    def kernel(low_ref, high_ref, first_ref, second_ref, *refs):
+    def kernel(matrix_ref, first_ref, second_ref, *refs):
         bulk_ref, tail_ref, high_half_ref, low_half_ref = refs[len(sent) :]
-        here = Rows.of((low_ref, high_ref), sizes)
+        here = Rows((matrix_ref, 0, rows, 0))
         there = Rows(*[(ref, *where) for ref, (_, *where) in zip(refs, sent)])
         out = Rows.of((bulk_ref, tail_ref), (bulk, rows - bulk))
         parts = right_parts(second_ref[...])
@@ -359,7 +343,7 @@
     return call(
         kernel,
         [((bulk, width), HERE), ((rows - bulk, width), HERE)] + [((rows, width), HERE, BF16)] * 2,
-        [(part, HERE) for part in (low, high, first, second, *arrays)],
+        [(part, HERE) for part in (matrix, first, second, *arrays)],
         "rest_parts",
         12 * (rows + early) * width * width,
     )
@@ -536,19 +520,19 @@
 
     low = raw_rows(matrix, early)
     far_raw = travel(low, outward)
-    high, keep, give = local_gram(matrix, low, step)
+    keep, give = local_gram(matrix, step)
     mine = chip_sum(keep + lax.ppermute(give, "row", core), 4)
     other = lax.ppermute(mine, "row", core)
     turn_first, turn_second, gram = first_rotation(mine, other)
 
-    sent_small = small_part(high, turn_first, gram, small, step)
+    sent_small = small_part(matrix, early, turn_first, gram, small, step)
     far_small = travel(sent_small, outward)
     turn_main, sent_small, far_raw = lax.optimization_barrier((turn_first, sent_small, far_raw))
-    sent_main, sent_last, second_gram = sent_parts(high, turn_main, turn_second, gram, small, last, step)
+    sent_main, sent_last, second_gram = sent_parts(matrix, early, turn_main, turn_second, gram, small, last, step)
     far_main, far_last = travel(sent_main, outward), travel(sent_last, outward)
     turn_second, sent_main = lax.optimization_barrier((turn_second, sent_main))
     sent = [(sent_small, early, small, offset), (sent_main, early + small, main, 0), (sent_last, rows - last, last, 0)]
-    second_bulk, second_tail, *first_halves = rest_parts(low, high, turn_first, turn_second, sent, bulk, step)
+    second_bulk, second_tail, *first_halves = rest_parts(matrix, early, turn_first, turn_second, sent, bulk, step)
 
     far_small, second_bulk = lax.optimization_barrier((far_small, second_bulk))
     share = lax.ppermute(far_small[:offset], "row", [(r, r ^ 2) for r in range(rows_count)])

time: 65.8 us -> 65.1 us (0.989)
  starting transfers between devices: 22.3 us -> 24.4 us
  waiting for transfers between devices: 22.4 us -> 20.7 us
  Pallas kernels: 20.6 us -> 19.4 us
    pallas_call x13, Pallas kernels: 20.6 us -> 19.4 us  [call(): pl.pallas_call(kernel, in_specs=[pl.BlockSpec(memory_space=place) for pla...]
    ppermute x1, starting transfers between devices: 1.14 us -> 2.11 us  [body(): lax.ppermute(far_small[:offset], 'row', [(r, r ^ 2) for r in range(rows_c...]
    ppermute x1, waiting for transfers between devices: 2.03 us -> 1.1 us  [body(): lax.ppermute(far_small[:offset], 'row', [(r, r ^ 2) for r in range(rows_c...]
    ppermute x7, starting transfers between devices: 12.2 us -> 13 us  [travel(): return lax.ppermute(block, ('pair', 'row'), moves)]
  transfers between devices with their start and end apart: 19 -> 19, of which waited for: 12 -> 11; matrix products, arithmetic and copies ran while one was open for 0% -> 0% of each run, Pallas kernels for 28% -> 26%
where the time goes in v6:
time: 65.1 us; the launch traced here: 64.9 us
  starting transfers between devices  24.4 us (37%)
  waiting for transfers between devices  20.7 us (32%)
  Pallas kernels  19.4 us (30%)
    pallas_call x13, Pallas kernels, call(): pl.pallas_call(kernel, in_specs=[pl.BlockSpec(memory_space=place) for pla...  19.4 us
    ppermute x7, starting transfers between devices, travel(): return lax.ppermute(block, ('pair', 'row'), moves)  13 us
    ppermute x7, waiting for transfers between devices, chip_sum(): lax.ppermute(block, 'row', [(r, r ^ d) for r in range(rows_count)])  9.34 us
    ppermute x7, starting transfers between devices, chip_sum(): lax.ppermute(block, 'row', [(r, r ^ d) for r in range(rows_count)])  8.73 us
    ppermute x7, waiting for transfers between devices, travel(): return lax.ppermute(block, ('pair', 'row'), moves)  7.79 us
    ppermute x1, starting transfers between devices, body(): lax.ppermute(far_small[:offset], 'row', [(r, r ^ 2) for r in range(rows_c...  2.11 us
  transfers between devices with their start and end apart: 19, of which 11 were waited for; matrix products, arithmetic and copies ran while one was open for 0% of the time, Pallas kernels for 26%

profile of v6, /device:TPU:0, one launch (start us, length us, event | category | flops | bytes accessed | tf_op | source)
XLA Modules:
  0.0 64.9 jit_solution(14103229739382564893)
XLA Ops:
  0.0 1.6 %raw_rows.1 = f32[2,1792,128]{2,1,0:T(8,128)S(1)} custom-call(f32[2,4096,128]{2,1,0:T(8,128)} %matrix_ref.9), custom_call_target="tpu_custom_call" | custom-call | tf_op jit(solution)/shard_map/raw_rows/pallas_call | solution.py:140
  1.6 3.0 %collective-permute-start.5 = (f32[2,1792,128]{2,1,0:T(8,128)S(1)}, f32[2,1792,128]{2,1,0:T(8,128)S(1)}, u32[]{:S(2)}, u32[]{:S(2)}) collective-permute-start(f32[2,1792,128]{2,1,0:T(8,128)S(1)} %raw_rows.1), channel_id=1, source_target_pairs={{0,8},{1,17},{2,10},{3,19},{4,12},{5,21},{6,14},{7,23},{8,24},{9,1... | collective-permute-start | bytes 5505032 | tf_op jit(solution)/shard_map/ppermute | solution.py:503
  4.6 1.4 %gram.1 = (f32[136,128]{1,0:T(8,128)S(1)}, f32[136,128]{1,0:T(8,128)S(1)}) custom-call(f32[2,4096,128]{2,1,0:T(8,128)S(1)} %copy-done), custom_call_target="tpu_custom_call" | custom-call | tf_op jit(solution)/shard_map/gram/pallas_call | solution.py:140
  6.1 1.2 %collective-permute-done = f32[136,128]{1,0:T(8,128)S(1)} collective-permute-done((f32[136,128]{1,0:T(8,128)S(1)}, f32[136,128]{1,0:T(8,128)S(1)}, u32[]{:S(2)}, u32[]{:S(2)}) %collective-permute-start) | collective-permute-done | bytes 69664 | tf_op jit(solution)/shard_map/ppermute | solution.py:524
  7.3 3.7 %collective-permute-start.3 = (f32[136,128]{1,0:T(8,128)S(1)}, f32[136,128]{1,0:T(8,128)S(1)}, u32[]{:S(2)}, u32[]{:S(2)}) collective-permute-start(f32[136,128]{1,0:T(8,128)S(1)} %add.21), channel_id=1, source_target_pairs={{0,6},{1,7},{2,4},{3,5},{4,2},{5,3},{6,0},{7,1},{8,14},{9,15},{10,... | collective-permute-start | bytes 208904 | tf_op jit(solution)/shard_map/ppermute | solution.py:510
  11.8 2.1 %collective-permute-done.3 = f32[136,128]{1,0:T(8,128)S(1)} collective-permute-done((f32[136,128]{1,0:T(8,128)S(1)}, f32[136,128]{1,0:T(8,128)S(1)}, u32[]{:S(2)}, u32[]{:S(2)}) %collective-permute-start.3) | collective-permute-done | bytes 69664 | tf_op jit(solution)/shard_map/ppermute | solution.py:510
  13.8 3.4 %collective-permute-done.2 = f32[136,128]{1,0:T(8,128)S(1)} collective-permute-done((f32[136,128]{1,0:T(8,128)S(1)}, f32[136,128]{1,0:T(8,128)S(1)}, u32[]{:S(2)}, u32[]{:S(2)}) %collective-permute-start.2) | collective-permute-done | bytes 69664 | tf_op jit(solution)/shard_map/ppermute | solution.py:510
  17.3 1.2 %collective-permute-done.4.other_ref = f32[136,128]{1,0:T(8,128)S(1)} collective-permute-done((f32[136,128]{1,0:T(8,128)S(1)}, f32[136,128]{1,0:T(8,128)S(1)}, u32[]{:S(2)}, u32[]{:S(2)}) %collective-permute-start.4) | collective-permute-done | bytes 69664 | tf_op jit(solution)/shard_map/ppermute | solution.py:525
  18.6 3.1 %first_rotation.1 = (f32[256,128]{1,0:T(8,128)S(1)}, f32[256,128]{1,0:T(8,128)S(1)}, f32[256,256]{1,0:T(8,128)S(1)}) custom-call(f32[136,128]{1,0:T(8,128)S(1)} %add_add_fusion.mine_ref, f32[136,128]{1,0:T(8,128)S(1)} %collective-permute-done.4.other_ref), custom_call_target="tpu_custom_call" | custom-call | tf_op jit(solution)/shard_map/first_rotation/pallas_call | solution.py:140
  22.3 1.6 %collective-permute-start.6 = (f32[1088,128]{1,0:T(8,128)S(1)}, f32[1088,128]{1,0:T(8,128)S(1)}, u32[]{:S(2)}, u32[]{:S(2)}) collective-permute-start(f32[1088,128]{1,0:T(8,128)S(1)} %small_part.1.refs_0_), channel_id=1, source_target_pairs={{0,8},{1,17},{2,10},{3,19},{4,12},{5,21},{6,14},{7,23},{8,24},{9,1... | collective-permute-start | bytes 1671176 | tf_op jit(solution)/shard_map/ppermute | solution.py:503
  23.8 2.0 %collective-permute-done.5.raw_ref = f32[2,1792,128]{2,1,0:T(8,128)S(1)} collective-permute-done((f32[2,1792,128]{2,1,0:T(8,128)S(1)}, f32[2,1792,128]{2,1,0:T(8,128)S(1)}, u32[]{:S(2)}, u32[]{:S(2)}) %collective-permute-start.5) | collective-permute-done | bytes 1835040 | tf_op jit(solution)/shard_map/ppermute | solution.py:503
  26.6 2.0 %collective-permute-start.10 = (f32[896,128]{1,0:T(8,128)S(1)}, f32[896,128]{1,0:T(8,128)S(1)}, u32[]{:S(2)}, u32[]{:S(2)}) collective-permute-start(f32[896,128]{1,0:T(8,128)S(1)} %get-tuple-element.48.refs_1_), channel_id=1, source_target_pairs={{0,8},{1,17},{2,10},{3,19},{4,12},{5,21},{6,14},{7,23},{8,24},{9,1... | collective-permute-start | bytes 1376264 | tf_op jit(solution)/shard_map/ppermute | solution.py:503
  28.7 1.9 %rest_parts.1 = (f32[3584,128]{1,0:T(8,128)S(1)}, f32[512,128]{1,0:T(8,128)S(1)}, bf16[4096,128]{1,0:T(8,128)(2,1)S(1)}, bf16[4096,128]{1,0:T(8,128)(2,1)S(1)}) custom-call(f32[2,4096,128]{2,1,0:T(8,128)S(1)} %copy-done, f32[256,128]{1,0:T(8,128)S(1)} %get-tuple-element.44.turn_ref.first_ref, f32[256,128]{1,0:T(8,128)S(1)} %get-tuple-element.46.second_ref, ...), custom_call_target="tpu_custom_call" | custom-call | tf_op jit(solution)/shard_map/rest_parts/pallas_call | solution.py:140
  30.6 1.3 %collective-permute-done.6.small_ref = f32[1088,128]{1,0:T(8,128)S(1)} collective-permute-done((f32[1088,128]{1,0:T(8,128)S(1)}, f32[1088,128]{1,0:T(8,128)S(1)}, u32[]{:S(2)}, u32[]{:S(2)}) %collective-permute-start.6) | collective-permute-done | bytes 557088 | tf_op jit(solution)/shard_map/ppermute | solution.py:503
  31.9 2.1 %collective-permute-start.7 = (f32[192,128]{1,0:T(8,128)S(1)}, f32[192,128]{1,0:T(8,128)S(1)}, u32[]{:S(2)}, u32[]{:S(2)}) collective-permute-start(f32[192,128]{1,0:T(8,128)S(1)} %slice.3), channel_id=1, source_target_pairs={{0,2},{1,3},{2,0},{3,1},{4,6},{5,7},{6,4},{7,5},{8,10},{9,11},{10,... | collective-permute-start | bytes 294920 | tf_op jit(solution)/shard_map/ppermute | solution.py:538
  34.0 1.5 %collective-permute-start.9 = (f32[512,128]{1,0:T(8,128)S(1)}, f32[512,128]{1,0:T(8,128)S(1)}, u32[]{:S(2)}, u32[]{:S(2)}) collective-permute-start(f32[512,128]{1,0:T(8,128)S(1)} %get-tuple-element.49.refs_2_), channel_id=1, source_target_pairs={{0,8},{1,17},{2,10},{3,19},{4,12},{5,21},{6,14},{7,23},{8,24},{9,1... | collective-permute-start | bytes 786440 | tf_op jit(solution)/shard_map/ppermute | solution.py:503
  35.5 1.1 %collective-permute-done.7.share_ref = f32[192,128]{1,0:T(8,128)S(1)} collective-permute-done((f32[192,128]{1,0:T(8,128)S(1)}, f32[192,128]{1,0:T(8,128)S(1)}, u32[]{:S(2)}, u32[]{:S(2)}) %collective-permute-start.7) | collective-permute-done | bytes 98336 | tf_op jit(solution)/shard_map/ppermute | solution.py:538
  36.6 2.0 %collective-permute-start.18 = (f32[3584,128]{1,0:T(8,128)S(1)}, f32[3584,128]{1,0:T(8,128)S(1)}, u32[]{:S(2)}, u32[]{:S(2)}) collective-permute-start(f32[3584,128]{1,0:T(8,128)S(1)} %get-tuple-element.66.bulk_ref), channel_id=1, source_target_pairs={{0,16},{1,9},{2,18},{3,11},{4,20},{5,13},{6,22},{7,15},{8,0},{9,25... | collective-permute-start | bytes 5505032 | tf_op jit(solution)/shard_map/ppermute | solution.py:503
  38.5 1.5 %raw_cross.1 = (bf16[2688,256]{1,0:T(8,128)(2,1)S(1)}, bf16[2688,256]{1,0:T(8,128)(2,1)S(1)}, f32[128,128]{1,0:T(8,128)S(1)}, f32[128,128]{1,0:T(8,128)S(1)}) custom-call(f32[2,1792,128]{2,1,0:T(8,128)S(1)} %collective-permute-done.5.raw_ref, f32[1088,128]{1,0:T(8,128)S(1)} %collective-permute-done.6.small_ref, ...), custom_call_target="tpu_custom_call" | custom-call | tf_op jit(solution)/shard_map/raw_cross/pallas_call | solution.py:140
  40.4 2.7 %collective-permute-done.9.far_ref = f32[512,128]{1,0:T(8,128)S(1)} collective-permute-done((f32[512,128]{1,0:T(8,128)S(1)}, f32[512,128]{1,0:T(8,128)S(1)}, u32[]{:S(2)}, u32[]{:S(2)}) %collective-permute-start.9) | collective-permute-done | bytes 262176 | tf_op jit(solution)/shard_map/ppermute | solution.py:503
  43.5 1.9 %collective-permute-start.13 = (f32[128,128]{1,0:T(8,128)S(1)}, f32[128,128]{1,0:T(8,128)S(1)}, u32[]{:S(2)}, u32[]{:S(2)}) collective-permute-start(f32[128,128]{1,0:T(8,128)S(1)} %get-tuple-element.65), channel_id=1, source_target_pairs={{0,5},{1,4},{2,7},{3,6},{4,1},{5,0},{6,3},{7,2},{8,13},{9,12},{10,... | collective-permute-start | bytes 196616 | tf_op jit(solution)/shard_map/ppermute | solution.py:510
  45.4 1.2 %collective-permute-start.12 = (f32[128,128]{1,0:T(8,128)S(1)}, f32[128,128]{1,0:T(8,128)S(1)}, u32[]{:S(2)}, u32[]{:S(2)}) collective-permute-start(f32[128,128]{1,0:T(8,128)S(1)} %get-tuple-element.65), channel_id=1, source_target_pairs={{0,3},{1,2},{2,1},{3,0},{4,7},{5,6},{6,5},{7,4},{8,11},{9,10},{10,... | collective-permute-start | bytes 196616 | tf_op jit(solution)/shard_map/ppermute | solution.py:510
  46.6 1.1 %collective-permute-start.11 = (f32[128,128]{1,0:T(8,128)S(1)}, f32[128,128]{1,0:T(8,128)S(1)}, u32[]{:S(2)}, u32[]{:S(2)}) collective-permute-start(f32[128,128]{1,0:T(8,128)S(1)} %get-tuple-element.65), channel_id=1, source_target_pairs={{0,1},{1,0},{2,3},{3,2},{4,5},{5,4},{6,7},{7,6},{8,9},{9,8},{10,11... | collective-permute-start | bytes 196616 | tf_op jit(solution)/shard_map/ppermute | solution.py:510
  47.7 1.7 %collective-permute-done.14 = f32[128,128]{1,0:T(8,128)S(1)} collective-permute-done((f32[128,128]{1,0:T(8,128)S(1)}, f32[128,128]{1,0:T(8,128)S(1)}, u32[]{:S(2)}, u32[]{:S(2)}) %collective-permute-start.14) | collective-permute-done | bytes 65568 | tf_op jit(solution)/shard_map/ppermute | solution.py:510
  49.4 2.2 %collective-permute-done.13 = f32[128,128]{1,0:T(8,128)S(1)} collective-permute-done((f32[128,128]{1,0:T(8,128)S(1)}, f32[128,128]{1,0:T(8,128)S(1)}, u32[]{:S(2)}, u32[]{:S(2)}) %collective-permute-start.13) | collective-permute-done | bytes 65568 | tf_op jit(solution)/shard_map/ppermute | solution.py:510
  51.6 1.4 %collective-permute-start.16 = (f32[128,128]{1,0:T(8,128)S(1)}, f32[128,128]{1,0:T(8,128)S(1)}, u32[]{:S(2)}, u32[]{:S(2)}) collective-permute-start(f32[128,128]{1,0:T(8,128)S(1)} %add_add_fusion.1), channel_id=1, source_target_pairs={{0,8},{1,17},{2,10},{3,19},{4,12},{5,21},{6,14},{7,23},{8,24},{9,1... | collective-permute-start | bytes 196616 | tf_op jit(solution)/shard_map/ppermute | solution.py:503
  53.4 1.5 %collective-permute-start.8 = (f32[512,128]{1,0:T(8,128)S(1)}, f32[512,128]{1,0:T(8,128)S(1)}, u32[]{:S(2)}, u32[]{:S(2)}) collective-permute-start(f32[512,128]{1,0:T(8,128)S(1)} %get-tuple-element.56.tail_ref), channel_id=1, source_target_pairs={{0,16},{1,9},{2,18},{3,11},{4,20},{5,13},{6,22},{7,15},{8,0},{9,25... | collective-permute-start | bytes 786440 | tf_op jit(solution)/shard_map/ppermute | solution.py:503
  54.9 1.8 %collective-permute-done.16.there_ref = f32[128,128]{1,0:T(8,128)S(1)} collective-permute-done((f32[128,128]{1,0:T(8,128)S(1)}, f32[128,128]{1,0:T(8,128)S(1)}, u32[]{:S(2)}, u32[]{:S(2)}) %collective-permute-start.16) | collective-permute-done | bytes 65568 | tf_op jit(solution)/shard_map/ppermute | solution.py:503
  56.7 2.9 %second_rotation.1.refs_6_ = f32[256,128]{1,0:T(8,128)S(1)} custom-call(f32[128,128]{1,0:T(8,128)S(1)} %get-tuple-element.57.own_gram_ref, f32[128,128]{1,0:T(8,128)S(1)} %get-tuple-element.60.far_ref, f32[128,128]{1,0:T(8,128)S(1)} %collective-permute-done.15.here_ref, f32[128,128]{1,0:T(8,128)S(1)} %collective-permute-done.16.there_ref), custom_call_target="tpu_custom_call" | custom-call | flops 11500000256 | tf_op jit(solution)/shard_map/second_rotation/pallas_call | solution.py:140
  59.7 2.0 %here_product.1.refs_5_ = f32[2,4096,128]{2,1,0:T(8,128)} custom-call(bf16[2688,256]{1,0:T(8,128)(2,1)S(1)} %get-tuple-element.67.refs_0_, bf16[2688,256]{1,0:T(8,128)(2,1)S(1)} %get-tuple-element.68.refs_1_, bf16[896,256]{1,0:T(8,128)(2,1)S(1)} %get-tuple-element.69.refs_2_, bf16[896,256]{1,0:T(8,128)(2,1)S(1)} %get-tuple-element.70.refs_3_, ...), custom_call_target="tpu_custom_call" | custom-call | tf_op jit(solution)/shard_map/here_product/pallas_call | solution.py:140
  61.8 1.9 %bulk_product.1.refs_4_ = f32[2,4096,128]{2,1,0:T(8,128)} custom-call(bf16[4096,128]{1,0:T(8,128)(2,1)S(1)} %get-tuple-element.50.refs_0_, bf16[4096,128]{1,0:T(8,128)(2,1)S(1)} %get-tuple-element.51.refs_1_, f32[3584,128]{1,0:T(8,128)S(1)} %collective-permute-done.18.refs_2_.refs_3_, ...), custom_call_target="tpu_custom_call", output_to_operand_aliasing={{}: (5, {})} | custom-call | tf_op jit(solution)/shard_map/bulk_product/pallas_call | solution.py:140
  63.7 1.0 %tail_product.1 = f32[2,4096,128]{2,1,0:T(8,128)} custom-call(bf16[4096,128]{1,0:T(8,128)(2,1)S(1)} %get-tuple-element.50.refs_0_, bf16[4096,128]{1,0:T(8,128)(2,1)S(1)} %get-tuple-element.51.refs_1_, f32[512,128]{1,0:T(8,128)S(1)} %collective-permute-done.8.refs_2_, ...), custom_call_target="tpu_custom_call", output_to_operand_aliasing={{}: (4, {})} | custom-call | tf_op jit(solution)/shard_map/tail_product/pallas_call | solution.py:140
  (25 shorter events, 3.6 us)
Async XLA Ops:
  0.0 4.6 %copy-start = (f32[2,4096,128]{2,1,0:T(8,128)S(1)}, f32[2,4096,128]{2,1,0:T(8,128)}, u32[]{:S(2)}) copy-start(f32[2,4096,128]{2,1,0:T(8,128)} %matrix_ref.9) | copy-start | bytes 12582916
  1.6 24.2 %collective-permute-start.5 = (f32[2,1792,128]{2,1,0:T(8,128)S(1)}, f32[2,1792,128]{2,1,0:T(8,128)S(1)}, u32[]{:S(2)}, u32[]{:S(2)}) collective-permute-start(f32[2,1792,128]{2,1,0:T(8,128)S(1)} %raw_rows.1), channel_id=1, source_target_pairs={{0,8},{1,17},{2,10},{3,19},{4,12},{5,21},{6,14},{7,23},{8,24},{9,1... | collective-permute-start | bytes 5505032 | tf_op jit(solution)/shard_map/ppermute | solution.py:503
  6.0 1.3 %collective-permute-start = (f32[136,128]{1,0:T(8,128)S(1)}, f32[136,128]{1,0:T(8,128)S(1)}, u32[]{:S(2)}, u32[]{:S(2)}) collective-permute-start(f32[136,128]{1,0:T(8,128)S(1)} %get-tuple-element.40), channel_id=1, source_target_pairs={{0,1},{1,0},{2,3},{3,2},{4,5},{5,4},{6,7},{7,6},{8,9},{9,8},{10,11... | collective-permute-start | bytes 208904 | tf_op jit(solution)/shard_map/ppermute | solution.py:524
  7.3 6.5 %collective-permute-start.3 = (f32[136,128]{1,0:T(8,128)S(1)}, f32[136,128]{1,0:T(8,128)S(1)}, u32[]{:S(2)}, u32[]{:S(2)}) collective-permute-start(f32[136,128]{1,0:T(8,128)S(1)} %add.21), channel_id=1, source_target_pairs={{0,6},{1,7},{2,4},{3,5},{4,2},{5,3},{6,0},{7,1},{8,14},{9,15},{10,... | collective-permute-start | bytes 208904 | tf_op jit(solution)/shard_map/ppermute | solution.py:510
  11.0 6.2 %collective-permute-start.2 = (f32[136,128]{1,0:T(8,128)S(1)}, f32[136,128]{1,0:T(8,128)S(1)}, u32[]{:S(2)}, u32[]{:S(2)}) collective-permute-start(f32[136,128]{1,0:T(8,128)S(1)} %add.21), channel_id=1, source_target_pairs={{0,4},{1,5},{2,6},{3,7},{4,0},{5,1},{6,2},{7,3},{8,12},{9,13},{10,... | collective-permute-start | bytes 208904 | tf_op jit(solution)/shard_map/ppermute | solution.py:510
  11.0 6.2 %collective-permute-start.1 = (f32[136,128]{1,0:T(8,128)S(1)}, f32[136,128]{1,0:T(8,128)S(1)}, u32[]{:S(2)}, u32[]{:S(2)}) collective-permute-start(f32[136,128]{1,0:T(8,128)S(1)} %add.21), channel_id=1, source_target_pairs={{0,2},{1,3},{2,0},{3,1},{4,6},{5,7},{6,4},{7,5},{8,10},{9,11},{10,... | collective-permute-start | bytes 208904 | tf_op jit(solution)/shard_map/ppermute | solution.py:510
  17.2 1.3 %collective-permute-start.4 = (f32[136,128]{1,0:T(8,128)S(1)}, f32[136,128]{1,0:T(8,128)S(1)}, u32[]{:S(2)}, u32[]{:S(2)}) collective-permute-start(f32[136,128]{1,0:T(8,128)S(1)} %add_add_fusion.mine_ref), channel_id=1, source_target_pairs={{0,1},{1,0},{2,3},{3,2},{4,5},{5,4},{6,7},{7,6},{8,9},{9,8},{10,11... | collective-permute-start | bytes 208904 | tf_op jit(solution)/shard_map/ppermute | solution.py:525
  22.3 9.6 %collective-permute-start.6 = (f32[1088,128]{1,0:T(8,128)S(1)}, f32[1088,128]{1,0:T(8,128)S(1)}, u32[]{:S(2)}, u32[]{:S(2)}) collective-permute-start(f32[1088,128]{1,0:T(8,128)S(1)} %small_part.1.refs_0_), channel_id=1, source_target_pairs={{0,8},{1,17},{2,10},{3,19},{4,12},{5,21},{6,14},{7,23},{8,24},{9,1... | collective-permute-start | bytes 1671176 | tf_op jit(solution)/shard_map/ppermute | solution.py:503
  26.6 13.4 %collective-permute-start.10 = (f32[896,128]{1,0:T(8,128)S(1)}, f32[896,128]{1,0:T(8,128)S(1)}, u32[]{:S(2)}, u32[]{:S(2)}) collective-permute-start(f32[896,128]{1,0:T(8,128)S(1)} %get-tuple-element.48.refs_1_), channel_id=1, source_target_pairs={{0,8},{1,17},{2,10},{3,19},{4,12},{5,21},{6,14},{7,23},{8,24},{9,1... | collective-permute-start | bytes 1376264 | tf_op jit(solution)/shard_map/ppermute | solution.py:503
  31.9 4.7 %collective-permute-start.7 = (f32[192,128]{1,0:T(8,128)S(1)}, f32[192,128]{1,0:T(8,128)S(1)}, u32[]{:S(2)}, u32[]{:S(2)}) collective-permute-start(f32[192,128]{1,0:T(8,128)S(1)} %slice.3), channel_id=1, source_target_pairs={{0,2},{1,3},{2,0},{3,1},{4,6},{5,7},{6,4},{7,5},{8,10},{9,11},{10,... | collective-permute-start | bytes 294920 | tf_op jit(solution)/shard_map/ppermute | solution.py:538
  34.0 9.1 %collective-permute-start.9 = (f32[512,128]{1,0:T(8,128)S(1)}, f32[512,128]{1,0:T(8,128)S(1)}, u32[]{:S(2)}, u32[]{:S(2)}) collective-permute-start(f32[512,128]{1,0:T(8,128)S(1)} %get-tuple-element.49.refs_2_), channel_id=1, source_target_pairs={{0,8},{1,17},{2,10},{3,19},{4,12},{5,21},{6,14},{7,23},{8,24},{9,1... | collective-permute-start | bytes 786440 | tf_op jit(solution)/shard_map/ppermute | solution.py:503
  36.6 25.2 %collective-permute-start.18 = (f32[3584,128]{1,0:T(8,128)S(1)}, f32[3584,128]{1,0:T(8,128)S(1)}, u32[]{:S(2)}, u32[]{:S(2)}) collective-permute-start(f32[3584,128]{1,0:T(8,128)S(1)} %get-tuple-element.66.bulk_ref), channel_id=1, source_target_pairs={{0,16},{1,9},{2,18},{3,11},{4,20},{5,13},{6,22},{7,15},{8,0},{9,25... | collective-permute-start | bytes 5505032 | tf_op jit(solution)/shard_map/ppermute | solution.py:503
  43.4 6.0 %collective-permute-start.14 = (f32[128,128]{1,0:T(8,128)S(1)}, f32[128,128]{1,0:T(8,128)S(1)}, u32[]{:S(2)}, u32[]{:S(2)}) collective-permute-start(f32[128,128]{1,0:T(8,128)S(1)} %get-tuple-element.65), channel_id=1, source_target_pairs={{0,7},{1,6},{2,5},{3,4},{4,3},{5,2},{6,1},{7,0},{8,15},{9,14},{10,... | collective-permute-start | bytes 196616 | tf_op jit(solution)/shard_map/ppermute | solution.py:510
  43.5 8.1 %collective-permute-start.13 = (f32[128,128]{1,0:T(8,128)S(1)}, f32[128,128]{1,0:T(8,128)S(1)}, u32[]{:S(2)}, u32[]{:S(2)}) collective-permute-start(f32[128,128]{1,0:T(8,128)S(1)} %get-tuple-element.65), channel_id=1, source_target_pairs={{0,5},{1,4},{2,7},{3,6},{4,1},{5,0},{6,3},{7,2},{8,13},{9,12},{10,... | collective-permute-start | bytes 196616 | tf_op jit(solution)/shard_map/ppermute | solution.py:510
  45.4 6.2 %collective-permute-start.12 = (f32[128,128]{1,0:T(8,128)S(1)}, f32[128,128]{1,0:T(8,128)S(1)}, u32[]{:S(2)}, u32[]{:S(2)}) collective-permute-start(f32[128,128]{1,0:T(8,128)S(1)} %get-tuple-element.65), channel_id=1, source_target_pairs={{0,3},{1,2},{2,1},{3,0},{4,7},{5,6},{6,5},{7,4},{8,11},{9,10},{10,... | collective-permute-start | bytes 196616 | tf_op jit(solution)/shard_map/ppermute | solution.py:510
  46.6 5.0 %collective-permute-start.11 = (f32[128,128]{1,0:T(8,128)S(1)}, f32[128,128]{1,0:T(8,128)S(1)}, u32[]{:S(2)}, u32[]{:S(2)}) collective-permute-start(f32[128,128]{1,0:T(8,128)S(1)} %get-tuple-element.65), channel_id=1, source_target_pairs={{0,1},{1,0},{2,3},{3,2},{4,5},{5,4},{6,7},{7,6},{8,9},{9,8},{10,11... | collective-permute-start | bytes 196616 | tf_op jit(solution)/shard_map/ppermute | solution.py:510
  51.6 5.1 %collective-permute-start.16 = (f32[128,128]{1,0:T(8,128)S(1)}, f32[128,128]{1,0:T(8,128)S(1)}, u32[]{:S(2)}, u32[]{:S(2)}) collective-permute-start(f32[128,128]{1,0:T(8,128)S(1)} %add_add_fusion.1), channel_id=1, source_target_pairs={{0,8},{1,17},{2,10},{3,19},{4,12},{5,21},{6,14},{7,23},{8,24},{9,1... | collective-permute-start | bytes 196616 | tf_op jit(solution)/shard_map/ppermute | solution.py:503
  53.1 3.6 %collective-permute-start.15 = (f32[128,128]{1,0:T(8,128)S(1)}, f32[128,128]{1,0:T(8,128)S(1)}, u32[]{:S(2)}, u32[]{:S(2)}) collective-permute-start(f32[128,128]{1,0:T(8,128)S(1)} %add_add_fusion.1), channel_id=1, source_target_pairs={{0,1},{1,0},{2,3},{3,2},{4,5},{5,4},{6,7},{7,6},{8,9},{9,8},{10,11... | collective-permute-start | bytes 196616 | tf_op jit(solution)/shard_map/ppermute | solution.py:550
  53.4 10.3 %collective-permute-start.8 = (f32[512,128]{1,0:T(8,128)S(1)}, f32[512,128]{1,0:T(8,128)S(1)}, u32[]{:S(2)}, u32[]{:S(2)}) collective-permute-start(f32[512,128]{1,0:T(8,128)S(1)} %get-tuple-element.56.tail_ref), channel_id=1, source_target_pairs={{0,16},{1,9},{2,18},{3,11},{4,20},{5,13},{6,22},{7,15},{8,0},{9,25... | collective-permute-start | bytes 786440 | tf_op jit(solution)/shard_map/ppermute | solution.py:503
  59.6 2.1 %collective-permute-start.17 = (f32[256,128]{1,0:T(8,128)S(1)}, f32[256,128]{1,0:T(8,128)S(1)}, u32[]{:S(2)}, u32[]{:S(2)}) collective-permute-start(f32[256,128]{1,0:T(8,128)S(1)} %second_rotation.1.refs_6_), channel_id=1, source_target_pairs={{0,1},{1,0},{2,3},{3,2},{4,5},{5,4},{6,7},{7,6},{8,9},{9,8},{10,11... | collective-permute-start | bytes 393224 | tf_op jit(solution)/shard_map/ppermute | solution.py:552

commit v7 on v6

--- a/solution.py
+++ b/solution.py
@@ -212,6 +212,15 @@
     )[0]
 
 
+def tapered(start, stop, step, unit, *cuts):
+    pieces = []
+    while start < stop:
+        count = min(step, max(unit, (stop - start) // 2 // unit * unit))
+        pieces += spans(start, start + count, step, *cuts)
+        start += count
+    return pieces
+
+
 def local_gram(matrix, step):
     rows, width = matrix.shape[1:]
 
@@ -447,7 +456,7 @@
 
 def last_product(load, arrays, turn, done, slot_of, start, count, rows, step, cuts, name):
     width = turn.shape[1]
-    pieces = spans(start, start + count, step, *cuts)
+    pieces = tapered(start, start + count, 2 * step, step // STEP, *cuts)
 
     def kernel(*refs):
         turn_ref = refs[len(arrays)]

time: 65.1 us -> 64.9 us (level)
  no operation moved by 1% of the time
where the time goes in v7:
time: 64.9 us; the launch traced here: 64.7 us
  starting transfers between devices  24.4 us (38%)
  waiting for transfers between devices  20.7 us (32%)
  Pallas kernels  19.2 us (30%)
    pallas_call x13, Pallas kernels, call(): pl.pallas_call(kernel, in_specs=[pl.BlockSpec(memory_space=place) for pla...  19.2 us
    ppermute x7, starting transfers between devices, travel(): return lax.ppermute(block, ('pair', 'row'), moves)  13 us
    ppermute x7, waiting for transfers between devices, chip_sum(): lax.ppermute(block, 'row', [(r, r ^ d) for r in range(rows_count)])  9.34 us
    ppermute x7, starting transfers between devices, chip_sum(): lax.ppermute(block, 'row', [(r, r ^ d) for r in range(rows_count)])  8.73 us
    ppermute x7, waiting for transfers between devices, travel(): return lax.ppermute(block, ('pair', 'row'), moves)  7.79 us
    ppermute x1, starting transfers between devices, body(): lax.ppermute(far_small[:offset], 'row', [(r, r ^ 2) for r in range(rows_c...  2.11 us
  transfers between devices with their start and end apart: 19, of which 11 were waited for; matrix products, arithmetic and copies ran while one was open for 0% of the time, Pallas kernels for 26%

profile of v7, /device:TPU:0, one launch (start us, length us, event | category | flops | bytes accessed | tf_op | source)
XLA Modules:
  0.0 64.7 jit_solution(4387755757805859273)
XLA Ops:
  0.0 1.6 %raw_rows.1 = f32[2,1792,128]{2,1,0:T(8,128)S(1)} custom-call(f32[2,4096,128]{2,1,0:T(8,128)} %matrix_ref.9), custom_call_target="tpu_custom_call" | custom-call | tf_op jit(solution)/shard_map/raw_rows/pallas_call | solution.py:140
  1.6 3.0 %collective-permute-start.5 = (f32[2,1792,128]{2,1,0:T(8,128)S(1)}, f32[2,1792,128]{2,1,0:T(8,128)S(1)}, u32[]{:S(2)}, u32[]{:S(2)}) collective-permute-start(f32[2,1792,128]{2,1,0:T(8,128)S(1)} %raw_rows.1), channel_id=1, source_target_pairs={{0,8},{1,17},{2,10},{3,19},{4,12},{5,21},{6,14},{7,23},{8,24},{9,1... | collective-permute-start | bytes 5505032 | tf_op jit(solution)/shard_map/ppermute | solution.py:512
  4.6 1.4 %gram.1 = (f32[136,128]{1,0:T(8,128)S(1)}, f32[136,128]{1,0:T(8,128)S(1)}) custom-call(f32[2,4096,128]{2,1,0:T(8,128)S(1)} %copy-done), custom_call_target="tpu_custom_call" | custom-call | tf_op jit(solution)/shard_map/gram/pallas_call | solution.py:140
  6.1 1.2 %collective-permute-done = f32[136,128]{1,0:T(8,128)S(1)} collective-permute-done((f32[136,128]{1,0:T(8,128)S(1)}, f32[136,128]{1,0:T(8,128)S(1)}, u32[]{:S(2)}, u32[]{:S(2)}) %collective-permute-start) | collective-permute-done | bytes 69664 | tf_op jit(solution)/shard_map/ppermute | solution.py:533
  7.3 3.7 %collective-permute-start.3 = (f32[136,128]{1,0:T(8,128)S(1)}, f32[136,128]{1,0:T(8,128)S(1)}, u32[]{:S(2)}, u32[]{:S(2)}) collective-permute-start(f32[136,128]{1,0:T(8,128)S(1)} %add.21), channel_id=1, source_target_pairs={{0,6},{1,7},{2,4},{3,5},{4,2},{5,3},{6,0},{7,1},{8,14},{9,15},{10,... | collective-permute-start | bytes 208904 | tf_op jit(solution)/shard_map/ppermute | solution.py:519
  11.8 2.1 %collective-permute-done.3 = f32[136,128]{1,0:T(8,128)S(1)} collective-permute-done((f32[136,128]{1,0:T(8,128)S(1)}, f32[136,128]{1,0:T(8,128)S(1)}, u32[]{:S(2)}, u32[]{:S(2)}) %collective-permute-start.3) | collective-permute-done | bytes 69664 | tf_op jit(solution)/shard_map/ppermute | solution.py:519
  13.8 3.4 %collective-permute-done.2 = f32[136,128]{1,0:T(8,128)S(1)} collective-permute-done((f32[136,128]{1,0:T(8,128)S(1)}, f32[136,128]{1,0:T(8,128)S(1)}, u32[]{:S(2)}, u32[]{:S(2)}) %collective-permute-start.2) | collective-permute-done | bytes 69664 | tf_op jit(solution)/shard_map/ppermute | solution.py:519
  17.3 1.2 %collective-permute-done.4.other_ref = f32[136,128]{1,0:T(8,128)S(1)} collective-permute-done((f32[136,128]{1,0:T(8,128)S(1)}, f32[136,128]{1,0:T(8,128)S(1)}, u32[]{:S(2)}, u32[]{:S(2)}) %collective-permute-start.4) | collective-permute-done | bytes 69664 | tf_op jit(solution)/shard_map/ppermute | solution.py:534
  18.6 3.1 %first_rotation.1 = (f32[256,128]{1,0:T(8,128)S(1)}, f32[256,128]{1,0:T(8,128)S(1)}, f32[256,256]{1,0:T(8,128)S(1)}) custom-call(f32[136,128]{1,0:T(8,128)S(1)} %add_add_fusion.mine_ref, f32[136,128]{1,0:T(8,128)S(1)} %collective-permute-done.4.other_ref), custom_call_target="tpu_custom_call" | custom-call | tf_op jit(solution)/shard_map/first_rotation/pallas_call | solution.py:140
  22.3 1.6 %collective-permute-start.6 = (f32[1088,128]{1,0:T(8,128)S(1)}, f32[1088,128]{1,0:T(8,128)S(1)}, u32[]{:S(2)}, u32[]{:S(2)}) collective-permute-start(f32[1088,128]{1,0:T(8,128)S(1)} %small_part.1.refs_0_), channel_id=1, source_target_pairs={{0,8},{1,17},{2,10},{3,19},{4,12},{5,21},{6,14},{7,23},{8,24},{9,1... | collective-permute-start | bytes 1671176 | tf_op jit(solution)/shard_map/ppermute | solution.py:512
  23.8 2.0 %collective-permute-done.5.raw_ref = f32[2,1792,128]{2,1,0:T(8,128)S(1)} collective-permute-done((f32[2,1792,128]{2,1,0:T(8,128)S(1)}, f32[2,1792,128]{2,1,0:T(8,128)S(1)}, u32[]{:S(2)}, u32[]{:S(2)}) %collective-permute-start.5) | collective-permute-done | bytes 1835040 | tf_op jit(solution)/shard_map/ppermute | solution.py:512
  26.6 2.0 %collective-permute-start.10 = (f32[896,128]{1,0:T(8,128)S(1)}, f32[896,128]{1,0:T(8,128)S(1)}, u32[]{:S(2)}, u32[]{:S(2)}) collective-permute-start(f32[896,128]{1,0:T(8,128)S(1)} %get-tuple-element.48.refs_1_), channel_id=1, source_target_pairs={{0,8},{1,17},{2,10},{3,19},{4,12},{5,21},{6,14},{7,23},{8,24},{9,1... | collective-permute-start | bytes 1376264 | tf_op jit(solution)/shard_map/ppermute | solution.py:512
  28.7 1.9 %rest_parts.1 = (f32[3584,128]{1,0:T(8,128)S(1)}, f32[512,128]{1,0:T(8,128)S(1)}, bf16[4096,128]{1,0:T(8,128)(2,1)S(1)}, bf16[4096,128]{1,0:T(8,128)(2,1)S(1)}) custom-call(f32[2,4096,128]{2,1,0:T(8,128)S(1)} %copy-done, f32[256,128]{1,0:T(8,128)S(1)} %get-tuple-element.44.turn_ref.first_ref, f32[256,128]{1,0:T(8,128)S(1)} %get-tuple-element.46.second_ref, ...), custom_call_target="tpu_custom_call" | custom-call | tf_op jit(solution)/shard_map/rest_parts/pallas_call | solution.py:140
  30.6 1.3 %collective-permute-done.6.small_ref = f32[1088,128]{1,0:T(8,128)S(1)} collective-permute-done((f32[1088,128]{1,0:T(8,128)S(1)}, f32[1088,128]{1,0:T(8,128)S(1)}, u32[]{:S(2)}, u32[]{:S(2)}) %collective-permute-start.6) | collective-permute-done | bytes 557088 | tf_op jit(solution)/shard_map/ppermute | solution.py:512
  31.9 2.1 %collective-permute-start.7 = (f32[192,128]{1,0:T(8,128)S(1)}, f32[192,128]{1,0:T(8,128)S(1)}, u32[]{:S(2)}, u32[]{:S(2)}) collective-permute-start(f32[192,128]{1,0:T(8,128)S(1)} %slice.3), channel_id=1, source_target_pairs={{0,2},{1,3},{2,0},{3,1},{4,6},{5,7},{6,4},{7,5},{8,10},{9,11},{10,... | collective-permute-start | bytes 294920 | tf_op jit(solution)/shard_map/ppermute | solution.py:547
  34.0 1.5 %collective-permute-start.9 = (f32[512,128]{1,0:T(8,128)S(1)}, f32[512,128]{1,0:T(8,128)S(1)}, u32[]{:S(2)}, u32[]{:S(2)}) collective-permute-start(f32[512,128]{1,0:T(8,128)S(1)} %get-tuple-element.49.refs_2_), channel_id=1, source_target_pairs={{0,8},{1,17},{2,10},{3,19},{4,12},{5,21},{6,14},{7,23},{8,24},{9,1... | collective-permute-start | bytes 786440 | tf_op jit(solution)/shard_map/ppermute | solution.py:512
  35.5 1.1 %collective-permute-done.7.share_ref = f32[192,128]{1,0:T(8,128)S(1)} collective-permute-done((f32[192,128]{1,0:T(8,128)S(1)}, f32[192,128]{1,0:T(8,128)S(1)}, u32[]{:S(2)}, u32[]{:S(2)}) %collective-permute-start.7) | collective-permute-done | bytes 98336 | tf_op jit(solution)/shard_map/ppermute | solution.py:547
  36.6 2.0 %collective-permute-start.18 = (f32[3584,128]{1,0:T(8,128)S(1)}, f32[3584,128]{1,0:T(8,128)S(1)}, u32[]{:S(2)}, u32[]{:S(2)}) collective-permute-start(f32[3584,128]{1,0:T(8,128)S(1)} %get-tuple-element.66.bulk_ref), channel_id=1, source_target_pairs={{0,16},{1,9},{2,18},{3,11},{4,20},{5,13},{6,22},{7,15},{8,0},{9,25... | collective-permute-start | bytes 5505032 | tf_op jit(solution)/shard_map/ppermute | solution.py:512
  38.5 1.5 %raw_cross.1 = (bf16[2688,256]{1,0:T(8,128)(2,1)S(1)}, bf16[2688,256]{1,0:T(8,128)(2,1)S(1)}, f32[128,128]{1,0:T(8,128)S(1)}, f32[128,128]{1,0:T(8,128)S(1)}) custom-call(f32[2,1792,128]{2,1,0:T(8,128)S(1)} %collective-permute-done.5.raw_ref, f32[1088,128]{1,0:T(8,128)S(1)} %collective-permute-done.6.small_ref, ...), custom_call_target="tpu_custom_call" | custom-call | tf_op jit(solution)/shard_map/raw_cross/pallas_call | solution.py:140
  40.4 2.7 %collective-permute-done.9.far_ref = f32[512,128]{1,0:T(8,128)S(1)} collective-permute-done((f32[512,128]{1,0:T(8,128)S(1)}, f32[512,128]{1,0:T(8,128)S(1)}, u32[]{:S(2)}, u32[]{:S(2)}) %collective-permute-start.9) | collective-permute-done | bytes 262176 | tf_op jit(solution)/shard_map/ppermute | solution.py:512
  43.5 1.9 %collective-permute-start.13 = (f32[128,128]{1,0:T(8,128)S(1)}, f32[128,128]{1,0:T(8,128)S(1)}, u32[]{:S(2)}, u32[]{:S(2)}) collective-permute-start(f32[128,128]{1,0:T(8,128)S(1)} %get-tuple-element.65), channel_id=1, source_target_pairs={{0,5},{1,4},{2,7},{3,6},{4,1},{5,0},{6,3},{7,2},{8,13},{9,12},{10,... | collective-permute-start | bytes 196616 | tf_op jit(solution)/shard_map/ppermute | solution.py:519
  45.4 1.2 %collective-permute-start.12 = (f32[128,128]{1,0:T(8,128)S(1)}, f32[128,128]{1,0:T(8,128)S(1)}, u32[]{:S(2)}, u32[]{:S(2)}) collective-permute-start(f32[128,128]{1,0:T(8,128)S(1)} %get-tuple-element.65), channel_id=1, source_target_pairs={{0,3},{1,2},{2,1},{3,0},{4,7},{5,6},{6,5},{7,4},{8,11},{9,10},{10,... | collective-permute-start | bytes 196616 | tf_op jit(solution)/shard_map/ppermute | solution.py:519
  46.6 1.1 %collective-permute-start.11 = (f32[128,128]{1,0:T(8,128)S(1)}, f32[128,128]{1,0:T(8,128)S(1)}, u32[]{:S(2)}, u32[]{:S(2)}) collective-permute-start(f32[128,128]{1,0:T(8,128)S(1)} %get-tuple-element.65), channel_id=1, source_target_pairs={{0,1},{1,0},{2,3},{3,2},{4,5},{5,4},{6,7},{7,6},{8,9},{9,8},{10,11... | collective-permute-start | bytes 196616 | tf_op jit(solution)/shard_map/ppermute | solution.py:519
  47.7 1.7 %collective-permute-done.14 = f32[128,128]{1,0:T(8,128)S(1)} collective-permute-done((f32[128,128]{1,0:T(8,128)S(1)}, f32[128,128]{1,0:T(8,128)S(1)}, u32[]{:S(2)}, u32[]{:S(2)}) %collective-permute-start.14) | collective-permute-done | bytes 65568 | tf_op jit(solution)/shard_map/ppermute | solution.py:519
  49.4 2.2 %collective-permute-done.13 = f32[128,128]{1,0:T(8,128)S(1)} collective-permute-done((f32[128,128]{1,0:T(8,128)S(1)}, f32[128,128]{1,0:T(8,128)S(1)}, u32[]{:S(2)}, u32[]{:S(2)}) %collective-permute-start.13) | collective-permute-done | bytes 65568 | tf_op jit(solution)/shard_map/ppermute | solution.py:519
  51.6 1.4 %collective-permute-start.16 = (f32[128,128]{1,0:T(8,128)S(1)}, f32[128,128]{1,0:T(8,128)S(1)}, u32[]{:S(2)}, u32[]{:S(2)}) collective-permute-start(f32[128,128]{1,0:T(8,128)S(1)} %add_add_fusion.1), channel_id=1, source_target_pairs={{0,8},{1,17},{2,10},{3,19},{4,12},{5,21},{6,14},{7,23},{8,24},{9,1... | collective-permute-start | bytes 196616 | tf_op jit(solution)/shard_map/ppermute | solution.py:512
  53.4 1.5 %collective-permute-start.8 = (f32[512,128]{1,0:T(8,128)S(1)}, f32[512,128]{1,0:T(8,128)S(1)}, u32[]{:S(2)}, u32[]{:S(2)}) collective-permute-start(f32[512,128]{1,0:T(8,128)S(1)} %get-tuple-element.56.tail_ref), channel_id=1, source_target_pairs={{0,16},{1,9},{2,18},{3,11},{4,20},{5,13},{6,22},{7,15},{8,0},{9,25... | collective-permute-start | bytes 786440 | tf_op jit(solution)/shard_map/ppermute | solution.py:512
  54.9 1.8 %collective-permute-done.16.there_ref = f32[128,128]{1,0:T(8,128)S(1)} collective-permute-done((f32[128,128]{1,0:T(8,128)S(1)}, f32[128,128]{1,0:T(8,128)S(1)}, u32[]{:S(2)}, u32[]{:S(2)}) %collective-permute-start.16) | collective-permute-done | bytes 65568 | tf_op jit(solution)/shard_map/ppermute | solution.py:512
  56.7 2.9 %second_rotation.1.refs_6_ = f32[256,128]{1,0:T(8,128)S(1)} custom-call(f32[128,128]{1,0:T(8,128)S(1)} %get-tuple-element.57.own_gram_ref, f32[128,128]{1,0:T(8,128)S(1)} %get-tuple-element.60.far_ref, f32[128,128]{1,0:T(8,128)S(1)} %collective-permute-done.15.here_ref, f32[128,128]{1,0:T(8,128)S(1)} %collective-permute-done.16.there_ref), custom_call_target="tpu_custom_call" | custom-call | flops 11500000256 | tf_op jit(solution)/shard_map/second_rotation/pallas_call | solution.py:140
  59.7 2.0 %here_product.1.refs_5_ = f32[2,4096,128]{2,1,0:T(8,128)} custom-call(bf16[2688,256]{1,0:T(8,128)(2,1)S(1)} %get-tuple-element.67.refs_0_, bf16[2688,256]{1,0:T(8,128)(2,1)S(1)} %get-tuple-element.68.refs_1_, bf16[896,256]{1,0:T(8,128)(2,1)S(1)} %get-tuple-element.69.refs_2_, bf16[896,256]{1,0:T(8,128)(2,1)S(1)} %get-tuple-element.70.refs_3_, ...), custom_call_target="tpu_custom_call" | custom-call | tf_op jit(solution)/shard_map/here_product/pallas_call | solution.py:140
  61.7 1.9 %bulk_product.1.refs_4_ = f32[2,4096,128]{2,1,0:T(8,128)} custom-call(bf16[4096,128]{1,0:T(8,128)(2,1)S(1)} %get-tuple-element.50.refs_0_, bf16[4096,128]{1,0:T(8,128)(2,1)S(1)} %get-tuple-element.51.refs_1_, f32[3584,128]{1,0:T(8,128)S(1)} %collective-permute-done.18.refs_2_.refs_3_, ...), custom_call_target="tpu_custom_call", output_to_operand_aliasing={{}: (5, {})} | custom-call | tf_op jit(solution)/shard_map/bulk_product/pallas_call | solution.py:140
  63.6 1.0 %tail_product.1 = f32[2,4096,128]{2,1,0:T(8,128)} custom-call(bf16[4096,128]{1,0:T(8,128)(2,1)S(1)} %get-tuple-element.50.refs_0_, bf16[4096,128]{1,0:T(8,128)(2,1)S(1)} %get-tuple-element.51.refs_1_, f32[512,128]{1,0:T(8,128)S(1)} %collective-permute-done.8.refs_2_, ...), custom_call_target="tpu_custom_call", output_to_operand_aliasing={{}: (4, {})} | custom-call | tf_op jit(solution)/shard_map/tail_product/pallas_call | solution.py:140
  (25 shorter events, 3.6 us)
Async XLA Ops:
  0.0 4.6 %copy-start = (f32[2,4096,128]{2,1,0:T(8,128)S(1)}, f32[2,4096,128]{2,1,0:T(8,128)}, u32[]{:S(2)}) copy-start(f32[2,4096,128]{2,1,0:T(8,128)} %matrix_ref.9) | copy-start | bytes 12582916
  1.6 24.2 %collective-permute-start.5 = (f32[2,1792,128]{2,1,0:T(8,128)S(1)}, f32[2,1792,128]{2,1,0:T(8,128)S(1)}, u32[]{:S(2)}, u32[]{:S(2)}) collective-permute-start(f32[2,1792,128]{2,1,0:T(8,128)S(1)} %raw_rows.1), channel_id=1, source_target_pairs={{0,8},{1,17},{2,10},{3,19},{4,12},{5,21},{6,14},{7,23},{8,24},{9,1... | collective-permute-start | bytes 5505032 | tf_op jit(solution)/shard_map/ppermute | solution.py:512
  6.0 1.3 %collective-permute-start = (f32[136,128]{1,0:T(8,128)S(1)}, f32[136,128]{1,0:T(8,128)S(1)}, u32[]{:S(2)}, u32[]{:S(2)}) collective-permute-start(f32[136,128]{1,0:T(8,128)S(1)} %get-tuple-element.40), channel_id=1, source_target_pairs={{0,1},{1,0},{2,3},{3,2},{4,5},{5,4},{6,7},{7,6},{8,9},{9,8},{10,11... | collective-permute-start | bytes 208904 | tf_op jit(solution)/shard_map/ppermute | solution.py:533
  7.3 6.5 %collective-permute-start.3 = (f32[136,128]{1,0:T(8,128)S(1)}, f32[136,128]{1,0:T(8,128)S(1)}, u32[]{:S(2)}, u32[]{:S(2)}) collective-permute-start(f32[136,128]{1,0:T(8,128)S(1)} %add.21), channel_id=1, source_target_pairs={{0,6},{1,7},{2,4},{3,5},{4,2},{5,3},{6,0},{7,1},{8,14},{9,15},{10,... | collective-permute-start | bytes 208904 | tf_op jit(solution)/shard_map/ppermute | solution.py:519
  11.0 6.2 %collective-permute-start.2 = (f32[136,128]{1,0:T(8,128)S(1)}, f32[136,128]{1,0:T(8,128)S(1)}, u32[]{:S(2)}, u32[]{:S(2)}) collective-permute-start(f32[136,128]{1,0:T(8,128)S(1)} %add.21), channel_id=1, source_target_pairs={{0,4},{1,5},{2,6},{3,7},{4,0},{5,1},{6,2},{7,3},{8,12},{9,13},{10,... | collective-permute-start | bytes 208904 | tf_op jit(solution)/shard_map/ppermute | solution.py:519
  11.0 6.2 %collective-permute-start.1 = (f32[136,128]{1,0:T(8,128)S(1)}, f32[136,128]{1,0:T(8,128)S(1)}, u32[]{:S(2)}, u32[]{:S(2)}) collective-permute-start(f32[136,128]{1,0:T(8,128)S(1)} %add.21), channel_id=1, source_target_pairs={{0,2},{1,3},{2,0},{3,1},{4,6},{5,7},{6,4},{7,5},{8,10},{9,11},{10,... | collective-permute-start | bytes 208904 | tf_op jit(solution)/shard_map/ppermute | solution.py:519
  17.2 1.3 %collective-permute-start.4 = (f32[136,128]{1,0:T(8,128)S(1)}, f32[136,128]{1,0:T(8,128)S(1)}, u32[]{:S(2)}, u32[]{:S(2)}) collective-permute-start(f32[136,128]{1,0:T(8,128)S(1)} %add_add_fusion.mine_ref), channel_id=1, source_target_pairs={{0,1},{1,0},{2,3},{3,2},{4,5},{5,4},{6,7},{7,6},{8,9},{9,8},{10,11... | collective-permute-start | bytes 208904 | tf_op jit(solution)/shard_map/ppermute | solution.py:534
  22.3 9.6 %collective-permute-start.6 = (f32[1088,128]{1,0:T(8,128)S(1)}, f32[1088,128]{1,0:T(8,128)S(1)}, u32[]{:S(2)}, u32[]{:S(2)}) collective-permute-start(f32[1088,128]{1,0:T(8,128)S(1)} %small_part.1.refs_0_), channel_id=1, source_target_pairs={{0,8},{1,17},{2,10},{3,19},{4,12},{5,21},{6,14},{7,23},{8,24},{9,1... | collective-permute-start | bytes 1671176 | tf_op jit(solution)/shard_map/ppermute | solution.py:512
  26.6 13.4 %collective-permute-start.10 = (f32[896,128]{1,0:T(8,128)S(1)}, f32[896,128]{1,0:T(8,128)S(1)}, u32[]{:S(2)}, u32[]{:S(2)}) collective-permute-start(f32[896,128]{1,0:T(8,128)S(1)} %get-tuple-element.48.refs_1_), channel_id=1, source_target_pairs={{0,8},{1,17},{2,10},{3,19},{4,12},{5,21},{6,14},{7,23},{8,24},{9,1... | collective-permute-start | bytes 1376264 | tf_op jit(solution)/shard_map/ppermute | solution.py:512
  31.9 4.7 %collective-permute-start.7 = (f32[192,128]{1,0:T(8,128)S(1)}, f32[192,128]{1,0:T(8,128)S(1)}, u32[]{:S(2)}, u32[]{:S(2)}) collective-permute-start(f32[192,128]{1,0:T(8,128)S(1)} %slice.3), channel_id=1, source_target_pairs={{0,2},{1,3},{2,0},{3,1},{4,6},{5,7},{6,4},{7,5},{8,10},{9,11},{10,... | collective-permute-start | bytes 294920 | tf_op jit(solution)/shard_map/ppermute | solution.py:547
  34.0 9.1 %collective-permute-start.9 = (f32[512,128]{1,0:T(8,128)S(1)}, f32[512,128]{1,0:T(8,128)S(1)}, u32[]{:S(2)}, u32[]{:S(2)}) collective-permute-start(f32[512,128]{1,0:T(8,128)S(1)} %get-tuple-element.49.refs_2_), channel_id=1, source_target_pairs={{0,8},{1,17},{2,10},{3,19},{4,12},{5,21},{6,14},{7,23},{8,24},{9,1... | collective-permute-start | bytes 786440 | tf_op jit(solution)/shard_map/ppermute | solution.py:512
  36.6 25.2 %collective-permute-start.18 = (f32[3584,128]{1,0:T(8,128)S(1)}, f32[3584,128]{1,0:T(8,128)S(1)}, u32[]{:S(2)}, u32[]{:S(2)}) collective-permute-start(f32[3584,128]{1,0:T(8,128)S(1)} %get-tuple-element.66.bulk_ref), channel_id=1, source_target_pairs={{0,16},{1,9},{2,18},{3,11},{4,20},{5,13},{6,22},{7,15},{8,0},{9,25... | collective-permute-start | bytes 5505032 | tf_op jit(solution)/shard_map/ppermute | solution.py:512
  43.4 6.0 %collective-permute-start.14 = (f32[128,128]{1,0:T(8,128)S(1)}, f32[128,128]{1,0:T(8,128)S(1)}, u32[]{:S(2)}, u32[]{:S(2)}) collective-permute-start(f32[128,128]{1,0:T(8,128)S(1)} %get-tuple-element.65), channel_id=1, source_target_pairs={{0,7},{1,6},{2,5},{3,4},{4,3},{5,2},{6,1},{7,0},{8,15},{9,14},{10,... | collective-permute-start | bytes 196616 | tf_op jit(solution)/shard_map/ppermute | solution.py:519
  43.5 8.1 %collective-permute-start.13 = (f32[128,128]{1,0:T(8,128)S(1)}, f32[128,128]{1,0:T(8,128)S(1)}, u32[]{:S(2)}, u32[]{:S(2)}) collective-permute-start(f32[128,128]{1,0:T(8,128)S(1)} %get-tuple-element.65), channel_id=1, source_target_pairs={{0,5},{1,4},{2,7},{3,6},{4,1},{5,0},{6,3},{7,2},{8,13},{9,12},{10,... | collective-permute-start | bytes 196616 | tf_op jit(solution)/shard_map/ppermute | solution.py:519
  45.4 6.2 %collective-permute-start.12 = (f32[128,128]{1,0:T(8,128)S(1)}, f32[128,128]{1,0:T(8,128)S(1)}, u32[]{:S(2)}, u32[]{:S(2)}) collective-permute-start(f32[128,128]{1,0:T(8,128)S(1)} %get-tuple-element.65), channel_id=1, source_target_pairs={{0,3},{1,2},{2,1},{3,0},{4,7},{5,6},{6,5},{7,4},{8,11},{9,10},{10,... | collective-permute-start | bytes 196616 | tf_op jit(solution)/shard_map/ppermute | solution.py:519
  46.6 5.0 %collective-permute-start.11 = (f32[128,128]{1,0:T(8,128)S(1)}, f32[128,128]{1,0:T(8,128)S(1)}, u32[]{:S(2)}, u32[]{:S(2)}) collective-permute-start(f32[128,128]{1,0:T(8,128)S(1)} %get-tuple-element.65), channel_id=1, source_target_pairs={{0,1},{1,0},{2,3},{3,2},{4,5},{5,4},{6,7},{7,6},{8,9},{9,8},{10,11... | collective-permute-start | bytes 196616 | tf_op jit(solution)/shard_map/ppermute | solution.py:519
  51.6 5.1 %collective-permute-start.16 = (f32[128,128]{1,0:T(8,128)S(1)}, f32[128,128]{1,0:T(8,128)S(1)}, u32[]{:S(2)}, u32[]{:S(2)}) collective-permute-start(f32[128,128]{1,0:T(8,128)S(1)} %add_add_fusion.1), channel_id=1, source_target_pairs={{0,8},{1,17},{2,10},{3,19},{4,12},{5,21},{6,14},{7,23},{8,24},{9,1... | collective-permute-start | bytes 196616 | tf_op jit(solution)/shard_map/ppermute | solution.py:512
  53.1 3.6 %collective-permute-start.15 = (f32[128,128]{1,0:T(8,128)S(1)}, f32[128,128]{1,0:T(8,128)S(1)}, u32[]{:S(2)}, u32[]{:S(2)}) collective-permute-start(f32[128,128]{1,0:T(8,128)S(1)} %add_add_fusion.1), channel_id=1, source_target_pairs={{0,1},{1,0},{2,3},{3,2},{4,5},{5,4},{6,7},{7,6},{8,9},{9,8},{10,11... | collective-permute-start | bytes 196616 | tf_op jit(solution)/shard_map/ppermute | solution.py:559
  53.4 10.2 %collective-permute-start.8 = (f32[512,128]{1,0:T(8,128)S(1)}, f32[512,128]{1,0:T(8,128)S(1)}, u32[]{:S(2)}, u32[]{:S(2)}) collective-permute-start(f32[512,128]{1,0:T(8,128)S(1)} %get-tuple-element.56.tail_ref), channel_id=1, source_target_pairs={{0,16},{1,9},{2,18},{3,11},{4,20},{5,13},{6,22},{7,15},{8,0},{9,25... | collective-permute-start | bytes 786440 | tf_op jit(solution)/shard_map/ppermute | solution.py:512
  59.6 2.1 %collective-permute-start.17 = (f32[256,128]{1,0:T(8,128)S(1)}, f32[256,128]{1,0:T(8,128)S(1)}, u32[]{:S(2)}, u32[]{:S(2)}) collective-permute-start(f32[256,128]{1,0:T(8,128)S(1)} %second_rotation.1.refs_6_), channel_id=1, source_target_pairs={{0,1},{1,0},{2,3},{3,2},{4,5},{5,4},{6,7},{7,6},{8,9},{9,8},{10,11... | collective-permute-start | bytes 393224 | tf_op jit(solution)/shard_map/ppermute | solution.py:561

commit v8 on v7

--- a/solution.py
+++ b/solution.py
@@ -251,7 +251,7 @@
 def first_rotation(mine, other):
     width = mine.shape[1]
 
-    def kernel(mine_ref, other_ref, first_ref, second_ref, gram_ref):
+    def kernel(mine_ref, other_ref, first_ref, base_ref, half_ref, gram_ref):
         holds_cross = core_of() == 0
         mine, other = mine_ref[...], other_ref[...]
         cross = jnp.where(holds_cross, mine[:width], other[:width])
@@ -267,10 +267,12 @@
         upper_first = first_is_upper()
         gram_ref[...] = gram
         first_ref[...] = rows_product(first, right_parts(jnp.where(upper_first, left, right)))
-        second_ref[...] = rows_product(first, right_parts(jnp.where(upper_first, right, left)))
+        base_ref[...] = first
+        half_ref[...] = jnp.where(upper_first, right, left)
 
     half = ((2 * width, width), HERE)
-    return call(kernel, [half, half, ((2 * width, 2 * width), HERE)], [(mine, HERE), (other, HERE)], "first_rotation")
+    square = ((2 * width, 2 * width), HERE)
+    return call(kernel, [half, square, half, square], [(mine, HERE), (other, HERE)], "first_rotation")
 
 
 def share_of():
@@ -307,23 +309,25 @@
     )[0]
 
 
-def sent_parts(matrix, early, first, second, gram, small, last, step):
+def sent_parts(matrix, early, first, base, half, gram, small, last, step):
     width = first.shape[1]
     count = matrix.shape[1] - early
 
-    def kernel(matrix_ref, first_ref, second_ref, gram_ref, main_ref, last_ref, second_gram_ref):
+    def kernel(matrix_ref, first_ref, base_ref, half_ref, gram_ref, main_ref, last_ref, second_ref, second_gram_ref):
         local = Rows((matrix_ref, -early, matrix.shape[1], 0))
         out = Rows((main_ref, small, count - small - last, 0), (last_ref, count - last, last, 0))
         parts = right_parts(first_ref[...])
         for start, number in spans(small, count, step, count - last):
             ref, place = out.at(start, number)
             ref[place, :] = rows_product(local.pair(start, number), parts)
-        second_gram_ref[...] = rotated_gram(gram_ref[...], second_ref[...])
-
-    return call(
-        kernel,
-        [((count - small - last, width), HERE), ((last, width), HERE), ((width, width), HERE)],
-        [(matrix, HERE), (first, HERE), (second, HERE), (gram, HERE)],
+        second = rows_product(base_ref[...], right_parts(half_ref[...]))
+        second_ref[...] = second
+        second_gram_ref[...] = rotated_gram(gram_ref[...], second)
+
+    return call(
+        kernel,
+        [((count - small - last, width), HERE), ((last, width), HERE), ((2 * width, width), HERE), ((width, width), HERE)],
+        [(part, HERE) for part in (matrix, first, base, half, gram)],
         "sent_parts",
         12 * count * width * width,
     )
@@ -532,12 +536,12 @@
     keep, give = local_gram(matrix, step)
     mine = chip_sum(keep + lax.ppermute(give, "row", core), 4)
     other = lax.ppermute(mine, "row", core)
-    turn_first, turn_second, gram = first_rotation(mine, other)
+    turn_first, base, half, gram = first_rotation(mine, other)
 
     sent_small = small_part(matrix, early, turn_first, gram, small, step)
     far_small = travel(sent_small, outward)
     turn_main, sent_small, far_raw = lax.optimization_barrier((turn_first, sent_small, far_raw))
-    sent_main, sent_last, second_gram = sent_parts(matrix, early, turn_main, turn_second, gram, small, last, step)
+    sent_main, sent_last, turn_second, second_gram = sent_parts(matrix, early, turn_main, base, half, gram, small, last, step)
     far_main, far_last = travel(sent_main, outward), travel(sent_last, outward)
     turn_second, sent_main = lax.optimization_barrier((turn_second, sent_main))
     sent = [(sent_small, early, small, offset), (sent_main, early + small, main, 0), (sent_last, rows - last, last, 0)]

time: 64.9 us -> 65 us (level)
  no operation moved by 1% of the time
where the time goes in v8:
time: 65 us; the launch traced here: 64.8 us
  starting transfers between devices  24.4 us (38%)
  waiting for transfers between devices  20.7 us (32%)
  Pallas kernels  19.4 us (30%)
    pallas_call x13, Pallas kernels, call(): pl.pallas_call(kernel, in_specs=[pl.BlockSpec(memory_space=place) for pla...  19.4 us
    ppermute x7, starting transfers between devices, travel(): return lax.ppermute(block, ('pair', 'row'), moves)  12.9 us
    ppermute x7, waiting for transfers between devices, chip_sum(): lax.ppermute(block, 'row', [(r, r ^ d) for r in range(rows_count)])  9.37 us
    ppermute x7, starting transfers between devices, chip_sum(): lax.ppermute(block, 'row', [(r, r ^ d) for r in range(rows_count)])  8.73 us
    ppermute x7, waiting for transfers between devices, travel(): return lax.ppermute(block, ('pair', 'row'), moves)  7.7 us
    ppermute x1, starting transfers between devices, body(): lax.ppermute(far_small[:offset], 'row', [(r, r ^ 2) for r in range(rows_c...  2.14 us
  transfers between devices with their start and end apart: 19, of which 11 were waited for; matrix products, arithmetic and copies ran while one was open for 0% of the time, Pallas kernels for 26%

profile of v8, /device:TPU:0, one launch (start us, length us, event | category | flops | bytes accessed | tf_op | source)
XLA Modules:
  0.0 64.8 jit_solution(3615960607098196997)
XLA Ops:
  0.0 1.6 %raw_rows.1 = f32[2,1792,128]{2,1,0:T(8,128)S(1)} custom-call(f32[2,4096,128]{2,1,0:T(8,128)} %matrix_ref.9), custom_call_target="tpu_custom_call" | custom-call | tf_op jit(solution)/shard_map/raw_rows/pallas_call | solution.py:140
  1.6 3.0 %collective-permute-start.5 = (f32[2,1792,128]{2,1,0:T(8,128)S(1)}, f32[2,1792,128]{2,1,0:T(8,128)S(1)}, u32[]{:S(2)}, u32[]{:S(2)}) collective-permute-start(f32[2,1792,128]{2,1,0:T(8,128)S(1)} %raw_rows.1), channel_id=1, source_target_pairs={{0,8},{1,17},{2,10},{3,19},{4,12},{5,21},{6,14},{7,23},{8,24},{9,1... | collective-permute-start | bytes 5505032 | tf_op jit(solution)/shard_map/ppermute | solution.py:516
  4.6 1.4 %gram.1 = (f32[136,128]{1,0:T(8,128)S(1)}, f32[136,128]{1,0:T(8,128)S(1)}) custom-call(f32[2,4096,128]{2,1,0:T(8,128)S(1)} %copy-done), custom_call_target="tpu_custom_call" | custom-call | tf_op jit(solution)/shard_map/gram/pallas_call | solution.py:140
  6.1 1.2 %collective-permute-done = f32[136,128]{1,0:T(8,128)S(1)} collective-permute-done((f32[136,128]{1,0:T(8,128)S(1)}, f32[136,128]{1,0:T(8,128)S(1)}, u32[]{:S(2)}, u32[]{:S(2)}) %collective-permute-start) | collective-permute-done | bytes 69664 | tf_op jit(solution)/shard_map/ppermute | solution.py:537
  7.3 3.7 %collective-permute-start.3 = (f32[136,128]{1,0:T(8,128)S(1)}, f32[136,128]{1,0:T(8,128)S(1)}, u32[]{:S(2)}, u32[]{:S(2)}) collective-permute-start(f32[136,128]{1,0:T(8,128)S(1)} %add.21), channel_id=1, source_target_pairs={{0,6},{1,7},{2,4},{3,5},{4,2},{5,3},{6,0},{7,1},{8,14},{9,15},{10,... | collective-permute-start | bytes 208904 | tf_op jit(solution)/shard_map/ppermute | solution.py:523
  11.8 2.1 %collective-permute-done.3 = f32[136,128]{1,0:T(8,128)S(1)} collective-permute-done((f32[136,128]{1,0:T(8,128)S(1)}, f32[136,128]{1,0:T(8,128)S(1)}, u32[]{:S(2)}, u32[]{:S(2)}) %collective-permute-start.3) | collective-permute-done | bytes 69664 | tf_op jit(solution)/shard_map/ppermute | solution.py:523
  13.8 3.4 %collective-permute-done.2 = f32[136,128]{1,0:T(8,128)S(1)} collective-permute-done((f32[136,128]{1,0:T(8,128)S(1)}, f32[136,128]{1,0:T(8,128)S(1)}, u32[]{:S(2)}, u32[]{:S(2)}) %collective-permute-start.2) | collective-permute-done | bytes 69664 | tf_op jit(solution)/shard_map/ppermute | solution.py:523
  17.3 1.2 %collective-permute-done.4.other_ref = f32[136,128]{1,0:T(8,128)S(1)} collective-permute-done((f32[136,128]{1,0:T(8,128)S(1)}, f32[136,128]{1,0:T(8,128)S(1)}, u32[]{:S(2)}, u32[]{:S(2)}) %collective-permute-start.4) | collective-permute-done | bytes 69664 | tf_op jit(solution)/shard_map/ppermute | solution.py:538
  18.6 3.0 %first_rotation.1 = (f32[256,128]{1,0:T(8,128)S(1)}, f32[256,256]{1,0:T(8,128)S(1)}, f32[256,128]{1,0:T(8,128)S(1)}, f32[256,256]{1,0:T(8,128)S(1)}) custom-call(f32[136,128]{1,0:T(8,128)S(1)} %add_add_fusion.mine_ref, f32[136,128]{1,0:T(8,128)S(1)} %collective-permute-done.4.other_ref), custom_call_target="tpu_custom_call" | custom-call | tf_op jit(solution)/shard_map/first_rotation/pallas_call | solution.py:140
  22.2 1.6 %collective-permute-start.6 = (f32[1088,128]{1,0:T(8,128)S(1)}, f32[1088,128]{1,0:T(8,128)S(1)}, u32[]{:S(2)}, u32[]{:S(2)}) collective-permute-start(f32[1088,128]{1,0:T(8,128)S(1)} %small_part.1.refs_0_), channel_id=1, source_target_pairs={{0,8},{1,17},{2,10},{3,19},{4,12},{5,21},{6,14},{7,23},{8,24},{9,1... | collective-permute-start | bytes 1671176 | tf_op jit(solution)/shard_map/ppermute | solution.py:516
  23.8 2.1 %collective-permute-done.5.raw_ref = f32[2,1792,128]{2,1,0:T(8,128)S(1)} collective-permute-done((f32[2,1792,128]{2,1,0:T(8,128)S(1)}, f32[2,1792,128]{2,1,0:T(8,128)S(1)}, u32[]{:S(2)}, u32[]{:S(2)}) %collective-permute-start.5) | collective-permute-done | bytes 1835040 | tf_op jit(solution)/shard_map/ppermute | solution.py:516
  25.9 1.0 %sent_parts.1 = (f32[896,128]{1,0:T(8,128)S(1)}, f32[512,128]{1,0:T(8,128)S(1)}, f32[256,128]{1,0:T(8,128)S(1)}, f32[128,128]{1,0:T(8,128)S(1)}) custom-call(f32[2,4096,128]{2,1,0:T(8,128)S(1)} %copy-done, f32[256,128]{1,0:T(8,128)S(1)} %get-tuple-element.45.turn_ref.first_ref, f32[256,256]{1,0:T(8,128)S(1)} %get-tuple-element.46.base_ref, ...), custom_call_target="tpu_custom_call" | custom-call | tf_op jit(solution)/shard_map/sent_parts/pallas_call | solution.py:140
  26.9 2.0 %collective-permute-start.10 = (f32[896,128]{1,0:T(8,128)S(1)}, f32[896,128]{1,0:T(8,128)S(1)}, u32[]{:S(2)}, u32[]{:S(2)}) collective-permute-start(f32[896,128]{1,0:T(8,128)S(1)} %get-tuple-element.52.refs_1_), channel_id=1, source_target_pairs={{0,8},{1,17},{2,10},{3,19},{4,12},{5,21},{6,14},{7,23},{8,24},{9,1... | collective-permute-start | bytes 1376264 | tf_op jit(solution)/shard_map/ppermute | solution.py:516
  28.9 1.9 %rest_parts.1 = (f32[3584,128]{1,0:T(8,128)S(1)}, f32[512,128]{1,0:T(8,128)S(1)}, bf16[4096,128]{1,0:T(8,128)(2,1)S(1)}, bf16[4096,128]{1,0:T(8,128)(2,1)S(1)}) custom-call(f32[2,4096,128]{2,1,0:T(8,128)S(1)} %copy-done, f32[256,128]{1,0:T(8,128)S(1)} %get-tuple-element.45.turn_ref.first_ref, f32[256,128]{1,0:T(8,128)S(1)} %get-tuple-element.50.second_ref, ...), custom_call_target="tpu_custom_call" | custom-call | tf_op jit(solution)/shard_map/rest_parts/pallas_call | solution.py:140
  30.8 1.0 %collective-permute-done.6.small_ref = f32[1088,128]{1,0:T(8,128)S(1)} collective-permute-done((f32[1088,128]{1,0:T(8,128)S(1)}, f32[1088,128]{1,0:T(8,128)S(1)}, u32[]{:S(2)}, u32[]{:S(2)}) %collective-permute-start.6) | collective-permute-done | bytes 557088 | tf_op jit(solution)/shard_map/ppermute | solution.py:516
  31.8 2.1 %collective-permute-start.7 = (f32[192,128]{1,0:T(8,128)S(1)}, f32[192,128]{1,0:T(8,128)S(1)}, u32[]{:S(2)}, u32[]{:S(2)}) collective-permute-start(f32[192,128]{1,0:T(8,128)S(1)} %slice.3), channel_id=1, source_target_pairs={{0,2},{1,3},{2,0},{3,1},{4,6},{5,7},{6,4},{7,5},{8,10},{9,11},{10,... | collective-permute-start | bytes 294920 | tf_op jit(solution)/shard_map/ppermute | solution.py:551
  34.0 1.5 %collective-permute-start.9 = (f32[512,128]{1,0:T(8,128)S(1)}, f32[512,128]{1,0:T(8,128)S(1)}, u32[]{:S(2)}, u32[]{:S(2)}) collective-permute-start(f32[512,128]{1,0:T(8,128)S(1)} %get-tuple-element.53.refs_2_), channel_id=1, source_target_pairs={{0,8},{1,17},{2,10},{3,19},{4,12},{5,21},{6,14},{7,23},{8,24},{9,1... | collective-permute-start | bytes 786440 | tf_op jit(solution)/shard_map/ppermute | solution.py:516
  35.5 1.1 %collective-permute-done.7.share_ref = f32[192,128]{1,0:T(8,128)S(1)} collective-permute-done((f32[192,128]{1,0:T(8,128)S(1)}, f32[192,128]{1,0:T(8,128)S(1)}, u32[]{:S(2)}, u32[]{:S(2)}) %collective-permute-start.7) | collective-permute-done | bytes 98336 | tf_op jit(solution)/shard_map/ppermute | solution.py:551
  36.6 2.0 %collective-permute-start.18 = (f32[3584,128]{1,0:T(8,128)S(1)}, f32[3584,128]{1,0:T(8,128)S(1)}, u32[]{:S(2)}, u32[]{:S(2)}) collective-permute-start(f32[3584,128]{1,0:T(8,128)S(1)} %get-tuple-element.70.bulk_ref), channel_id=1, source_target_pairs={{0,16},{1,9},{2,18},{3,11},{4,20},{5,13},{6,22},{7,15},{8,0},{9,25... | collective-permute-start | bytes 5505032 | tf_op jit(solution)/shard_map/ppermute | solution.py:516
  38.5 1.5 %raw_cross.1 = (bf16[2688,256]{1,0:T(8,128)(2,1)S(1)}, bf16[2688,256]{1,0:T(8,128)(2,1)S(1)}, f32[128,128]{1,0:T(8,128)S(1)}, f32[128,128]{1,0:T(8,128)S(1)}) custom-call(f32[2,1792,128]{2,1,0:T(8,128)S(1)} %collective-permute-done.5.raw_ref, f32[1088,128]{1,0:T(8,128)S(1)} %collective-permute-done.6.small_ref, ...), custom_call_target="tpu_custom_call" | custom-call | tf_op jit(solution)/shard_map/raw_cross/pallas_call | solution.py:140
  40.4 2.7 %collective-permute-done.9.far_ref = f32[512,128]{1,0:T(8,128)S(1)} collective-permute-done((f32[512,128]{1,0:T(8,128)S(1)}, f32[512,128]{1,0:T(8,128)S(1)}, u32[]{:S(2)}, u32[]{:S(2)}) %collective-permute-start.9) | collective-permute-done | bytes 262176 | tf_op jit(solution)/shard_map/ppermute | solution.py:516
  43.5 1.9 %collective-permute-start.13 = (f32[128,128]{1,0:T(8,128)S(1)}, f32[128,128]{1,0:T(8,128)S(1)}, u32[]{:S(2)}, u32[]{:S(2)}) collective-permute-start(f32[128,128]{1,0:T(8,128)S(1)} %get-tuple-element.69), channel_id=1, source_target_pairs={{0,5},{1,4},{2,7},{3,6},{4,1},{5,0},{6,3},{7,2},{8,13},{9,12},{10,... | collective-permute-start | bytes 196616 | tf_op jit(solution)/shard_map/ppermute | solution.py:523
  45.4 1.2 %collective-permute-start.12 = (f32[128,128]{1,0:T(8,128)S(1)}, f32[128,128]{1,0:T(8,128)S(1)}, u32[]{:S(2)}, u32[]{:S(2)}) collective-permute-start(f32[128,128]{1,0:T(8,128)S(1)} %get-tuple-element.69), channel_id=1, source_target_pairs={{0,3},{1,2},{2,1},{3,0},{4,7},{5,6},{6,5},{7,4},{8,11},{9,10},{10,... | collective-permute-start | bytes 196616 | tf_op jit(solution)/shard_map/ppermute | solution.py:523
  46.6 1.1 %collective-permute-start.11 = (f32[128,128]{1,0:T(8,128)S(1)}, f32[128,128]{1,0:T(8,128)S(1)}, u32[]{:S(2)}, u32[]{:S(2)}) collective-permute-start(f32[128,128]{1,0:T(8,128)S(1)} %get-tuple-element.69), channel_id=1, source_target_pairs={{0,1},{1,0},{2,3},{3,2},{4,5},{5,4},{6,7},{7,6},{8,9},{9,8},{10,11... | collective-permute-start | bytes 196616 | tf_op jit(solution)/shard_map/ppermute | solution.py:523
  47.7 1.7 %collective-permute-done.14 = f32[128,128]{1,0:T(8,128)S(1)} collective-permute-done((f32[128,128]{1,0:T(8,128)S(1)}, f32[128,128]{1,0:T(8,128)S(1)}, u32[]{:S(2)}, u32[]{:S(2)}) %collective-permute-start.14) | collective-permute-done | bytes 65568 | tf_op jit(solution)/shard_map/ppermute | solution.py:523
  49.4 2.3 %collective-permute-done.13 = f32[128,128]{1,0:T(8,128)S(1)} collective-permute-done((f32[128,128]{1,0:T(8,128)S(1)}, f32[128,128]{1,0:T(8,128)S(1)}, u32[]{:S(2)}, u32[]{:S(2)}) %collective-permute-start.13) | collective-permute-done | bytes 65568 | tf_op jit(solution)/shard_map/ppermute | solution.py:523
  51.7 1.4 %collective-permute-start.16 = (f32[128,128]{1,0:T(8,128)S(1)}, f32[128,128]{1,0:T(8,128)S(1)}, u32[]{:S(2)}, u32[]{:S(2)}) collective-permute-start(f32[128,128]{1,0:T(8,128)S(1)} %add_add_fusion.1), channel_id=1, source_target_pairs={{0,8},{1,17},{2,10},{3,19},{4,12},{5,21},{6,14},{7,23},{8,24},{9,1... | collective-permute-start | bytes 196616 | tf_op jit(solution)/shard_map/ppermute | solution.py:516
  53.4 1.5 %collective-permute-start.8 = (f32[512,128]{1,0:T(8,128)S(1)}, f32[512,128]{1,0:T(8,128)S(1)}, u32[]{:S(2)}, u32[]{:S(2)}) collective-permute-start(f32[512,128]{1,0:T(8,128)S(1)} %get-tuple-element.60.tail_ref), channel_id=1, source_target_pairs={{0,16},{1,9},{2,18},{3,11},{4,20},{5,13},{6,22},{7,15},{8,0},{9,25... | collective-permute-start | bytes 786440 | tf_op jit(solution)/shard_map/ppermute | solution.py:516
  54.9 1.9 %collective-permute-done.16.there_ref = f32[128,128]{1,0:T(8,128)S(1)} collective-permute-done((f32[128,128]{1,0:T(8,128)S(1)}, f32[128,128]{1,0:T(8,128)S(1)}, u32[]{:S(2)}, u32[]{:S(2)}) %collective-permute-start.16) | collective-permute-done | bytes 65568 | tf_op jit(solution)/shard_map/ppermute | solution.py:516
  56.8 2.9 %second_rotation.1.refs_6_ = f32[256,128]{1,0:T(8,128)S(1)} custom-call(f32[128,128]{1,0:T(8,128)S(1)} %get-tuple-element.61.own_gram_ref, f32[128,128]{1,0:T(8,128)S(1)} %get-tuple-element.64.far_ref, f32[128,128]{1,0:T(8,128)S(1)} %collective-permute-done.15.here_ref, f32[128,128]{1,0:T(8,128)S(1)} %collective-permute-done.16.there_ref), custom_call_target="tpu_custom_call" | custom-call | flops 11500000256 | tf_op jit(solution)/shard_map/second_rotation/pallas_call | solution.py:140
  59.8 2.0 %here_product.1.refs_5_ = f32[2,4096,128]{2,1,0:T(8,128)} custom-call(bf16[2688,256]{1,0:T(8,128)(2,1)S(1)} %get-tuple-element.71.refs_0_, bf16[2688,256]{1,0:T(8,128)(2,1)S(1)} %get-tuple-element.72.refs_1_, bf16[896,256]{1,0:T(8,128)(2,1)S(1)} %get-tuple-element.73.refs_2_, bf16[896,256]{1,0:T(8,128)(2,1)S(1)} %get-tuple-element.74.refs_3_, ...), custom_call_target="tpu_custom_call" | custom-call | tf_op jit(solution)/shard_map/here_product/pallas_call | solution.py:140
  61.8 1.9 %bulk_product.1.refs_4_ = f32[2,4096,128]{2,1,0:T(8,128)} custom-call(bf16[4096,128]{1,0:T(8,128)(2,1)S(1)} %get-tuple-element.54.refs_0_, bf16[4096,128]{1,0:T(8,128)(2,1)S(1)} %get-tuple-element.55.refs_1_, f32[3584,128]{1,0:T(8,128)S(1)} %collective-permute-done.18.refs_2_.refs_3_, ...), custom_call_target="tpu_custom_call", output_to_operand_aliasing={{}: (5, {})} | custom-call | tf_op jit(solution)/shard_map/bulk_product/pallas_call | solution.py:140
  (25 shorter events, 3.7 us)
Async XLA Ops:
  0.0 4.6 %copy-start = (f32[2,4096,128]{2,1,0:T(8,128)S(1)}, f32[2,4096,128]{2,1,0:T(8,128)}, u32[]{:S(2)}) copy-start(f32[2,4096,128]{2,1,0:T(8,128)} %matrix_ref.9) | copy-start | bytes 12582916
  1.6 24.2 %collective-permute-start.5 = (f32[2,1792,128]{2,1,0:T(8,128)S(1)}, f32[2,1792,128]{2,1,0:T(8,128)S(1)}, u32[]{:S(2)}, u32[]{:S(2)}) collective-permute-start(f32[2,1792,128]{2,1,0:T(8,128)S(1)} %raw_rows.1), channel_id=1, source_target_pairs={{0,8},{1,17},{2,10},{3,19},{4,12},{5,21},{6,14},{7,23},{8,24},{9,1... | collective-permute-start | bytes 5505032 | tf_op jit(solution)/shard_map/ppermute | solution.py:516
  6.0 1.3 %collective-permute-start = (f32[136,128]{1,0:T(8,128)S(1)}, f32[136,128]{1,0:T(8,128)S(1)}, u32[]{:S(2)}, u32[]{:S(2)}) collective-permute-start(f32[136,128]{1,0:T(8,128)S(1)} %get-tuple-element.42), channel_id=1, source_target_pairs={{0,1},{1,0},{2,3},{3,2},{4,5},{5,4},{6,7},{7,6},{8,9},{9,8},{10,11... | collective-permute-start | bytes 208904 | tf_op jit(solution)/shard_map/ppermute | solution.py:537
  7.3 6.5 %collective-permute-start.3 = (f32[136,128]{1,0:T(8,128)S(1)}, f32[136,128]{1,0:T(8,128)S(1)}, u32[]{:S(2)}, u32[]{:S(2)}) collective-permute-start(f32[136,128]{1,0:T(8,128)S(1)} %add.21), channel_id=1, source_target_pairs={{0,6},{1,7},{2,4},{3,5},{4,2},{5,3},{6,0},{7,1},{8,14},{9,15},{10,... | collective-permute-start | bytes 208904 | tf_op jit(solution)/shard_map/ppermute | solution.py:523
  11.0 6.2 %collective-permute-start.2 = (f32[136,128]{1,0:T(8,128)S(1)}, f32[136,128]{1,0:T(8,128)S(1)}, u32[]{:S(2)}, u32[]{:S(2)}) collective-permute-start(f32[136,128]{1,0:T(8,128)S(1)} %add.21), channel_id=1, source_target_pairs={{0,4},{1,5},{2,6},{3,7},{4,0},{5,1},{6,2},{7,3},{8,12},{9,13},{10,... | collective-permute-start | bytes 208904 | tf_op jit(solution)/shard_map/ppermute | solution.py:523
  11.0 6.2 %collective-permute-start.1 = (f32[136,128]{1,0:T(8,128)S(1)}, f32[136,128]{1,0:T(8,128)S(1)}, u32[]{:S(2)}, u32[]{:S(2)}) collective-permute-start(f32[136,128]{1,0:T(8,128)S(1)} %add.21), channel_id=1, source_target_pairs={{0,2},{1,3},{2,0},{3,1},{4,6},{5,7},{6,4},{7,5},{8,10},{9,11},{10,... | collective-permute-start | bytes 208904 | tf_op jit(solution)/shard_map/ppermute | solution.py:523
  17.2 1.3 %collective-permute-start.4 = (f32[136,128]{1,0:T(8,128)S(1)}, f32[136,128]{1,0:T(8,128)S(1)}, u32[]{:S(2)}, u32[]{:S(2)}) collective-permute-start(f32[136,128]{1,0:T(8,128)S(1)} %add_add_fusion.mine_ref), channel_id=1, source_target_pairs={{0,1},{1,0},{2,3},{3,2},{4,5},{5,4},{6,7},{7,6},{8,9},{9,8},{10,11... | collective-permute-start | bytes 208904 | tf_op jit(solution)/shard_map/ppermute | solution.py:538
  22.2 9.6 %collective-permute-start.6 = (f32[1088,128]{1,0:T(8,128)S(1)}, f32[1088,128]{1,0:T(8,128)S(1)}, u32[]{:S(2)}, u32[]{:S(2)}) collective-permute-start(f32[1088,128]{1,0:T(8,128)S(1)} %small_part.1.refs_0_), channel_id=1, source_target_pairs={{0,8},{1,17},{2,10},{3,19},{4,12},{5,21},{6,14},{7,23},{8,24},{9,1... | collective-permute-start | bytes 1671176 | tf_op jit(solution)/shard_map/ppermute | solution.py:516
  26.9 13.2 %collective-permute-start.10 = (f32[896,128]{1,0:T(8,128)S(1)}, f32[896,128]{1,0:T(8,128)S(1)}, u32[]{:S(2)}, u32[]{:S(2)}) collective-permute-start(f32[896,128]{1,0:T(8,128)S(1)} %get-tuple-element.52.refs_1_), channel_id=1, source_target_pairs={{0,8},{1,17},{2,10},{3,19},{4,12},{5,21},{6,14},{7,23},{8,24},{9,1... | collective-permute-start | bytes 1376264 | tf_op jit(solution)/shard_map/ppermute | solution.py:516
  31.8 4.7 %collective-permute-start.7 = (f32[192,128]{1,0:T(8,128)S(1)}, f32[192,128]{1,0:T(8,128)S(1)}, u32[]{:S(2)}, u32[]{:S(2)}) collective-permute-start(f32[192,128]{1,0:T(8,128)S(1)} %slice.3), channel_id=1, source_target_pairs={{0,2},{1,3},{2,0},{3,1},{4,6},{5,7},{6,4},{7,5},{8,10},{9,11},{10,... | collective-permute-start | bytes 294920 | tf_op jit(solution)/shard_map/ppermute | solution.py:551
  34.0 9.1 %collective-permute-start.9 = (f32[512,128]{1,0:T(8,128)S(1)}, f32[512,128]{1,0:T(8,128)S(1)}, u32[]{:S(2)}, u32[]{:S(2)}) collective-permute-start(f32[512,128]{1,0:T(8,128)S(1)} %get-tuple-element.53.refs_2_), channel_id=1, source_target_pairs={{0,8},{1,17},{2,10},{3,19},{4,12},{5,21},{6,14},{7,23},{8,24},{9,1... | collective-permute-start | bytes 786440 | tf_op jit(solution)/shard_map/ppermute | solution.py:516
  36.6 25.2 %collective-permute-start.18 = (f32[3584,128]{1,0:T(8,128)S(1)}, f32[3584,128]{1,0:T(8,128)S(1)}, u32[]{:S(2)}, u32[]{:S(2)}) collective-permute-start(f32[3584,128]{1,0:T(8,128)S(1)} %get-tuple-element.70.bulk_ref), channel_id=1, source_target_pairs={{0,16},{1,9},{2,18},{3,11},{4,20},{5,13},{6,22},{7,15},{8,0},{9,25... | collective-permute-start | bytes 5505032 | tf_op jit(solution)/shard_map/ppermute | solution.py:516
  43.4 6.0 %collective-permute-start.14 = (f32[128,128]{1,0:T(8,128)S(1)}, f32[128,128]{1,0:T(8,128)S(1)}, u32[]{:S(2)}, u32[]{:S(2)}) collective-permute-start(f32[128,128]{1,0:T(8,128)S(1)} %get-tuple-element.69), channel_id=1, source_target_pairs={{0,7},{1,6},{2,5},{3,4},{4,3},{5,2},{6,1},{7,0},{8,15},{9,14},{10,... | collective-permute-start | bytes 196616 | tf_op jit(solution)/shard_map/ppermute | solution.py:523
  43.5 8.2 %collective-permute-start.13 = (f32[128,128]{1,0:T(8,128)S(1)}, f32[128,128]{1,0:T(8,128)S(1)}, u32[]{:S(2)}, u32[]{:S(2)}) collective-permute-start(f32[128,128]{1,0:T(8,128)S(1)} %get-tuple-element.69), channel_id=1, source_target_pairs={{0,5},{1,4},{2,7},{3,6},{4,1},{5,0},{6,3},{7,2},{8,13},{9,12},{10,... | collective-permute-start | bytes 196616 | tf_op jit(solution)/shard_map/ppermute | solution.py:523
  45.4 6.2 %collective-permute-start.12 = (f32[128,128]{1,0:T(8,128)S(1)}, f32[128,128]{1,0:T(8,128)S(1)}, u32[]{:S(2)}, u32[]{:S(2)}) collective-permute-start(f32[128,128]{1,0:T(8,128)S(1)} %get-tuple-element.69), channel_id=1, source_target_pairs={{0,3},{1,2},{2,1},{3,0},{4,7},{5,6},{6,5},{7,4},{8,11},{9,10},{10,... | collective-permute-start | bytes 196616 | tf_op jit(solution)/shard_map/ppermute | solution.py:523
  46.6 5.0 %collective-permute-start.11 = (f32[128,128]{1,0:T(8,128)S(1)}, f32[128,128]{1,0:T(8,128)S(1)}, u32[]{:S(2)}, u32[]{:S(2)}) collective-permute-start(f32[128,128]{1,0:T(8,128)S(1)} %get-tuple-element.69), channel_id=1, source_target_pairs={{0,1},{1,0},{2,3},{3,2},{4,5},{5,4},{6,7},{7,6},{8,9},{9,8},{10,11... | collective-permute-start | bytes 196616 | tf_op jit(solution)/shard_map/ppermute | solution.py:523
  51.7 5.1 %collective-permute-start.16 = (f32[128,128]{1,0:T(8,128)S(1)}, f32[128,128]{1,0:T(8,128)S(1)}, u32[]{:S(2)}, u32[]{:S(2)}) collective-permute-start(f32[128,128]{1,0:T(8,128)S(1)} %add_add_fusion.1), channel_id=1, source_target_pairs={{0,8},{1,17},{2,10},{3,19},{4,12},{5,21},{6,14},{7,23},{8,24},{9,1... | collective-permute-start | bytes 196616 | tf_op jit(solution)/shard_map/ppermute | solution.py:516
  53.1 3.7 %collective-permute-start.15 = (f32[128,128]{1,0:T(8,128)S(1)}, f32[128,128]{1,0:T(8,128)S(1)}, u32[]{:S(2)}, u32[]{:S(2)}) collective-permute-start(f32[128,128]{1,0:T(8,128)S(1)} %add_add_fusion.1), channel_id=1, source_target_pairs={{0,1},{1,0},{2,3},{3,2},{4,5},{5,4},{6,7},{7,6},{8,9},{9,8},{10,11... | collective-permute-start | bytes 196616 | tf_op jit(solution)/shard_map/ppermute | solution.py:563
  53.4 10.2 %collective-permute-start.8 = (f32[512,128]{1,0:T(8,128)S(1)}, f32[512,128]{1,0:T(8,128)S(1)}, u32[]{:S(2)}, u32[]{:S(2)}) collective-permute-start(f32[512,128]{1,0:T(8,128)S(1)} %get-tuple-element.60.tail_ref), channel_id=1, source_target_pairs={{0,16},{1,9},{2,18},{3,11},{4,20},{5,13},{6,22},{7,15},{8,0},{9,25... | collective-permute-start | bytes 786440 | tf_op jit(solution)/shard_map/ppermute | solution.py:516
  59.7 2.1 %collective-permute-start.17 = (f32[256,128]{1,0:T(8,128)S(1)}, f32[256,128]{1,0:T(8,128)S(1)}, u32[]{:S(2)}, u32[]{:S(2)}) collective-permute-start(f32[256,128]{1,0:T(8,128)S(1)} %second_rotation.1.refs_6_), channel_id=1, source_target_pairs={{0,1},{1,0},{2,3},{3,2},{4,5},{5,4},{6,7},{7,6},{8,9},{9,8},{10,11... | collective-permute-start | bytes 393224 | tf_op jit(solution)/shard_map/ppermute | solution.py:565

commit v9 on v7

--- a/solution.py
+++ b/solution.py
@@ -16,7 +16,7 @@
 RAW = 14
 SMALL = 7
 LAST = 4
-BULK = 28
+BULK = 29
 STEP = 4
 SHARE = 3
 
@@ -152,7 +152,7 @@
     )(*[pltpu.with_memory_space_constraint(array, place) for array, place in args])
 
 
-LONG = 11500000000
+LONG = 12650000000
 HERE = pltpu.VMEM
 FAR = pltpu.HBM
 

time: 64.9 us -> 64.9 us (level)
  no operation moved by 1% of the time
where the time goes in v9:
time: 64.9 us; the launch traced here: 64.7 us
  starting transfers between devices  24.4 us (38%)
  waiting for transfers between devices  20.7 us (32%)
  Pallas kernels  19.2 us (30%)
    pallas_call x13, Pallas kernels, call(): pl.pallas_call(kernel, in_specs=[pl.BlockSpec(memory_space=place) for pla...  19.2 us
    ppermute x7, starting transfers between devices, travel(): return lax.ppermute(block, ('pair', 'row'), moves)  13 us
    ppermute x7, waiting for transfers between devices, chip_sum(): lax.ppermute(block, 'row', [(r, r ^ d) for r in range(rows_count)])  9.34 us
    ppermute x7, starting transfers between devices, chip_sum(): lax.ppermute(block, 'row', [(r, r ^ d) for r in range(rows_count)])  8.73 us
    ppermute x7, waiting for transfers between devices, travel(): return lax.ppermute(block, ('pair', 'row'), moves)  7.78 us
    ppermute x1, starting transfers between devices, body(): lax.ppermute(far_small[:offset], 'row', [(r, r ^ 2) for r in range(rows_c...  2.11 us
  transfers between devices with their start and end apart: 19, of which 11 were waited for; matrix products, arithmetic and copies ran while one was open for 0% of the time, Pallas kernels for 26%

profile of v9, /device:TPU:0, one launch (start us, length us, event | category | flops | bytes accessed | tf_op | source)
XLA Modules:
  0.0 64.7 jit_solution(17571151763572101961)
XLA Ops:
  0.0 1.6 %raw_rows.1 = f32[2,1792,128]{2,1,0:T(8,128)S(1)} custom-call(f32[2,4096,128]{2,1,0:T(8,128)} %matrix_ref.9), custom_call_target="tpu_custom_call" | custom-call | tf_op jit(solution)/shard_map/raw_rows/pallas_call | solution.py:140
  1.6 3.0 %collective-permute-start.5 = (f32[2,1792,128]{2,1,0:T(8,128)S(1)}, f32[2,1792,128]{2,1,0:T(8,128)S(1)}, u32[]{:S(2)}, u32[]{:S(2)}) collective-permute-start(f32[2,1792,128]{2,1,0:T(8,128)S(1)} %raw_rows.1), channel_id=1, source_target_pairs={{0,8},{1,17},{2,10},{3,19},{4,12},{5,21},{6,14},{7,23},{8,24},{9,1... | collective-permute-start | bytes 5505032 | tf_op jit(solution)/shard_map/ppermute | solution.py:512
  4.6 1.4 %gram.1 = (f32[136,128]{1,0:T(8,128)S(1)}, f32[136,128]{1,0:T(8,128)S(1)}) custom-call(f32[2,4096,128]{2,1,0:T(8,128)S(1)} %copy-done), custom_call_target="tpu_custom_call" | custom-call | tf_op jit(solution)/shard_map/gram/pallas_call | solution.py:140
  6.1 1.2 %collective-permute-done = f32[136,128]{1,0:T(8,128)S(1)} collective-permute-done((f32[136,128]{1,0:T(8,128)S(1)}, f32[136,128]{1,0:T(8,128)S(1)}, u32[]{:S(2)}, u32[]{:S(2)}) %collective-permute-start) | collective-permute-done | bytes 69664 | tf_op jit(solution)/shard_map/ppermute | solution.py:533
  7.3 3.7 %collective-permute-start.3 = (f32[136,128]{1,0:T(8,128)S(1)}, f32[136,128]{1,0:T(8,128)S(1)}, u32[]{:S(2)}, u32[]{:S(2)}) collective-permute-start(f32[136,128]{1,0:T(8,128)S(1)} %add.21), channel_id=1, source_target_pairs={{0,6},{1,7},{2,4},{3,5},{4,2},{5,3},{6,0},{7,1},{8,14},{9,15},{10,... | collective-permute-start | bytes 208904 | tf_op jit(solution)/shard_map/ppermute | solution.py:519
  11.8 2.1 %collective-permute-done.3 = f32[136,128]{1,0:T(8,128)S(1)} collective-permute-done((f32[136,128]{1,0:T(8,128)S(1)}, f32[136,128]{1,0:T(8,128)S(1)}, u32[]{:S(2)}, u32[]{:S(2)}) %collective-permute-start.3) | collective-permute-done | bytes 69664 | tf_op jit(solution)/shard_map/ppermute | solution.py:519
  13.8 3.4 %collective-permute-done.2 = f32[136,128]{1,0:T(8,128)S(1)} collective-permute-done((f32[136,128]{1,0:T(8,128)S(1)}, f32[136,128]{1,0:T(8,128)S(1)}, u32[]{:S(2)}, u32[]{:S(2)}) %collective-permute-start.2) | collective-permute-done | bytes 69664 | tf_op jit(solution)/shard_map/ppermute | solution.py:519
  17.3 1.2 %collective-permute-done.4.other_ref = f32[136,128]{1,0:T(8,128)S(1)} collective-permute-done((f32[136,128]{1,0:T(8,128)S(1)}, f32[136,128]{1,0:T(8,128)S(1)}, u32[]{:S(2)}, u32[]{:S(2)}) %collective-permute-start.4) | collective-permute-done | bytes 69664 | tf_op jit(solution)/shard_map/ppermute | solution.py:534
  18.6 3.1 %first_rotation.1 = (f32[256,128]{1,0:T(8,128)S(1)}, f32[256,128]{1,0:T(8,128)S(1)}, f32[256,256]{1,0:T(8,128)S(1)}) custom-call(f32[136,128]{1,0:T(8,128)S(1)} %add_add_fusion.mine_ref, f32[136,128]{1,0:T(8,128)S(1)} %collective-permute-done.4.other_ref), custom_call_target="tpu_custom_call" | custom-call | tf_op jit(solution)/shard_map/first_rotation/pallas_call | solution.py:140
  22.3 1.6 %collective-permute-start.6 = (f32[1088,128]{1,0:T(8,128)S(1)}, f32[1088,128]{1,0:T(8,128)S(1)}, u32[]{:S(2)}, u32[]{:S(2)}) collective-permute-start(f32[1088,128]{1,0:T(8,128)S(1)} %small_part.1.refs_0_), channel_id=1, source_target_pairs={{0,8},{1,17},{2,10},{3,19},{4,12},{5,21},{6,14},{7,23},{8,24},{9,1... | collective-permute-start | bytes 1671176 | tf_op jit(solution)/shard_map/ppermute | solution.py:512
  23.8 2.0 %collective-permute-done.5.raw_ref = f32[2,1792,128]{2,1,0:T(8,128)S(1)} collective-permute-done((f32[2,1792,128]{2,1,0:T(8,128)S(1)}, f32[2,1792,128]{2,1,0:T(8,128)S(1)}, u32[]{:S(2)}, u32[]{:S(2)}) %collective-permute-start.5) | collective-permute-done | bytes 1835040 | tf_op jit(solution)/shard_map/ppermute | solution.py:512
  26.6 2.0 %collective-permute-start.10 = (f32[896,128]{1,0:T(8,128)S(1)}, f32[896,128]{1,0:T(8,128)S(1)}, u32[]{:S(2)}, u32[]{:S(2)}) collective-permute-start(f32[896,128]{1,0:T(8,128)S(1)} %get-tuple-element.48.refs_1_), channel_id=1, source_target_pairs={{0,8},{1,17},{2,10},{3,19},{4,12},{5,21},{6,14},{7,23},{8,24},{9,1... | collective-permute-start | bytes 1376264 | tf_op jit(solution)/shard_map/ppermute | solution.py:512
  28.7 1.9 %rest_parts.1 = (f32[3712,128]{1,0:T(8,128)S(1)}, f32[384,128]{1,0:T(8,128)S(1)}, bf16[4096,128]{1,0:T(8,128)(2,1)S(1)}, bf16[4096,128]{1,0:T(8,128)(2,1)S(1)}) custom-call(f32[2,4096,128]{2,1,0:T(8,128)S(1)} %copy-done, f32[256,128]{1,0:T(8,128)S(1)} %get-tuple-element.44.turn_ref.first_ref, f32[256,128]{1,0:T(8,128)S(1)} %get-tuple-element.46.second_ref, ...), custom_call_target="tpu_custom_call" | custom-call | tf_op jit(solution)/shard_map/rest_parts/pallas_call | solution.py:140
  30.6 1.3 %collective-permute-done.6.small_ref = f32[1088,128]{1,0:T(8,128)S(1)} collective-permute-done((f32[1088,128]{1,0:T(8,128)S(1)}, f32[1088,128]{1,0:T(8,128)S(1)}, u32[]{:S(2)}, u32[]{:S(2)}) %collective-permute-start.6) | collective-permute-done | bytes 557088 | tf_op jit(solution)/shard_map/ppermute | solution.py:512
  31.9 2.1 %collective-permute-start.7 = (f32[192,128]{1,0:T(8,128)S(1)}, f32[192,128]{1,0:T(8,128)S(1)}, u32[]{:S(2)}, u32[]{:S(2)}) collective-permute-start(f32[192,128]{1,0:T(8,128)S(1)} %slice.3), channel_id=1, source_target_pairs={{0,2},{1,3},{2,0},{3,1},{4,6},{5,7},{6,4},{7,5},{8,10},{9,11},{10,... | collective-permute-start | bytes 294920 | tf_op jit(solution)/shard_map/ppermute | solution.py:547
  34.0 1.5 %collective-permute-start.9 = (f32[512,128]{1,0:T(8,128)S(1)}, f32[512,128]{1,0:T(8,128)S(1)}, u32[]{:S(2)}, u32[]{:S(2)}) collective-permute-start(f32[512,128]{1,0:T(8,128)S(1)} %get-tuple-element.49.refs_2_), channel_id=1, source_target_pairs={{0,8},{1,17},{2,10},{3,19},{4,12},{5,21},{6,14},{7,23},{8,24},{9,1... | collective-permute-start | bytes 786440 | tf_op jit(solution)/shard_map/ppermute | solution.py:512
  35.5 1.1 %collective-permute-done.7.share_ref = f32[192,128]{1,0:T(8,128)S(1)} collective-permute-done((f32[192,128]{1,0:T(8,128)S(1)}, f32[192,128]{1,0:T(8,128)S(1)}, u32[]{:S(2)}, u32[]{:S(2)}) %collective-permute-start.7) | collective-permute-done | bytes 98336 | tf_op jit(solution)/shard_map/ppermute | solution.py:547
  36.6 2.0 %collective-permute-start.18 = (f32[3712,128]{1,0:T(8,128)S(1)}, f32[3712,128]{1,0:T(8,128)S(1)}, u32[]{:S(2)}, u32[]{:S(2)}) collective-permute-start(f32[3712,128]{1,0:T(8,128)S(1)} %get-tuple-element.66.bulk_ref), channel_id=1, source_target_pairs={{0,16},{1,9},{2,18},{3,11},{4,20},{5,13},{6,22},{7,15},{8,0},{9,25... | collective-permute-start | bytes 5701640 | tf_op jit(solution)/shard_map/ppermute | solution.py:512
  38.5 1.5 %raw_cross.1 = (bf16[2688,256]{1,0:T(8,128)(2,1)S(1)}, bf16[2688,256]{1,0:T(8,128)(2,1)S(1)}, f32[128,128]{1,0:T(8,128)S(1)}, f32[128,128]{1,0:T(8,128)S(1)}) custom-call(f32[2,1792,128]{2,1,0:T(8,128)S(1)} %collective-permute-done.5.raw_ref, f32[1088,128]{1,0:T(8,128)S(1)} %collective-permute-done.6.small_ref, ...), custom_call_target="tpu_custom_call" | custom-call | tf_op jit(solution)/shard_map/raw_cross/pallas_call | solution.py:140
  40.4 2.7 %collective-permute-done.9.far_ref = f32[512,128]{1,0:T(8,128)S(1)} collective-permute-done((f32[512,128]{1,0:T(8,128)S(1)}, f32[512,128]{1,0:T(8,128)S(1)}, u32[]{:S(2)}, u32[]{:S(2)}) %collective-permute-start.9) | collective-permute-done | bytes 262176 | tf_op jit(solution)/shard_map/ppermute | solution.py:512
  43.5 1.9 %collective-permute-start.13 = (f32[128,128]{1,0:T(8,128)S(1)}, f32[128,128]{1,0:T(8,128)S(1)}, u32[]{:S(2)}, u32[]{:S(2)}) collective-permute-start(f32[128,128]{1,0:T(8,128)S(1)} %get-tuple-element.65), channel_id=1, source_target_pairs={{0,5},{1,4},{2,7},{3,6},{4,1},{5,0},{6,3},{7,2},{8,13},{9,12},{10,... | collective-permute-start | bytes 196616 | tf_op jit(solution)/shard_map/ppermute | solution.py:519
  45.4 1.2 %collective-permute-start.12 = (f32[128,128]{1,0:T(8,128)S(1)}, f32[128,128]{1,0:T(8,128)S(1)}, u32[]{:S(2)}, u32[]{:S(2)}) collective-permute-start(f32[128,128]{1,0:T(8,128)S(1)} %get-tuple-element.65), channel_id=1, source_target_pairs={{0,3},{1,2},{2,1},{3,0},{4,7},{5,6},{6,5},{7,4},{8,11},{9,10},{10,... | collective-permute-start | bytes 196616 | tf_op jit(solution)/shard_map/ppermute | solution.py:519
  46.6 1.1 %collective-permute-start.11 = (f32[128,128]{1,0:T(8,128)S(1)}, f32[128,128]{1,0:T(8,128)S(1)}, u32[]{:S(2)}, u32[]{:S(2)}) collective-permute-start(f32[128,128]{1,0:T(8,128)S(1)} %get-tuple-element.65), channel_id=1, source_target_pairs={{0,1},{1,0},{2,3},{3,2},{4,5},{5,4},{6,7},{7,6},{8,9},{9,8},{10,11... | collective-permute-start | bytes 196616 | tf_op jit(solution)/shard_map/ppermute | solution.py:519
  47.7 1.7 %collective-permute-done.14 = f32[128,128]{1,0:T(8,128)S(1)} collective-permute-done((f32[128,128]{1,0:T(8,128)S(1)}, f32[128,128]{1,0:T(8,128)S(1)}, u32[]{:S(2)}, u32[]{:S(2)}) %collective-permute-start.14) | collective-permute-done | bytes 65568 | tf_op jit(solution)/shard_map/ppermute | solution.py:519
  49.4 2.2 %collective-permute-done.13 = f32[128,128]{1,0:T(8,128)S(1)} collective-permute-done((f32[128,128]{1,0:T(8,128)S(1)}, f32[128,128]{1,0:T(8,128)S(1)}, u32[]{:S(2)}, u32[]{:S(2)}) %collective-permute-start.13) | collective-permute-done | bytes 65568 | tf_op jit(solution)/shard_map/ppermute | solution.py:519
  51.6 1.4 %collective-permute-start.16 = (f32[128,128]{1,0:T(8,128)S(1)}, f32[128,128]{1,0:T(8,128)S(1)}, u32[]{:S(2)}, u32[]{:S(2)}) collective-permute-start(f32[128,128]{1,0:T(8,128)S(1)} %add_add_fusion.1), channel_id=1, source_target_pairs={{0,8},{1,17},{2,10},{3,19},{4,12},{5,21},{6,14},{7,23},{8,24},{9,1... | collective-permute-start | bytes 196616 | tf_op jit(solution)/shard_map/ppermute | solution.py:512
  53.4 1.5 %collective-permute-start.8 = (f32[384,128]{1,0:T(8,128)S(1)}, f32[384,128]{1,0:T(8,128)S(1)}, u32[]{:S(2)}, u32[]{:S(2)}) collective-permute-start(f32[384,128]{1,0:T(8,128)S(1)} %get-tuple-element.56.tail_ref), channel_id=1, source_target_pairs={{0,16},{1,9},{2,18},{3,11},{4,20},{5,13},{6,22},{7,15},{8,0},{9,25... | collective-permute-start | bytes 589832 | tf_op jit(solution)/shard_map/ppermute | solution.py:512
  54.9 1.8 %collective-permute-done.16.there_ref = f32[128,128]{1,0:T(8,128)S(1)} collective-permute-done((f32[128,128]{1,0:T(8,128)S(1)}, f32[128,128]{1,0:T(8,128)S(1)}, u32[]{:S(2)}, u32[]{:S(2)}) %collective-permute-start.16) | collective-permute-done | bytes 65568 | tf_op jit(solution)/shard_map/ppermute | solution.py:512
  56.7 2.9 %second_rotation.1.refs_6_ = f32[256,128]{1,0:T(8,128)S(1)} custom-call(f32[128,128]{1,0:T(8,128)S(1)} %get-tuple-element.57.own_gram_ref, f32[128,128]{1,0:T(8,128)S(1)} %get-tuple-element.60.far_ref, f32[128,128]{1,0:T(8,128)S(1)} %collective-permute-done.15.here_ref, f32[128,128]{1,0:T(8,128)S(1)} %collective-permute-done.16.there_ref), custom_call_target="tpu_custom_call" | custom-call | flops 12650000384 | tf_op jit(solution)/shard_map/second_rotation/pallas_call | solution.py:140
  59.7 2.0 %here_product.1.refs_5_ = f32[2,4096,128]{2,1,0:T(8,128)} custom-call(bf16[2688,256]{1,0:T(8,128)(2,1)S(1)} %get-tuple-element.67.refs_0_, bf16[2688,256]{1,0:T(8,128)(2,1)S(1)} %get-tuple-element.68.refs_1_, bf16[896,256]{1,0:T(8,128)(2,1)S(1)} %get-tuple-element.69.refs_2_, bf16[896,256]{1,0:T(8,128)(2,1)S(1)} %get-tuple-element.70.refs_3_, ...), custom_call_target="tpu_custom_call" | custom-call | tf_op jit(solution)/shard_map/here_product/pallas_call | solution.py:140
  61.8 1.9 %bulk_product.1.refs_4_ = f32[2,4096,128]{2,1,0:T(8,128)} custom-call(bf16[4096,128]{1,0:T(8,128)(2,1)S(1)} %get-tuple-element.50.refs_0_, bf16[4096,128]{1,0:T(8,128)(2,1)S(1)} %get-tuple-element.51.refs_1_, f32[3712,128]{1,0:T(8,128)S(1)} %collective-permute-done.18.refs_2_.refs_3_, ...), custom_call_target="tpu_custom_call", output_to_operand_aliasing={{}: (5, {})} | custom-call | tf_op jit(solution)/shard_map/bulk_product/pallas_call | solution.py:140
  63.7 0.9 %tail_product.1 = f32[2,4096,128]{2,1,0:T(8,128)} custom-call(bf16[4096,128]{1,0:T(8,128)(2,1)S(1)} %get-tuple-element.50.refs_0_, bf16[4096,128]{1,0:T(8,128)(2,1)S(1)} %get-tuple-element.51.refs_1_, f32[384,128]{1,0:T(8,128)S(1)} %collective-permute-done.8.refs_2_, ...), custom_call_target="tpu_custom_call", output_to_operand_aliasing={{}: (4, {})} | custom-call | tf_op jit(solution)/shard_map/tail_product/pallas_call | solution.py:140
  (25 shorter events, 3.6 us)
Async XLA Ops:
  0.0 4.6 %copy-start = (f32[2,4096,128]{2,1,0:T(8,128)S(1)}, f32[2,4096,128]{2,1,0:T(8,128)}, u32[]{:S(2)}) copy-start(f32[2,4096,128]{2,1,0:T(8,128)} %matrix_ref.9) | copy-start | bytes 12582916
  1.6 24.2 %collective-permute-start.5 = (f32[2,1792,128]{2,1,0:T(8,128)S(1)}, f32[2,1792,128]{2,1,0:T(8,128)S(1)}, u32[]{:S(2)}, u32[]{:S(2)}) collective-permute-start(f32[2,1792,128]{2,1,0:T(8,128)S(1)} %raw_rows.1), channel_id=1, source_target_pairs={{0,8},{1,17},{2,10},{3,19},{4,12},{5,21},{6,14},{7,23},{8,24},{9,1... | collective-permute-start | bytes 5505032 | tf_op jit(solution)/shard_map/ppermute | solution.py:512
  6.0 1.3 %collective-permute-start = (f32[136,128]{1,0:T(8,128)S(1)}, f32[136,128]{1,0:T(8,128)S(1)}, u32[]{:S(2)}, u32[]{:S(2)}) collective-permute-start(f32[136,128]{1,0:T(8,128)S(1)} %get-tuple-element.40), channel_id=1, source_target_pairs={{0,1},{1,0},{2,3},{3,2},{4,5},{5,4},{6,7},{7,6},{8,9},{9,8},{10,11... | collective-permute-start | bytes 208904 | tf_op jit(solution)/shard_map/ppermute | solution.py:533
  7.3 6.5 %collective-permute-start.3 = (f32[136,128]{1,0:T(8,128)S(1)}, f32[136,128]{1,0:T(8,128)S(1)}, u32[]{:S(2)}, u32[]{:S(2)}) collective-permute-start(f32[136,128]{1,0:T(8,128)S(1)} %add.21), channel_id=1, source_target_pairs={{0,6},{1,7},{2,4},{3,5},{4,2},{5,3},{6,0},{7,1},{8,14},{9,15},{10,... | collective-permute-start | bytes 208904 | tf_op jit(solution)/shard_map/ppermute | solution.py:519
  11.0 6.2 %collective-permute-start.2 = (f32[136,128]{1,0:T(8,128)S(1)}, f32[136,128]{1,0:T(8,128)S(1)}, u32[]{:S(2)}, u32[]{:S(2)}) collective-permute-start(f32[136,128]{1,0:T(8,128)S(1)} %add.21), channel_id=1, source_target_pairs={{0,4},{1,5},{2,6},{3,7},{4,0},{5,1},{6,2},{7,3},{8,12},{9,13},{10,... | collective-permute-start | bytes 208904 | tf_op jit(solution)/shard_map/ppermute | solution.py:519
  11.0 6.2 %collective-permute-start.1 = (f32[136,128]{1,0:T(8,128)S(1)}, f32[136,128]{1,0:T(8,128)S(1)}, u32[]{:S(2)}, u32[]{:S(2)}) collective-permute-start(f32[136,128]{1,0:T(8,128)S(1)} %add.21), channel_id=1, source_target_pairs={{0,2},{1,3},{2,0},{3,1},{4,6},{5,7},{6,4},{7,5},{8,10},{9,11},{10,... | collective-permute-start | bytes 208904 | tf_op jit(solution)/shard_map/ppermute | solution.py:519
  17.2 1.3 %collective-permute-start.4 = (f32[136,128]{1,0:T(8,128)S(1)}, f32[136,128]{1,0:T(8,128)S(1)}, u32[]{:S(2)}, u32[]{:S(2)}) collective-permute-start(f32[136,128]{1,0:T(8,128)S(1)} %add_add_fusion.mine_ref), channel_id=1, source_target_pairs={{0,1},{1,0},{2,3},{3,2},{4,5},{5,4},{6,7},{7,6},{8,9},{9,8},{10,11... | collective-permute-start | bytes 208904 | tf_op jit(solution)/shard_map/ppermute | solution.py:534
  22.3 9.6 %collective-permute-start.6 = (f32[1088,128]{1,0:T(8,128)S(1)}, f32[1088,128]{1,0:T(8,128)S(1)}, u32[]{:S(2)}, u32[]{:S(2)}) collective-permute-start(f32[1088,128]{1,0:T(8,128)S(1)} %small_part.1.refs_0_), channel_id=1, source_target_pairs={{0,8},{1,17},{2,10},{3,19},{4,12},{5,21},{6,14},{7,23},{8,24},{9,1... | collective-permute-start | bytes 1671176 | tf_op jit(solution)/shard_map/ppermute | solution.py:512
  26.6 13.4 %collective-permute-start.10 = (f32[896,128]{1,0:T(8,128)S(1)}, f32[896,128]{1,0:T(8,128)S(1)}, u32[]{:S(2)}, u32[]{:S(2)}) collective-permute-start(f32[896,128]{1,0:T(8,128)S(1)} %get-tuple-element.48.refs_1_), channel_id=1, source_target_pairs={{0,8},{1,17},{2,10},{3,19},{4,12},{5,21},{6,14},{7,23},{8,24},{9,1... | collective-permute-start | bytes 1376264 | tf_op jit(solution)/shard_map/ppermute | solution.py:512
  31.9 4.7 %collective-permute-start.7 = (f32[192,128]{1,0:T(8,128)S(1)}, f32[192,128]{1,0:T(8,128)S(1)}, u32[]{:S(2)}, u32[]{:S(2)}) collective-permute-start(f32[192,128]{1,0:T(8,128)S(1)} %slice.3), channel_id=1, source_target_pairs={{0,2},{1,3},{2,0},{3,1},{4,6},{5,7},{6,4},{7,5},{8,10},{9,11},{10,... | collective-permute-start | bytes 294920 | tf_op jit(solution)/shard_map/ppermute | solution.py:547
  34.0 9.1 %collective-permute-start.9 = (f32[512,128]{1,0:T(8,128)S(1)}, f32[512,128]{1,0:T(8,128)S(1)}, u32[]{:S(2)}, u32[]{:S(2)}) collective-permute-start(f32[512,128]{1,0:T(8,128)S(1)} %get-tuple-element.49.refs_2_), channel_id=1, source_target_pairs={{0,8},{1,17},{2,10},{3,19},{4,12},{5,21},{6,14},{7,23},{8,24},{9,1... | collective-permute-start | bytes 786440 | tf_op jit(solution)/shard_map/ppermute | solution.py:512
  36.6 25.2 %collective-permute-start.18 = (f32[3712,128]{1,0:T(8,128)S(1)}, f32[3712,128]{1,0:T(8,128)S(1)}, u32[]{:S(2)}, u32[]{:S(2)}) collective-permute-start(f32[3712,128]{1,0:T(8,128)S(1)} %get-tuple-element.66.bulk_ref), channel_id=1, source_target_pairs={{0,16},{1,9},{2,18},{3,11},{4,20},{5,13},{6,22},{7,15},{8,0},{9,25... | collective-permute-start | bytes 5701640 | tf_op jit(solution)/shard_map/ppermute | solution.py:512
  43.4 6.0 %collective-permute-start.14 = (f32[128,128]{1,0:T(8,128)S(1)}, f32[128,128]{1,0:T(8,128)S(1)}, u32[]{:S(2)}, u32[]{:S(2)}) collective-permute-start(f32[128,128]{1,0:T(8,128)S(1)} %get-tuple-element.65), channel_id=1, source_target_pairs={{0,7},{1,6},{2,5},{3,4},{4,3},{5,2},{6,1},{7,0},{8,15},{9,14},{10,... | collective-permute-start | bytes 196616 | tf_op jit(solution)/shard_map/ppermute | solution.py:519
  43.5 8.1 %collective-permute-start.13 = (f32[128,128]{1,0:T(8,128)S(1)}, f32[128,128]{1,0:T(8,128)S(1)}, u32[]{:S(2)}, u32[]{:S(2)}) collective-permute-start(f32[128,128]{1,0:T(8,128)S(1)} %get-tuple-element.65), channel_id=1, source_target_pairs={{0,5},{1,4},{2,7},{3,6},{4,1},{5,0},{6,3},{7,2},{8,13},{9,12},{10,... | collective-permute-start | bytes 196616 | tf_op jit(solution)/shard_map/ppermute | solution.py:519
  45.4 6.2 %collective-permute-start.12 = (f32[128,128]{1,0:T(8,128)S(1)}, f32[128,128]{1,0:T(8,128)S(1)}, u32[]{:S(2)}, u32[]{:S(2)}) collective-permute-start(f32[128,128]{1,0:T(8,128)S(1)} %get-tuple-element.65), channel_id=1, source_target_pairs={{0,3},{1,2},{2,1},{3,0},{4,7},{5,6},{6,5},{7,4},{8,11},{9,10},{10,... | collective-permute-start | bytes 196616 | tf_op jit(solution)/shard_map/ppermute | solution.py:519
  46.6 5.0 %collective-permute-start.11 = (f32[128,128]{1,0:T(8,128)S(1)}, f32[128,128]{1,0:T(8,128)S(1)}, u32[]{:S(2)}, u32[]{:S(2)}) collective-permute-start(f32[128,128]{1,0:T(8,128)S(1)} %get-tuple-element.65), channel_id=1, source_target_pairs={{0,1},{1,0},{2,3},{3,2},{4,5},{5,4},{6,7},{7,6},{8,9},{9,8},{10,11... | collective-permute-start | bytes 196616 | tf_op jit(solution)/shard_map/ppermute | solution.py:519
  51.6 5.1 %collective-permute-start.16 = (f32[128,128]{1,0:T(8,128)S(1)}, f32[128,128]{1,0:T(8,128)S(1)}, u32[]{:S(2)}, u32[]{:S(2)}) collective-permute-start(f32[128,128]{1,0:T(8,128)S(1)} %add_add_fusion.1), channel_id=1, source_target_pairs={{0,8},{1,17},{2,10},{3,19},{4,12},{5,21},{6,14},{7,23},{8,24},{9,1... | collective-permute-start | bytes 196616 | tf_op jit(solution)/shard_map/ppermute | solution.py:512
  53.1 3.6 %collective-permute-start.15 = (f32[128,128]{1,0:T(8,128)S(1)}, f32[128,128]{1,0:T(8,128)S(1)}, u32[]{:S(2)}, u32[]{:S(2)}) collective-permute-start(f32[128,128]{1,0:T(8,128)S(1)} %add_add_fusion.1), channel_id=1, source_target_pairs={{0,1},{1,0},{2,3},{3,2},{4,5},{5,4},{6,7},{7,6},{8,9},{9,8},{10,11... | collective-permute-start | bytes 196616 | tf_op jit(solution)/shard_map/ppermute | solution.py:559
  53.4 10.2 %collective-permute-start.8 = (f32[384,128]{1,0:T(8,128)S(1)}, f32[384,128]{1,0:T(8,128)S(1)}, u32[]{:S(2)}, u32[]{:S(2)}) collective-permute-start(f32[384,128]{1,0:T(8,128)S(1)} %get-tuple-element.56.tail_ref), channel_id=1, source_target_pairs={{0,16},{1,9},{2,18},{3,11},{4,20},{5,13},{6,22},{7,15},{8,0},{9,25... | collective-permute-start | bytes 589832 | tf_op jit(solution)/shard_map/ppermute | solution.py:512
  59.7 2.1 %collective-permute-start.17 = (f32[256,128]{1,0:T(8,128)S(1)}, f32[256,128]{1,0:T(8,128)S(1)}, u32[]{:S(2)}, u32[]{:S(2)}) collective-permute-start(f32[256,128]{1,0:T(8,128)S(1)} %second_rotation.1.refs_6_), channel_id=1, source_target_pairs={{0,1},{1,0},{2,3},{3,2},{4,5},{5,4},{6,7},{7,6},{8,9},{9,8},{10,11... | collective-permute-start | bytes 393224 | tf_op jit(solution)/shard_map/ppermute | solution.py:561
